TPU v7x, 256 devices: a whole 4x4x8 slice. The times are simulated.
256 devices in a mesh: img: 8 (over x, y_hi), txt: 32 (over y_lo, z, core).
Axes of the slice: x: 4, y: 4 (y_hi: 2, y_lo: 2; y = y_hi * 2 + y_lo), z: 8, core: 2. Of those that a mesh axis runs over, the one named last changes fastest.
Arguments:
- image: bfloat16 [16384, 1280], P(('img', 'txt')), may hold values from -8 to 8
- text: bfloat16 [16384, 1280], P(('txt', 'img')), may hold values from -8 to 8
Outputs:
- image_grad: bfloat16 [16384, 1280], P(('img', 'txt'))
- text_grad: bfloat16 [16384, 1280], P(('txt', 'img'))
- loss: float32 [], replicated
All inputs are finite; a program needn't handle non-finite values.
Results may differ from a plain program's by a relative error of at most 0.0034.
Values may be sent and summed in bfloat16 or wider, within the bound.
No kernel may reach another device: no remote copies, remote signals or barrier semaphores. Data moves between devices by JAX's collectives and lax.ppermute only.
A program may use at most 64 MiB of HBM per device.

v0:
```python
import math

import jax
import jax.numpy as jnp
from jax import lax
from jax.sharding import PartitionSpec as P


def combined_all(value, axis, join):
    pieces = jax.tree.map(lambda part: lax.all_gather(part, axis), value)
    head = jax.tree.map(lambda part: part[0], pieces)
    tail = jax.tree.map(lambda part: part[1:], pieces)
    so_far, _ = lax.scan(lambda so_far, share: (join(so_far, share), None), head, tail)
    return so_far


def lse_merge(first, second):
    top = jnp.maximum(first[0], second[0])
    total = first[1] * jnp.exp(first[0] - top) + second[1] * jnp.exp(second[0] - top)
    return (top, total)


def shards(image, text):
    rows_dev = image.shape[0]
    embed = image.shape[1]
    logit_scale = 4.0 / math.sqrt(embed)
    n_img = lax.axis_size("img")
    n_txt = lax.axis_size("txt")
    img_pos = lax.axis_index("img")
    txt_pos = lax.axis_index("txt")
    pairs = rows_dev * n_img * n_txt
    img_block = lax.all_gather(image, "txt", axis=0, tiled=True)
    txt_block = lax.all_gather(text, "img", axis=0, tiled=True)
    img_count = img_block.shape[0]
    txt_count = txt_block.shape[0]
    scores = logit_scale * lax.dot_general(
        img_block, txt_block, (((1,), (1,)), ((), ())), preferred_element_type=jnp.float32
    )
    row_top = jnp.max(scores, axis=1)
    row_sum = jnp.sum(jnp.exp(scores - row_top[:, None]), axis=1)
    col_top = jnp.max(scores, axis=0)
    col_sum = jnp.sum(jnp.exp(scores - col_top[None, :]), axis=0)
    row_top, row_sum = combined_all((row_top, row_sum), "txt", lse_merge)
    row_lse = row_top + jnp.log(row_sum)
    own_rows = lax.dynamic_slice_in_dim(row_lse, txt_pos * rows_dev, rows_dev)
    col_top, col_sum = combined_all((col_top, col_sum), "img", lse_merge)
    col_lse = col_top + jnp.log(col_sum)
    own_cols = lax.dynamic_slice_in_dim(col_lse, img_pos * rows_dev, rows_dev)
    rows = img_pos * img_count + jnp.arange(img_count, dtype=jnp.int32)[:, None]
    cols = txt_pos * txt_count + jnp.arange(txt_count, dtype=jnp.int32)[None, :]
    diagonal = rows == cols
    diag_sum = jnp.sum(jnp.where(diagonal, scores, 0.0))
    local_loss = 0.5 * (jnp.sum(own_rows) + jnp.sum(own_cols)) - diag_sum
    loss = lax.psum(local_loss, ("img", "txt")) / pairs
    weights = (
        (jnp.exp(scores - row_lse[:, None]) + jnp.exp(scores - col_lse[None, :])) * 0.5
        - diagonal.astype(jnp.float32)
    ).astype(jnp.bfloat16)
    picked = weights
    image_grad = lax.psum_scatter(
        jnp.dot(picked, txt_block, preferred_element_type=jnp.float32),
        "txt",
        scatter_dimension=0,
        tiled=True,
    )
    picked = weights
    text_grad = lax.psum_scatter(
        lax.dot_general(
            picked, img_block, (((0,), (0,)), ((), ())), preferred_element_type=jnp.float32
        ),
        "img",
        scatter_dimension=0,
        tiled=True,
    )
    return (image_grad.astype(jnp.bfloat16), text_grad.astype(jnp.bfloat16), loss)


def solution(mesh):
    return jax.shard_map(
        shards,
        mesh=mesh,
        in_specs=(P(("img", "txt"), None), P(("txt", "img"), None)),
        out_specs=(P(("img", "txt"), None), P(("txt", "img"), None), P()),
        check_vma=False,
    )
```

profile of v0, /device:TPU:32, one launch (start us, length us, event | category | flops | bytes accessed | tf_op | source)
XLA Modules:
  0.0 499.2 jit_solution(5522389297347997598)
XLA Ops:
  7.2 0.0 all-gather.11.cloned.1.call-start
  7.2 0.7 all-gather.11.cloned.1.call-update
  7.9 0.0 all-gather.9.cloned.1.call-start
  7.9 0.7 all-gather.9.cloned.1.call-update
  8.6 0.0 reduce-scatter.5.cloned.1.call-start
  8.7 59.0 %all-gather.11.cloned.1.call-done = bf16[512,1280]{1,0:T(8,128)(2,1)} async-done(((bf16[64,1280]{1,0:T(8,128)(2,1)}), bf16[512,1280]{1,0:T(8,128)(2,1)}) %all-gather.11.cloned.1.call-update) | async-done | bytes 1310736 | tf_op jit(solution)/shard_map/all_gather | solution.py:33
  67.7 68.3 %all-gather.9.cloned.1.call-done = bf16[2048,1280]{1,0:T(8,128)(2,1)} async-done(((bf16[64,1280]{1,0:T(8,128)(2,1)}), bf16[2048,1280]{1,0:T(8,128)(2,1)}) %all-gather.9.cloned.1.call-update) | async-done | bytes 5242896 | tf_op jit(solution)/shard_map/all_gather | solution.py:32
  136.0 5.4 %fusion.7 = (f32[2048]{0:T(1024)S(1)}, f32[512]{0:T(512)S(1)}, f32[2048,512]{1,0:T(8,128)S(1)}) fusion(bf16[2048,1280]{1,0:T(8,128)(2,1)} %all-gather.9.cloned.1.call-done, bf16[512,1280]{1,0:T(8,128)(2,1)} %all-gather.11.cloned.1.call-done), kind=kOutput, calls=%fused_computation.24 | convolution fusion | flops 2687497728 | bytes 10758144 | tf_op jit(solution)/shard_map/dot_general | solution.py:36
  141.4 0.0 copy-start
  141.4 2.1 copy-done
  143.5 2.8 fusion.2
  146.3 29.9 %all-gather.5 = f32[8,1,512]{2,1,0:T(1,128)S(1)} all-gather(f32[1,1,512]{2,1,0:T(1,128)S(1)} %bitcast.35), channel_id=5, replica_groups=mesh['img'=8,'txt'=32] {'img'}, dimensions={0}, use_global_device_ids=true | all-gather | bytes 18432 | tf_op jit(solution)/shard_map/all_gather | solution.py:10
  176.2 29.7 %all-gather.4 = f32[8,1,512]{2,1,0:T(1,128)S(1)} all-gather(f32[1,1,512]{2,1,0:T(1,128)S(1)} %bitcast.34), channel_id=4, replica_groups=mesh['img'=8,'txt'=32] {'img'}, dimensions={0}, use_global_device_ids=true | all-gather | bytes 18432 | tf_op jit(solution)/shard_map/all_gather | solution.py:10
  205.9 32.1 %all-gather = f32[65536]{0:T(1024)S(1)} all-gather(f32[2048]{0:T(1024)S(1)} %get-tuple-element.66), channel_id=2, replica_groups=mesh['img'=8,'txt'=32] {'txt'}, dimensions={0}, use_global_device_ids=true | all-gather | bytes 270336 | tf_op jit(solution)/shard_map/all_gather | solution.py:10
  238.0 33.1 %all-gather.1 = f32[65536]{0:T(1024)S(1)} all-gather(f32[2048]{0:T(1024)S(1)} %get-tuple-element.65), channel_id=3, replica_groups=mesh['img'=8,'txt'=32] {'txt'}, dimensions={0}, use_global_device_ids=true | all-gather | bytes 270336 | tf_op jit(solution)/shard_map/all_gather | solution.py:10
  271.2 0.4 while.25
  271.7 1.9 while.24
  273.6 0.0 copy-start.1
  273.6 8.7 %fusion.3 = f32[512,1280]{1,0:T(8,128)} fusion(bf16[2048,1280]{1,0:T(8,128)(2,1)} %all-gather.9.cloned.1.call-done, f32[2048,512]{1,0:T(8,128)} %copy-done, s32[512]{0:T(512)S(1)} %iota_add_fusion.1, f32[512]{0:T(512)S(1)} %log_add_fusion.1, f32[2048]{0:T(1024)S(1)} %log_add_fusion, s32[2048]{0:T(1024)S(1)} %iota_add_fusion), kind=kOutput, calls=%fused_computation.22 | convolution fusion | flops 2692743168 | bytes 12079104 | tf_op jit(solution)/shard_map/dot_general | solution.py:68
  282.4 0.0 reduce-scatter.5.cloned.1.call-update
  282.4 0.0 reduce-scatter.3.cloned.1.call-start
  282.5 0.0 copy-done.1
  282.5 8.2 %fusion.5 = f32[2048,1280]{1,0:T(8,128)} fusion(bf16[512,1280]{1,0:T(8,128)(2,1)S(1)} %copy-done.1, f32[2048,512]{1,0:T(8,128)} %copy-done, s32[512]{0:T(512)S(1)} %iota_add_fusion.1, f32[512]{0:T(512)S(1)} %log_add_fusion.1, f32[2048]{0:T(1024)S(1)} %log_add_fusion, s32[2048]{0:T(1024)S(1)} %iota_add_fusion), kind=kOutput, calls=%fused_computation.23 | convolution fusion | flops 2692743168 | bytes 16011264 | tf_op jit(solution)/shard_map/dot_general | solution.py:61
  290.7 0.0 reduce-scatter.3.cloned.1.call-update
  290.7 0.7 dynamic-slice_reduce_fusion
  293.3 75.1 %psum.7 = f32[]{:T(128)} all-reduce(f32[]{:T(128)S(6)} %sub.59), channel_id=1, replica_groups=mesh['img'=8,'txt'=32] {'img','txt'}, use_global_device_ids=true, to_apply=%region_13.14 | all-reduce | flops 1 | bytes 8 | tf_op jit(solution)/shard_map/psum | solution.py:54
  369.1 0.0 reduce-scatter.5.cloned.1.call-done
  369.1 1.7 convert_element_type.15
  370.8 119.1 %reduce-scatter.3.cloned.1.call-done = f32[64,1280]{1,0:T(8,128)} async-done(((f32[2048,1280]{1,0:T(8,128)}), f32[64,1280]{1,0:T(8,128)}) %reduce-scatter.3.cloned.1.call-update) | async-done | bytes 327696 | tf_op jit(solution)/shard_map/reduce_scatter | solution.py:60
  489.9 1.7 convert_element_type.14
  (92 shorter events, 1.4 us)
Async XLA Ops:
  7.2 60.5 %all-gather.11.cloned.1.call-start = ((), (), s32[]{:S(2)}) async-start(), calls=%async_computation.3 | async-start | bytes 1474560 | tf_op jit(solution)/shard_map/all_gather | solution.py:33
  7.9 128.1 %all-gather.9.cloned.1.call-start = ((), (), s32[]{:S(2)}) async-start(), calls=%async_computation.2 | async-start | bytes 5406720 | tf_op jit(solution)/shard_map/all_gather | solution.py:32
  8.6 360.5 %reduce-scatter.5.cloned.1.call-start = ((), (), s32[]{:S(2)}) async-start(), calls=%async_computation.5 | async-start | bytes 2949120 | tf_op jit(solution)/shard_map/reduce_scatter | solution.py:67
  141.4 2.1 copy-start
  273.6 8.8 %copy-start.1 = (bf16[512,1280]{1,0:T(8,128)(2,1)S(1)}, bf16[512,1280]{1,0:T(8,128)(2,1)}, u32[]{:S(2)}) copy-start(bf16[512,1280]{1,0:T(8,128)(2,1)} %all-gather.11.cloned.1.call-done) | copy-start | bytes 3932164
  282.4 207.5 %reduce-scatter.3.cloned.1.call-start = ((), (), s32[]{:S(2)}) async-start(), calls=%async_computation.4 | async-start | bytes 10813440 | tf_op jit(solution)/shard_map/reduce_scatter | solution.py:60
Sparse Core Ops, SparseCore 0:
  10.6 57.0 all-gather.10
  69.5 66.4 all-gather.8
  282.5 77.4 reduce-scatter.4
  362.4 127.3 reduce-scatter.2
where the time goes:
time: 504 us; the launch traced here: 499 us
  waiting for transfers between devices  248 us (49%)
  blocking collectives  200 us (40%)
  matrix products  22.3 us (4%)
  between operations  17.6 us (3%)
  other arithmetic  7.36 us (1%)
    all_gather x4, blocking collectives, combined_all(): pieces = jax.tree.map(lambda part: lax.all_gather(part, axis), value)  125 us
    reduce_scatter x1, waiting for transfers between devices, shards(): lax.psum_scatter(jnp.dot(picked, txt_block, preferred_element_type=jnp.fl...  119 us
    psum x1, blocking collectives, shards(): loss = lax.psum(local_loss, ('img', 'txt')) / pairs  75.1 us
    all_gather x1, waiting for transfers between devices, shards(): img_block = lax.all_gather(image, 'txt', axis=0, tiled=True)  68.3 us
    all_gather x1, waiting for transfers between devices, shards(): txt_block = lax.all_gather(text, 'img', axis=0, tiled=True)  59 us
  transfers between devices with their start and end apart: 4, of which 3 were waited for; matrix products, arithmetic and copies ran while one was open for 2% of the time, Pallas kernels for 0%

commit v1 on v0

v1 whole, which is shorter than its diff:
```python
import functools
import math

import jax
import jax.numpy as jnp
from jax import lax
from jax.experimental import pallas as pl
from jax.experimental.pallas import tpu as pltpu
from jax.sharding import PartitionSpec as P

NX, NY, NZ, NC = 4, 4, 8, 2
AXES = ("img", "txt")
SHARD = 64
HALF = SHARD // 2
ROWS = NZ * SHARD
PLANE = NX * NY * SHARD
COLS = NC * PLANE
NOTE = 16
BF16, F32 = jnp.bfloat16, jnp.float32


def device_id(x, y, z, c):
    return (((x % NX) * NY + y % NY) * NZ + z % NZ) * NC + c % NC


COORDINATES = [(x, y, z, c) for x in range(NX) for y in range(NY) for z in range(NZ) for c in range(NC)]


def shift_z(value, by):
    pairs = [(device_id(x, y, z, c), device_id(x, y, z + by, c)) for x, y, z, c in COORDINATES]
    return lax.ppermute(value, AXES, pairs)


def shift_plane(value, by, first):
    pairs = []
    for x, y, z, c in COORDINATES:
        along_y = (c == 0) == first
        to = (x, y + by) if along_y else (x + by, y)
        pairs.append((device_id(x, y, z, c), device_id(*to, z, c)))
    return lax.ppermute(value, AXES, pairs)


def swap(value, axis, bit):
    pairs = []
    for at in COORDINATES:
        to = list(at)
        to[axis] ^= bit
        pairs.append((device_id(*at), device_id(*to)))
    return lax.ppermute(value, AXES, pairs)


def swap_core(value):
    return swap(value, 3, 1)


def merge(first, second):
    top = jnp.maximum(first, second)
    return top + jnp.log(jnp.exp(first - top) + jnp.exp(second - top))


def merge_columns(first, second):
    lanes = lax.broadcasted_iota(jnp.int32, first.shape, 1)
    return jnp.where(lanes < COLS, merge(first, second), first + second)


def call(kernel, outs, args, scratch, flops, transcendentals, moved, at, vmem_mib):
    vmem = pl.BlockSpec(memory_space=pltpu.VMEM)
    return pl.pallas_call(
        kernel,
        out_shape=[jax.ShapeDtypeStruct(shape, dtype) for shape, dtype in outs],
        in_specs=[pl.BlockSpec(memory_space=pltpu.SMEM)] + [vmem] * len(args),
        out_specs=[vmem] * len(outs),
        scratch_shapes=scratch,
        cost_estimate=pl.CostEstimate(flops=flops, transcendentals=transcendentals, bytes_accessed=moved),
        compiler_params=pltpu.CompilerParams(vmem_limit_bytes=vmem_mib << 20),
    )(at, *args)


def diagonal_blocks(c):
    for zz in range(NZ):
        col = (zz // 4) * PLANE + (zz % 4) * NY * SHARD + c * 2 * SHARD
        yield zz * SHARD, pl.multiple_of(col, 128)


def on_diagonal(x):
    rows = lax.broadcasted_iota(jnp.int32, (SHARD, 128), 0)
    lanes = lax.broadcasted_iota(jnp.int32, (SHARD, 128), 1)
    return lanes == rows + (x // 2) * SHARD


def has_diagonal(x, y, z):
    return z == (x % 2) * 4 + y


def block_row(xx, yy):
    return pl.multiple_of((lax.rem(xx + NX, NX) * NY + lax.rem(yy + NY, NY)) * SHARD, SHARD)


def write_note(ref, value):
    high = value.astype(BF16)
    rest = value - high.astype(F32)
    middle = rest.astype(BF16)
    low = (rest - middle.astype(F32)).astype(BF16)
    for i, term in enumerate((high, middle, low)):
        ref[:, i * 128 : (i + 1) * 128] = jnp.broadcast_to(term.astype(F32), (NOTE, 128)).astype(BF16)
    ref[:, 384:] = jnp.zeros((NOTE, ref.shape[1] - 384), BF16)


def read_note(rows):
    terms = [rows[0:1, i * 128 : (i + 1) * 128].astype(F32) for i in range(3)]
    return terms[0] + terms[1] + terms[2]


STEPS = (0, 1, -1, 2)


def scores_kernel(scale, at, *refs):
    image_in, text_in = refs[:8], refs[8:16]
    scores, img, txt, row_out, col_out, row_top, row_part = refs[16:]
    x, y, z, c = at[0], at[1], at[2], at[3]
    for ref, step in zip(image_in, (0, -1, 1, -2, 2, -3, 3, -4)):
        where = lax.rem(z + step + NZ, NZ) * SHARD
        img[pl.ds(pl.multiple_of(where, SHARD), SHARD), :] = ref[...]
    for own in range(2):
        core = c if own == 0 else 1 - c
        for i, d in enumerate(STEPS):
            for j, e in enumerate(STEPS):
                dx, dy = jnp.where(core == 0, d, e), jnp.where(core == 0, e, d)
                where = pl.multiple_of(core * PLANE + block_row(x - dx, y - dy), SHARD)
                txt[pl.ds(where, SHARD), :] = text_in[own * 4 + i][j * SHARD : (j + 1) * SHARD, :]

    chunk = 512
    row_part[...] = jnp.full((ROWS, 128), -jnp.inf, F32)

    @pl.loop(0, COLS // chunk)
    def _(i):
        cols = pl.ds(pl.multiple_of(i * chunk, chunk), chunk)
        s = scale * lax.dot_general(
            img[...], txt[cols, :], (((1,), (1,)), ((), ())), preferred_element_type=F32
        )
        scores[:, cols] = s
        tops = row_part[...]
        for j in range(chunk // 128):
            tops = jnp.maximum(tops, s[:, j * 128 : (j + 1) * 128])
        row_part[...] = tops
        top = jnp.max(s, axis=0, keepdims=True)
        col_out[:, cols] = top + jnp.log(jnp.sum(jnp.exp(s - top), axis=0, keepdims=True))

    row_top[...] = jnp.broadcast_to(jnp.max(row_part[...], axis=1, keepdims=True), (ROWS, 128))
    row_part[...] = jnp.zeros((ROWS, 128), F32)

    @pl.loop(0, COLS // chunk)
    def _(i):
        for j in range(chunk // 128):
            cols = pl.ds(pl.multiple_of(i * chunk + j * 128, 128), 128)
            row_part[...] += jnp.exp(scores[:, cols] - row_top[...])

    row = row_top[...] + jnp.log(jnp.sum(row_part[...], axis=1, keepdims=True))
    row_out[...] = jnp.transpose(row)[0:1, :]
    col_out[:, COLS:] = jnp.zeros((1, 128), F32)

    @pl.when(has_diagonal(x, y, z))
    def _():
        mask = on_diagonal(x)
        total = jnp.zeros((1, 128), F32)
        for row, col in diagonal_blocks(c):
            block = scores[row : row + SHARD, pl.ds(col, 128)]
            total += jnp.sum(jnp.where(mask, block, 0.0), axis=0, keepdims=True)
        total = jnp.sum(total, axis=1, keepdims=True)
        col_out[:, COLS:] = jnp.broadcast_to(total, (1, 128))


def concat_kernel(at, *refs):
    for i, ref in enumerate(refs[:-1]):
        refs[-1][i * SHARD : (i + 1) * SHARD, :] = ref[...]


def weights_kernel(at, scores, row_lse, col_lse, own_out, other_out, p_out, q_out, row_col):
    x, y, z, c = at[0], at[1], at[2], at[3]
    row_col[...] = jnp.transpose(jnp.broadcast_to(row_lse[...], (128, ROWS)))

    def weigh(s, rows, cols):
        return 0.5 * (jnp.exp(s - rows) + jnp.exp(s - cols))

    chunk = 128
    for half, out in ((1 - c, other_out), (c, own_out)):

        @pl.loop(0, PLANE // chunk)
        def _(i, half=half, out=out):
            cols = pl.ds(pl.multiple_of(half * PLANE + i * chunk, chunk), chunk)
            out[:, pl.ds(pl.multiple_of(i * chunk, chunk), chunk)] = weigh(
                scores[:, cols], row_col[...], col_lse[:, cols]
            ).astype(BF16)

    @pl.when(has_diagonal(x, y, z))
    def _():
        mask = on_diagonal(x).astype(F32)
        for zz, (row, col) in enumerate(diagonal_blocks(c)):
            rows, cols = pl.ds(row, SHARD), pl.ds(col, 128)
            block = (weigh(scores[rows, cols], row_col[rows, :], col_lse[:, cols]) - mask).astype(BF16)
            core = zz // 4
            within = pl.ds(pl.multiple_of(col - core * PLANE, 128), 128)

            @pl.when(c == core)
            def _():
                own_out[rows, within] = block

            @pl.when(c != core)
            def _():
                other_out[rows, within] = block

    row_sum = 0.5 * jnp.sum(row_lse[...], axis=1, keepdims=True)
    p_out[...] = jnp.broadcast_to(row_sum, (1, 128))
    col_sum = 0.5 * jnp.sum(col_lse[:, :COLS], axis=1, keepdims=True)
    q_out[...] = jnp.broadcast_to(col_sum, (1, 128)) - col_lse[:, COLS:]


def image_kernel(at, own, other, txt, q, *refs):
    up, down, up_far, down_far, here, up_two, down_two = refs[:7]
    total = refs[7]
    z, c = at[2], at[3]
    mine = pl.ds(pl.multiple_of(c * PLANE, PLANE), PLANE)
    theirs = pl.ds(pl.multiple_of((1 - c) * PLANE, PLANE), PLANE)
    chunk = 256

    @pl.loop(0, total.shape[1] // chunk)
    def _(i):
        cols = pl.ds(pl.multiple_of(i * chunk, chunk), chunk)
        total[:, cols] = jnp.dot(own[...], txt[mine, cols], preferred_element_type=F32) + jnp.dot(
            other[...], txt[theirs, cols], preferred_element_type=F32
        )

    def block(dz, start=0, size=SHARD):
        return total[pl.ds(pl.multiple_of(lax.rem(z + dz + NZ, NZ) * SHARD + start, HALF), size), :]

    up[:SHARD] = block(1).astype(BF16)
    up[SHARD : 2 * SHARD] = block(3).astype(BF16)
    down[:SHARD] = block(-1).astype(BF16)
    down[SHARD : 2 * SHARD] = block(-3).astype(BF16)
    up_far[:HALF] = block(4, 0, HALF).astype(BF16)
    down_far[:HALF] = block(4, HALF, HALF).astype(BF16)
    here[...] = block(0)
    up_two[...] = block(2)
    down_two[...] = block(-2)
    for ref in (up, down):
        write_note(ref.at[2 * SHARD :], q[...])
    for ref in (up_far, down_far):
        write_note(ref.at[HALF:], q[...])


def text_kernel(at, own, received, img, img_other, p_own, p_other, *refs):
    sent, kept, p_out = refs[:3], refs[3], refs[4]
    total = refs[5]
    x, y, c = at[0], at[1], at[3]
    p = p_own[...] + p_other[...]
    p_out[...] = p
    chunk = 256

    @pl.loop(0, PLANE // chunk)
    def _(i):
        cols = pl.ds(pl.multiple_of(i * chunk, chunk), chunk)
        total[cols, :] = lax.dot_general(
            own[:, cols], img[...], (((0,), (0,)), ((), ())), preferred_element_type=F32
        ) + lax.dot_general(
            received[:, cols], img_other[...], (((0,), (0,)), ((), ())), preferred_element_type=F32
        )

    for d in range(4):
        for e in range(4):
            dx, dy = jnp.where(c == 0, e, d), jnp.where(c == 0, d, e)
            part = total[pl.ds(block_row(x + dx, y + dy), SHARD), :]
            place = slice(e * SHARD, (e + 1) * SHARD)
            if d == 0:
                kept[place] = part
            else:
                sent[d - 1][place] = part.astype(BF16)
        if d:
            write_note(sent[d - 1].at[4 * SHARD :], p)


def image_middle_kernel(at, up, down, up_far, down_far, here, up_two, down_two, q, up_out, down_out, here_out, q_out):
    near, far = slice(0, SHARD), slice(SHARD, 2 * SHARD)
    here_out[...] = here[...] + up[near].astype(F32) + down[near].astype(F32)
    low, high = slice(0, HALF), slice(HALF, SHARD)
    above, below = up_two[...] + up[far].astype(F32), down_two[...] + down[far].astype(F32)
    up_out[low] = (above[low] + up_far[low].astype(F32)).astype(BF16)
    up_out[high] = above[high].astype(BF16)
    down_out[low] = below[low].astype(BF16)
    down_out[high] = (below[high] + down_far[low].astype(F32)).astype(BF16)
    note_up, note_down = read_note(up[2 * SHARD :]), read_note(down[2 * SHARD :])
    write_note(up_out.at[SHARD:], q[...] + note_up + read_note(up_far[HALF:]))
    write_note(down_out.at[SHARD:], q[...] + note_down)
    q_out[...] = q[...] + note_up + note_down


def text_middle_kernel(at, first, second, third, kept, p, *refs):
    sent, kept_out, p_out = refs[:3], refs[3], refs[4]
    total = p[...] + read_note(first[4 * SHARD :]) + read_note(second[4 * SHARD :]) + read_note(third[4 * SHARD :])
    p_out[...] = total
    for e in range(4):
        rows = slice(e * SHARD, (e + 1) * SHARD)
        part = kept[rows] + first[rows].astype(F32) + second[rows].astype(F32) + third[rows].astype(F32)
        if e == 0:
            kept_out[...] = part
        else:
            sent[e - 1][:SHARD] = part.astype(BF16)
            write_note(sent[e - 1].at[SHARD:], total)


def last_kernel(at, up, down, here, q, first, second, third, kept, p, image_out, text_out, loss_out):
    body = slice(0, SHARD)
    image_out[...] = (here[...] + up[body].astype(F32) + down[body].astype(F32)).astype(BF16)
    text = kept[...] + first[body].astype(F32) + second[body].astype(F32) + third[body].astype(F32)
    text_out[...] = text.astype(BF16)
    loss = q[...] + p[...]
    for message in (up, down, first, second, third):
        loss += read_note(message[SHARD:])
    loss_out[...] = loss / (ROWS * NC * NX * NY)


def shards(image, text):
    embed = image.shape[1]
    scale = 4.0 / math.sqrt(embed)
    me = lax.axis_index(AXES)
    at = jnp.stack([me // (NY * NZ * NC), lax.rem(me // (NZ * NC), NY), lax.rem(me // NC, NZ), lax.rem(me, NC)])
    at = at.astype(jnp.int32)

    up, down = shift_z(image, 1), shift_z(image, -1)
    near = [shift_plane(text, d, True) for d in STEPS[1:]]
    up, down, *near = lax.optimization_barrier((up, down, *near))
    (line,) = call(concat_kernel, [((4 * SHARD, embed), BF16)], [text, *near], [], 0, 0, 1 << 20, at, 4)
    far = [shift_plane(line, d, False) for d in STEPS[1:]]
    image_in = [image, up, down]
    up, down = lax.optimization_barrier((shift_z(up, 1), shift_z(down, -1)))
    image_in += [up, down]
    up, down, *far = lax.optimization_barrier((shift_z(up, 1), shift_z(down, -1), *far))
    image_in += [up, down]
    image_in.append(shift_z(up, 1))
    text_in = [line, *far]
    text_in += [swap_core(part) for part in text_in]

    tile = 2 * ROWS * COLS * embed
    scores, img, txt, row_lse, col_lse = call(
        functools.partial(scores_kernel, scale),
        [
            ((ROWS, COLS), F32),
            ((ROWS, embed), BF16),
            ((COLS, embed), BF16),
            ((1, ROWS), F32),
            ((1, COLS + 128), F32),
        ],
        image_in + text_in,
        [pltpu.VMEM((ROWS, 128), F32), pltpu.VMEM((ROWS, 128), F32)],
        tile,
        2 * ROWS * COLS,
        14 << 20,
        at,
        16,
    )
    img_other = swap_core(img)
    col_lse = merge_columns(col_lse, swap_core(col_lse))
    for axis, bit in ((1, 1), (1, 2), (0, 1), (0, 2)):
        col_lse = merge_columns(col_lse, swap(col_lse, axis, bit))
    for bit in (1, 2, 4):
        row_lse = merge(row_lse, swap(row_lse, 2, bit))

    half = ((ROWS, PLANE), BF16)
    scalar = ((1, 128), F32)
    own, other, p, q = call(
        weights_kernel,
        [half, half, scalar, scalar],
        (scores, row_lse, col_lse),
        [pltpu.VMEM((ROWS, 128), F32)],
        8 * ROWS * COLS,
        2 * ROWS * COLS,
        6 << 20,
        at,
        12,
    )
    received = swap_core(other)
    p_other = swap_core(p)
    message = lambda rows: ((rows + NOTE, embed), BF16)
    up, down, up_far, down_far, here, up_two, down_two = call(
        image_kernel,
        [message(2 * SHARD)] * 2 + [message(HALF)] * 2 + [((SHARD, embed), F32)] * 3,
        (own, other, txt, q),
        [pltpu.VMEM((ROWS, embed), F32)],
        tile,
        0,
        10 << 20,
        at,
        16,
    )
    received, here = lax.optimization_barrier((received, here))
    *sent, kept, p = call(
        text_kernel,
        [message(4 * SHARD)] * 3 + [((4 * SHARD, embed), F32), scalar],
        (own, received, img, img_other, p, p_other),
        [pltpu.VMEM((PLANE, embed), F32)],
        tile,
        0,
        8 << 20,
        at,
        20,
    )
    up, down = shift_z(up, 1), shift_z(down, -1)
    up_far, down_far = shift_z(up_far, 2), shift_z(down_far, -2)
    sent = [shift_plane(part, d, True) for d, part in enumerate(sent, 1)]
    up, down, here, q = call(
        image_middle_kernel,
        [message(SHARD)] * 2 + [((SHARD, embed), F32), scalar],
        (up, down, up_far, down_far, here, up_two, down_two, q),
        [],
        1 << 20,
        0,
        2 << 20,
        at,
        12,
    )
    up, down = shift_z(up, 2), shift_z(down, -2)
    *sent, kept, p = call(
        text_middle_kernel,
        [message(SHARD)] * 3 + [((SHARD, embed), F32), scalar],
        (*sent, kept, p),
        [],
        1 << 20,
        0,
        4 << 20,
        at,
        12,
    )
    sent = [shift_plane(part, d, False) for d, part in enumerate(sent, 1)]
    image_grad, text_grad, loss = call(
        last_kernel,
        [((SHARD, embed), BF16)] * 2 + [scalar],
        (up, down, here, q, *sent, kept, p),
        [],
        1 << 20,
        0,
        2 << 20,
        at,
        12,
    )
    return image_grad, text_grad, loss[0, 0]


def solution(mesh):
    return jax.shard_map(
        shards,
        mesh=mesh,
        in_specs=(P(("img", "txt"), None), P(("txt", "img"), None)),
        out_specs=(P(("img", "txt"), None), P(("txt", "img"), None), P()),
        check_vma=False,
    )
```

time: 504 us -> 131 us (0.26)
  blocking collectives: 200 us -> 0 us
  waiting for transfers between devices: 248 us -> 50.2 us
  starting transfers between devices: 0.16 us -> 56.4 us
  matrix products: 22.3 us -> 0 us
  Pallas kernels: 0 us -> 21 us
  between operations: 17.6 us -> 0.79 us
  other arithmetic: 7.36 us -> 0.35 us
    all_gather x2 -> x0, waiting for transfers between devices: 127 us -> none  [the longest x1 68.3 us: shards(): img_block = lax.all_gather(image, 'txt', axis=0, tiled=True)]
    all_gather x4 -> x0, blocking collectives: 125 us -> none  [combined_all(): pieces = jax.tree.map(lambda part: lax.all_gather(part, axis), value)]
    reduce_scatter x2 -> x0, waiting for transfers between devices: 119 us -> none  [the longest x1 119 us: shards(): lax.psum_scatter(jnp.dot(picked, txt_block, preferred_element_type=jnp.fl...]
    psum x1 -> x0, blocking collectives: 75.1 us -> none  [shards(): loss = lax.psum(local_loss, ('img', 'txt')) / pairs]
    ppermute x0 -> x40, starting transfers between devices: none -> 56.4 us  [the longest x13 23.9 us: shift_z(): return lax.ppermute(value, AXES, pairs)]
    ppermute x0 -> x40, waiting for transfers between devices: none -> 50.2 us  [the longest x13 36 us: shift_z(): return lax.ppermute(value, AXES, pairs)]
    dot_general x3 -> x0, matrix products: 22.3 us -> none  [the longest x1 8.74 us: shards(): lax.dot_general(picked, img_block, (((0,), (0,)), ((), ())), preferred_el...]
    pallas_call x0 -> x8, Pallas kernels: none -> 21 us  [call(): pl.pallas_call(kernel, out_shape=[jax.ShapeDtypeStruct(shape, dtype) for...]
  transfers between devices with their start and end apart: 4 -> 40, of which waited for: 3 -> 20; matrix products, arithmetic and copies ran while one was open for 2% -> 0% of each run, Pallas kernels for 0% -> 6%
where the time goes in v1:
time: 131 us; the launch traced here: 130 us
  starting transfers between devices  56.4 us (43%)
  waiting for transfers between devices  50.2 us (38%)
  Pallas kernels  21 us (16%)
    ppermute x13, waiting for transfers between devices, shift_z(): return lax.ppermute(value, AXES, pairs)  36 us
    ppermute x13, starting transfers between devices, shift_z(): return lax.ppermute(value, AXES, pairs)  23.9 us
    pallas_call x8, Pallas kernels, call(): pl.pallas_call(kernel, out_shape=[jax.ShapeDtypeStruct(shape, dtype) for...  21 us
    ppermute x12, starting transfers between devices, shift_plane(): return lax.ppermute(value, AXES, pairs)  18.5 us
    ppermute x15, starting transfers between devices, swap(): return lax.ppermute(value, AXES, pairs)  14 us
    ppermute x15, waiting for transfers between devices, swap(): return lax.ppermute(value, AXES, pairs)  7.2 us
    ppermute x12, waiting for transfers between devices, shift_plane(): return lax.ppermute(value, AXES, pairs)  6.98 us
  transfers between devices with their start and end apart: 40, of which 20 were waited for; matrix products, arithmetic and copies ran while one was open for 0% of the time, Pallas kernels for 6%

profile of v1, /device:TPU:32, one launch (start us, length us, event | category | flops | bytes accessed | tf_op | source)
XLA Modules:
  0.0 129.7 jit_solution(16369382114208584576)
XLA Ops:
  0.6 2.0 %collective-permute-start = (bf16[64,1280]{1,0:T(8,128)(2,1)}, bf16[64,1280]{1,0:T(8,128)(2,1)S(1)}, u32[]{:S(2)}, u32[]{:S(2)}) collective-permute-start(bf16[64,1280]{1,0:T(8,128)(2,1)} %refs_0_.3), channel_id=1, source_target_pairs={{0,2},{1,3},{2,4},{3,5},{4,6},{5,7},{6,8},{7,9},{8,10},{9,11},{10,... | collective-permute-start | bytes 491528 | tf_op jit(solution)/shard_map/ppermute | solution.py:31
  2.7 3.0 %collective-permute-start.3 = (bf16[64,1280]{1,0:T(8,128)(2,1)}, bf16[64,1280]{1,0:T(8,128)(2,1)S(1)}, u32[]{:S(2)}, u32[]{:S(2)}) collective-permute-start(bf16[64,1280]{1,0:T(8,128)(2,1)} %refs_0_.2), channel_id=1, source_target_pairs={{0,48},{1,193},{2,50},{3,195},{4,52},{5,197},{6,54},{7,199},{8,56}... | collective-permute-start | bytes 491528 | tf_op jit(solution)/shard_map/ppermute | solution.py:40
  5.8 2.2 %collective-permute-start.4 = (bf16[64,1280]{1,0:T(8,128)(2,1)}, bf16[64,1280]{1,0:T(8,128)(2,1)S(1)}, u32[]{:S(2)}, u32[]{:S(2)}) collective-permute-start(bf16[64,1280]{1,0:T(8,128)(2,1)} %refs_0_.2), channel_id=1, source_target_pairs={{0,32},{1,129},{2,34},{3,131},{4,36},{5,133},{6,38},{7,135},{8,40}... | collective-permute-start | bytes 491528 | tf_op jit(solution)/shard_map/ppermute | solution.py:40
  8.9 5.3 %collective-permute-done.2.refs_1_ = bf16[64,1280]{1,0:T(8,128)(2,1)S(1)} collective-permute-done((bf16[64,1280]{1,0:T(8,128)(2,1)}, bf16[64,1280]{1,0:T(8,128)(2,1)S(1)}, u32[]{:S(2)}, u32[]{:S(2)}) %collective-permute-start.2) | collective-permute-done | bytes 163872 | tf_op jit(solution)/shard_map/ppermute | solution.py:40
  14.2 0.9 copy-done
  15.8 3.1 %collective-permute-start.11 = (bf16[256,1280]{1,0:T(8,128)(2,1)S(1)}, bf16[256,1280]{1,0:T(8,128)(2,1)S(1)}, u32[]{:S(2)}, u32[]{:S(2)}) collective-permute-start(bf16[256,1280]{1,0:T(8,128)(2,1)S(1)} %shard_map.49.refs_8_), channel_id=1, source_target_pairs={{0,128},{1,33},{2,130},{3,35},{4,132},{5,37},{6,134},{7,39},{8,136... | collective-permute-start | bytes 1966088 | tf_op jit(solution)/shard_map/ppermute | solution.py:40
  18.9 1.1 collective-permute-start.10
  20.0 0.9 collective-permute-start.9
  20.9 1.9 %collective-permute-start.5 = (bf16[64,1280]{1,0:T(8,128)(2,1)S(1)}, bf16[64,1280]{1,0:T(8,128)(2,1)S(1)}, u32[]{:S(2)}, u32[]{:S(2)}) collective-permute-start(bf16[64,1280]{1,0:T(8,128)(2,1)S(1)} %collective-permute-done.refs_1_), channel_id=1, source_target_pairs={{0,2},{1,3},{2,4},{3,5},{4,6},{5,7},{6,8},{7,9},{8,10},{9,11},{10,... | collective-permute-start | bytes 491528 | tf_op jit(solution)/shard_map/ppermute | solution.py:31
  22.8 2.1 %collective-permute-start.6 = (bf16[64,1280]{1,0:T(8,128)(2,1)S(1)}, bf16[64,1280]{1,0:T(8,128)(2,1)S(1)}, u32[]{:S(2)}, u32[]{:S(2)}) collective-permute-start(bf16[64,1280]{1,0:T(8,128)(2,1)S(1)} %collective-permute-done.1.refs_2_), channel_id=1, source_target_pairs={{0,14},{1,15},{2,0},{3,1},{4,2},{5,3},{6,4},{7,5},{8,6},{9,7},{10,... | collective-permute-start | bytes 491528 | tf_op jit(solution)/shard_map/ppermute | solution.py:31
  24.9 3.3 %collective-permute-done.5.refs_3_ = bf16[64,1280]{1,0:T(8,128)(2,1)S(1)} collective-permute-done((bf16[64,1280]{1,0:T(8,128)(2,1)S(1)}, bf16[64,1280]{1,0:T(8,128)(2,1)S(1)}, u32[]{:S(2)}, u32[]{:S(2)}) %collective-permute-start.5) | collective-permute-done | bytes 163872 | tf_op jit(solution)/shard_map/ppermute | solution.py:31
  28.2 0.9 collective-permute-done.6.refs_4_
  29.1 3.2 %collective-permute-start.7 = (bf16[64,1280]{1,0:T(8,128)(2,1)S(1)}, bf16[64,1280]{1,0:T(8,128)(2,1)S(1)}, u32[]{:S(2)}, u32[]{:S(2)}) collective-permute-start(bf16[64,1280]{1,0:T(8,128)(2,1)S(1)} %collective-permute-done.5.refs_3_), channel_id=1, source_target_pairs={{0,2},{1,3},{2,4},{3,5},{4,6},{5,7},{6,8},{7,9},{8,10},{9,11},{10,... | collective-permute-start | bytes 491528 | tf_op jit(solution)/shard_map/ppermute | solution.py:31
  32.4 2.8 %collective-permute-done.7.refs_5_ = bf16[64,1280]{1,0:T(8,128)(2,1)S(1)} collective-permute-done((bf16[64,1280]{1,0:T(8,128)(2,1)S(1)}, bf16[64,1280]{1,0:T(8,128)(2,1)S(1)}, u32[]{:S(2)}, u32[]{:S(2)}) %collective-permute-start.7) | collective-permute-done | bytes 163872 | tf_op jit(solution)/shard_map/ppermute | solution.py:31
  35.2 4.0 %collective-permute-done.8.refs_6_ = bf16[64,1280]{1,0:T(8,128)(2,1)S(1)} collective-permute-done((bf16[64,1280]{1,0:T(8,128)(2,1)S(1)}, bf16[64,1280]{1,0:T(8,128)(2,1)S(1)}, u32[]{:S(2)}, u32[]{:S(2)}) %collective-permute-start.8) | collective-permute-done | bytes 163872 | tf_op jit(solution)/shard_map/ppermute | solution.py:31
  39.9 2.0 %collective-permute-start.12 = (bf16[64,1280]{1,0:T(8,128)(2,1)S(1)}, bf16[64,1280]{1,0:T(8,128)(2,1)S(1)}, u32[]{:S(2)}, u32[]{:S(2)}) collective-permute-start(bf16[64,1280]{1,0:T(8,128)(2,1)S(1)} %collective-permute-done.7.refs_5_), channel_id=1, source_target_pairs={{0,2},{1,3},{2,4},{3,5},{4,6},{5,7},{6,8},{7,9},{8,10},{9,11},{10,... | collective-permute-start | bytes 491528 | tf_op jit(solution)/shard_map/ppermute | solution.py:31
  41.9 4.5 %collective-permute-done.12.refs_7_ = bf16[64,1280]{1,0:T(8,128)(2,1)S(1)} collective-permute-done((bf16[64,1280]{1,0:T(8,128)(2,1)S(1)}, bf16[64,1280]{1,0:T(8,128)(2,1)S(1)}, u32[]{:S(2)}, u32[]{:S(2)}) %collective-permute-start.12) | collective-permute-done | bytes 163872 | tf_op jit(solution)/shard_map/ppermute | solution.py:31
  46.4 6.6 %shard_map.50 = (f32[512,2048]{1,0:T(8,128)S(1)}, bf16[512,1280]{1,0:T(8,128)(2,1)S(1)}, bf16[2048,1280]{1,0:T(8,128)(2,1)S(1)}, f32[1,512]{1,0:T(1,128)S(1)}, f32[1,2176]{1,0:T(1,128)S(1)}) custom-call(s32[4]{0:T(128)S(1)} %pad_add_fusion.at, bf16[64,1280]{1,0:T(8,128)(2,1)S(1)} %copy-done.1, bf16[64,1280]{1,0:T(8,128)(2,1)S(1)} %collective-permute-done.refs_1_, ...), custom_call_target="tpu_custom_call" | custom-call | flops 2684354560 | bytes 14680064 | tf_op jit(solution)/shard_map/pallas_call | solution.py:68
  53.1 1.2 collective-permute-done.20
  54.4 1.2 collective-permute-start.17
  55.6 2.4 %collective-permute-done.21 = f32[1,2176]{1,0:T(1,128)S(1)} collective-permute-done((f32[1,2176]{1,0:T(1,128)S(1)}, f32[1,2176]{1,0:T(1,128)S(1)}, u32[]{:S(2)}, u32[]{:S(2)}) %collective-permute-start.21) | collective-permute-done | bytes 8736 | tf_op jit(solution)/shard_map/ppermute | solution.py:49
  58.1 1.0 collective-permute-start.22
  59.2 2.8 %collective-permute-start.18 = (f32[1,512]{1,0:T(1,128)S(1)}, f32[1,512]{1,0:T(1,128)S(1)}, u32[]{:S(2)}, u32[]{:S(2)}) collective-permute-start(f32[1,512]{1,0:T(1,128)S(1)} %log_add_fusion.2), channel_id=1, source_target_pairs={{0,4},{1,5},{2,6},{3,7},{4,0},{5,1},{6,2},{7,3},{8,12},{9,13},{10,... | collective-permute-start | bytes 6152 | tf_op jit(solution)/shard_map/ppermute | solution.py:49
  62.0 1.3 %collective-permute-done.22 = f32[1,2176]{1,0:T(1,128)S(1)} collective-permute-done((f32[1,2176]{1,0:T(1,128)S(1)}, f32[1,2176]{1,0:T(1,128)S(1)}, u32[]{:S(2)}, u32[]{:S(2)}) %collective-permute-start.22) | collective-permute-done | bytes 8736 | tf_op jit(solution)/shard_map/ppermute | solution.py:49
  63.4 1.9 %collective-permute-start.23 = (f32[1,2176]{1,0:T(1,128)S(1)}, f32[1,2176]{1,0:T(1,128)S(1)}, u32[]{:S(2)}, u32[]{:S(2)}) collective-permute-start(f32[1,2176]{1,0:T(1,128)S(1)} %add_select_fusion.2), channel_id=1, source_target_pairs={{0,64},{1,65},{2,66},{3,67},{4,68},{5,69},{6,70},{7,71},{8,72},{9,... | collective-permute-start | bytes 26120 | tf_op jit(solution)/shard_map/ppermute | solution.py:49
  65.3 2.7 %collective-permute-start.19 = (f32[1,512]{1,0:T(1,128)S(1)}, f32[1,512]{1,0:T(1,128)S(1)}, u32[]{:S(2)}, u32[]{:S(2)}) collective-permute-start(f32[1,512]{1,0:T(1,128)S(1)} %log_add_fusion.1), channel_id=1, source_target_pairs={{0,8},{1,9},{2,10},{3,11},{4,12},{5,13},{6,14},{7,15},{8,0},{9,1},... | collective-permute-start | bytes 6152 | tf_op jit(solution)/shard_map/ppermute | solution.py:49
  68.1 3.0 %collective-permute-start.24 = (f32[1,2176]{1,0:T(1,128)S(1)}, f32[1,2176]{1,0:T(1,128)S(1)}, u32[]{:S(2)}, u32[]{:S(2)}) collective-permute-start(f32[1,2176]{1,0:T(1,128)S(1)} %add_select_fusion.1), channel_id=1, source_target_pairs={{0,128},{1,129},{2,130},{3,131},{4,132},{5,133},{6,134},{7,135},{8... | collective-permute-start | bytes 26120 | tf_op jit(solution)/shard_map/ppermute | solution.py:49
  71.0 1.9 %collective-permute-done.19 = f32[1,512]{1,0:T(1,128)S(1)} collective-permute-done((f32[1,512]{1,0:T(1,128)S(1)}, f32[1,512]{1,0:T(1,128)S(1)}, u32[]{:S(2)}, u32[]{:S(2)}) %collective-permute-start.19) | collective-permute-done | bytes 2080 | tf_op jit(solution)/shard_map/ppermute | solution.py:49
  73.4 2.2 %shard_map.51 = (bf16[512,1024]{1,0:T(8,128)(2,1)S(1)}, bf16[512,1024]{1,0:T(8,128)(2,1)S(1)}, f32[1,128]{1,0:T(1,128)S(1)}, f32[1,128]{1,0:T(1,128)S(1)}) custom-call(s32[4]{0:T(128)S(1)} %pad_add_fusion.at, f32[512,2048]{1,0:T(8,128)S(1)} %get-tuple-element.62.scores, f32[1,512]{1,0:T(1,128)S(1)} %log_add_fusion.row_lse, f32[1,2176]{1,0:T(1,128)S(1)} %add_select_fusion.col_lse), custom_call_target="tpu_custom_call" | custom-call | flops 8388608 | bytes 6291456 | tf_op jit(solution)/shard_map/pallas_call | solution.py:68
  76.1 4.3 %shard_map.52 = (bf16[144,1280]{1,0:T(8,128)(2,1)S(1)}, bf16[144,1280]{1,0:T(8,128)(2,1)S(1)}, bf16[48,1280]{1,0:T(8,128)(2,1)S(1)}, bf16[48,1280]{1,0:T(8,128)(...) custom-call(s32[4]{0:T(128)S(1)} %pad_add_fusion.at, ...), custom_call_target="tpu_custom_call" | custom-call | flops 2684354560 | bytes 10485760 | tf_op jit(solution)/shard_map/pallas_call | solution.py:68
  80.5 4.4 %shard_map.54 = (bf16[272,1280]{1,0:T(8,128)(2,1)S(1)}, bf16[272,1280]{1,0:T(8,128)(2,1)S(1)}, bf16[272,1280]{1,0:T(8,128)(2,1)S(1)}, f32[256,1280]{1,0:T(8,128)S(1)}, f32[1,128]{1,0:T(1,128)S(1)}) custom-call(s32[4]{0:T(128)S(1)} %pad_add_fusion.at, bf16[512,1024]{1,0:T(8,128)(2,1)S(1)} %get-tuple-element.65.own, ...), custom_call_target="tpu_custom_call" | custom-call | flops 2684354560 | bytes 8388608 | tf_op jit(solution)/shard_map/pallas_call | solution.py:68
  84.9 1.4 %collective-permute-start.34 = (bf16[272,1280]{1,0:T(8,128)(2,1)S(1)}, bf16[272,1280]{1,0:T(8,128)(2,1)S(1)}, u32[]{:S(2)}, u32[]{:S(2)}) collective-permute-start(bf16[272,1280]{1,0:T(8,128)(2,1)S(1)} %get-tuple-element.84), channel_id=1, source_target_pairs={{0,16},{1,65},{2,18},{3,67},{4,20},{5,69},{6,22},{7,71},{8,24},{9,... | collective-permute-start | bytes 2088968 | tf_op jit(solution)/shard_map/ppermute | solution.py:40
  86.3 1.6 %collective-permute-start.35 = (bf16[272,1280]{1,0:T(8,128)(2,1)S(1)}, bf16[272,1280]{1,0:T(8,128)(2,1)S(1)}, u32[]{:S(2)}, u32[]{:S(2)}) collective-permute-start(bf16[272,1280]{1,0:T(8,128)(2,1)S(1)} %get-tuple-element.85), channel_id=1, source_target_pairs={{0,32},{1,129},{2,34},{3,131},{4,36},{5,133},{6,38},{7,135},{8,40}... | collective-permute-start | bytes 2088968 | tf_op jit(solution)/shard_map/ppermute | solution.py:40
  87.9 1.8 %collective-permute-start.36 = (bf16[272,1280]{1,0:T(8,128)(2,1)S(1)}, bf16[272,1280]{1,0:T(8,128)(2,1)S(1)}, u32[]{:S(2)}, u32[]{:S(2)}) collective-permute-start(bf16[272,1280]{1,0:T(8,128)(2,1)S(1)} %get-tuple-element.86), channel_id=1, source_target_pairs={{0,48},{1,193},{2,50},{3,195},{4,52},{5,197},{6,54},{7,199},{8,56}... | collective-permute-start | bytes 2088968 | tf_op jit(solution)/shard_map/ppermute | solution.py:40
  89.7 1.4 %collective-permute-start.27 = (bf16[48,1280]{1,0:T(8,128)(2,1)S(1)}, bf16[48,1280]{1,0:T(8,128)(2,1)S(1)}, u32[]{:S(2)}, u32[]{:S(2)}) collective-permute-start(bf16[48,1280]{1,0:T(8,128)(2,1)S(1)} %get-tuple-element.71), channel_id=1, source_target_pairs={{0,4},{1,5},{2,6},{3,7},{4,8},{5,9},{6,10},{7,11},{8,12},{9,13},{1... | collective-permute-start | bytes 368648 | tf_op jit(solution)/shard_map/ppermute | solution.py:31
  91.1 2.7 %collective-permute-start.28 = (bf16[48,1280]{1,0:T(8,128)(2,1)S(1)}, bf16[48,1280]{1,0:T(8,128)(2,1)S(1)}, u32[]{:S(2)}, u32[]{:S(2)}) collective-permute-start(bf16[48,1280]{1,0:T(8,128)(2,1)S(1)} %get-tuple-element.72), channel_id=1, source_target_pairs={{0,12},{1,13},{2,14},{3,15},{4,0},{5,1},{6,2},{7,3},{8,4},{9,5},{1... | collective-permute-start | bytes 368648 | tf_op jit(solution)/shard_map/ppermute | solution.py:31
  93.9 4.3 %collective-permute-done.27.up_far = bf16[48,1280]{1,0:T(8,128)(2,1)S(1)} collective-permute-done((bf16[48,1280]{1,0:T(8,128)(2,1)S(1)}, bf16[48,1280]{1,0:T(8,128)(2,1)S(1)}, u32[]{:S(2)}, u32[]{:S(2)}) %collective-permute-start.27) | collective-permute-done | bytes 122912 | tf_op jit(solution)/shard_map/ppermute | solution.py:31
  98.2 2.2 %collective-permute-start.25 = (bf16[144,1280]{1,0:T(8,128)(2,1)S(1)}, bf16[144,1280]{1,0:T(8,128)(2,1)S(1)}, u32[]{:S(2)}, u32[]{:S(2)}) collective-permute-start(bf16[144,1280]{1,0:T(8,128)(2,1)S(1)} %get-tuple-element.69), channel_id=1, source_target_pairs={{0,2},{1,3},{2,4},{3,5},{4,6},{5,7},{6,8},{7,9},{8,10},{9,11},{10,... | collective-permute-start | bytes 1105928 | tf_op jit(solution)/shard_map/ppermute | solution.py:31
  100.3 1.8 %collective-permute-start.26 = (bf16[144,1280]{1,0:T(8,128)(2,1)S(1)}, bf16[144,1280]{1,0:T(8,128)(2,1)S(1)}, u32[]{:S(2)}, u32[]{:S(2)}) collective-permute-start(bf16[144,1280]{1,0:T(8,128)(2,1)S(1)} %get-tuple-element.70), channel_id=1, source_target_pairs={{0,14},{1,15},{2,0},{3,1},{4,2},{5,3},{6,4},{7,5},{8,6},{9,7},{10,... | collective-permute-start | bytes 1105928 | tf_op jit(solution)/shard_map/ppermute | solution.py:31
  102.1 9.0 %collective-permute-done.25.up = bf16[144,1280]{1,0:T(8,128)(2,1)S(1)} collective-permute-done((bf16[144,1280]{1,0:T(8,128)(2,1)S(1)}, bf16[144,1280]{1,0:T(8,128)(2,1)S(1)}, u32[]{:S(2)}, u32[]{:S(2)}) %collective-permute-start.25) | collective-permute-done | bytes 368672 | tf_op jit(solution)/shard_map/ppermute | solution.py:31
  111.1 1.1 collective-permute-done.26.down
  112.9 3.0 %collective-permute-start.30 = (bf16[80,1280]{1,0:T(8,128)(2,1)S(1)}, bf16[80,1280]{1,0:T(8,128)(2,1)S(1)}, u32[]{:S(2)}, u32[]{:S(2)}) collective-permute-start(bf16[80,1280]{1,0:T(8,128)(2,1)S(1)} %get-tuple-element.77), channel_id=1, source_target_pairs={{0,4},{1,5},{2,6},{3,7},{4,8},{5,9},{6,10},{7,11},{8,12},{9,13},{1... | collective-permute-start | bytes 614408 | tf_op jit(solution)/shard_map/ppermute | solution.py:31
  115.8 1.4 %collective-permute-start.31 = (bf16[80,1280]{1,0:T(8,128)(2,1)S(1)}, bf16[80,1280]{1,0:T(8,128)(2,1)S(1)}, u32[]{:S(2)}, u32[]{:S(2)}) collective-permute-start(bf16[80,1280]{1,0:T(8,128)(2,1)S(1)} %get-tuple-element.78), channel_id=1, source_target_pairs={{0,12},{1,13},{2,14},{3,15},{4,0},{5,1},{6,2},{7,3},{8,4},{9,5},{1... | collective-permute-start | bytes 614408 | tf_op jit(solution)/shard_map/ppermute | solution.py:31
  118.6 2.8 %collective-permute-start.39 = (bf16[80,1280]{1,0:T(8,128)(2,1)S(1)}, bf16[80,1280]{1,0:T(8,128)(2,1)S(1)}, u32[]{:S(2)}, u32[]{:S(2)}) collective-permute-start(bf16[80,1280]{1,0:T(8,128)(2,1)S(1)} %get-tuple-element.91), channel_id=1, source_target_pairs={{0,192},{1,49},{2,194},{3,51},{4,196},{5,53},{6,198},{7,55},{8,200... | collective-permute-start | bytes 614408 | tf_op jit(solution)/shard_map/ppermute | solution.py:40
  121.5 4.4 %collective-permute-done.30.up = bf16[80,1280]{1,0:T(8,128)(2,1)S(1)} collective-permute-done((bf16[80,1280]{1,0:T(8,128)(2,1)S(1)}, bf16[80,1280]{1,0:T(8,128)(2,1)S(1)}, u32[]{:S(2)}, u32[]{:S(2)}) %collective-permute-start.30) | collective-permute-done | bytes 204832 | tf_op jit(solution)/shard_map/ppermute | solution.py:31
  125.9 1.0 collective-permute-done.31.down
  127.4 0.9 collective-permute-done.39.third
  128.3 1.3 %shard_map.56 = (bf16[64,1280]{1,0:T(8,128)(2,1)}, bf16[64,1280]{1,0:T(8,128)(2,1)}, f32[1,128]{1,0:T(1,128)}) custom-call(s32[4]{0:T(128)S(1)} %pad_add_fusion.at, bf16[80,1280]{1,0:T(8,128)(2,1)S(1)} %collective-permute-done.30.up, bf16[80,1280]{1,0:T(8,128)(2,1)S(1)} %collective-permute-done.31.down, f32[64,1280]{1,0:T(8,128)S(1)} %get-tuple-element.79.here, ...), custom_call_target="tpu_custom_call" | custom-call | flops 1048576 | bytes 2097152 | tf_op jit(solution)/shard_map/pallas_call | solution.py:68
  (53 shorter events, 6.3 us)
Async XLA Ops:
  0.6 7.4 %collective-permute-start = (bf16[64,1280]{1,0:T(8,128)(2,1)}, bf16[64,1280]{1,0:T(8,128)(2,1)S(1)}, u32[]{:S(2)}, u32[]{:S(2)}) collective-permute-start(bf16[64,1280]{1,0:T(8,128)(2,1)} %refs_0_.3), channel_id=1, source_target_pairs={{0,2},{1,3},{2,4},{3,5},{4,6},{5,7},{6,8},{7,9},{8,10},{9,11},{10,... | collective-permute-start | bytes 491528 | tf_op jit(solution)/shard_map/ppermute | solution.py:31
  2.6 6.1 %collective-permute-start.1 = (bf16[64,1280]{1,0:T(8,128)(2,1)}, bf16[64,1280]{1,0:T(8,128)(2,1)S(1)}, u32[]{:S(2)}, u32[]{:S(2)}) collective-permute-start(bf16[64,1280]{1,0:T(8,128)(2,1)} %refs_0_.3), channel_id=1, source_target_pairs={{0,14},{1,15},{2,0},{3,1},{4,2},{5,3},{6,4},{7,5},{8,6},{9,7},{10,... | collective-permute-start | bytes 491528 | tf_op jit(solution)/shard_map/ppermute | solution.py:31
  2.7 6.2 %collective-permute-start.3 = (bf16[64,1280]{1,0:T(8,128)(2,1)}, bf16[64,1280]{1,0:T(8,128)(2,1)S(1)}, u32[]{:S(2)}, u32[]{:S(2)}) collective-permute-start(bf16[64,1280]{1,0:T(8,128)(2,1)} %refs_0_.2), channel_id=1, source_target_pairs={{0,48},{1,193},{2,50},{3,195},{4,52},{5,197},{6,54},{7,199},{8,56}... | collective-permute-start | bytes 491528 | tf_op jit(solution)/shard_map/ppermute | solution.py:40
  5.7 8.5 %collective-permute-start.2 = (bf16[64,1280]{1,0:T(8,128)(2,1)}, bf16[64,1280]{1,0:T(8,128)(2,1)S(1)}, u32[]{:S(2)}, u32[]{:S(2)}) collective-permute-start(bf16[64,1280]{1,0:T(8,128)(2,1)} %refs_0_.2), channel_id=1, source_target_pairs={{0,16},{1,65},{2,18},{3,67},{4,20},{5,69},{6,22},{7,71},{8,24},{9,... | collective-permute-start | bytes 491528 | tf_op jit(solution)/shard_map/ppermute | solution.py:40
  5.8 8.5 %collective-permute-start.4 = (bf16[64,1280]{1,0:T(8,128)(2,1)}, bf16[64,1280]{1,0:T(8,128)(2,1)S(1)}, u32[]{:S(2)}, u32[]{:S(2)}) collective-permute-start(bf16[64,1280]{1,0:T(8,128)(2,1)} %refs_0_.2), channel_id=1, source_target_pairs={{0,32},{1,129},{2,34},{3,131},{4,36},{5,133},{6,38},{7,135},{8,40}... | collective-permute-start | bytes 491528 | tf_op jit(solution)/shard_map/ppermute | solution.py:40
  14.2 0.9 copy-start
  15.2 31.3 %copy-start.1 = (bf16[64,1280]{1,0:T(8,128)(2,1)S(1)}, bf16[64,1280]{1,0:T(8,128)(2,1)}, u32[]{:S(2)}) copy-start(bf16[64,1280]{1,0:T(8,128)(2,1)} %refs_0_.3) | copy-start | bytes 491524
  15.8 23.4 %collective-permute-start.11 = (bf16[256,1280]{1,0:T(8,128)(2,1)S(1)}, bf16[256,1280]{1,0:T(8,128)(2,1)S(1)}, u32[]{:S(2)}, u32[]{:S(2)}) collective-permute-start(bf16[256,1280]{1,0:T(8,128)(2,1)S(1)} %shard_map.49.refs_8_), channel_id=1, source_target_pairs={{0,128},{1,33},{2,130},{3,35},{4,132},{5,37},{6,134},{7,39},{8,136... | collective-permute-start | bytes 1966088 | tf_op jit(solution)/shard_map/ppermute | solution.py:40
  18.9 20.3 %collective-permute-start.10 = (bf16[256,1280]{1,0:T(8,128)(2,1)S(1)}, bf16[256,1280]{1,0:T(8,128)(2,1)S(1)}, u32[]{:S(2)}, u32[]{:S(2)}) collective-permute-start(bf16[256,1280]{1,0:T(8,128)(2,1)S(1)} %shard_map.49.refs_8_), channel_id=1, source_target_pairs={{0,192},{1,49},{2,194},{3,51},{4,196},{5,53},{6,198},{7,55},{8,200... | collective-permute-start | bytes 1966088 | tf_op jit(solution)/shard_map/ppermute | solution.py:40
  20.0 19.2 %collective-permute-start.9 = (bf16[256,1280]{1,0:T(8,128)(2,1)S(1)}, bf16[256,1280]{1,0:T(8,128)(2,1)S(1)}, u32[]{:S(2)}, u32[]{:S(2)}) collective-permute-start(bf16[256,1280]{1,0:T(8,128)(2,1)S(1)} %shard_map.49.refs_8_), channel_id=1, source_target_pairs={{0,64},{1,17},{2,66},{3,19},{4,68},{5,21},{6,70},{7,23},{8,72},{9,... | collective-permute-start | bytes 1966088 | tf_op jit(solution)/shard_map/ppermute | solution.py:40
  20.9 7.3 %collective-permute-start.5 = (bf16[64,1280]{1,0:T(8,128)(2,1)S(1)}, bf16[64,1280]{1,0:T(8,128)(2,1)S(1)}, u32[]{:S(2)}, u32[]{:S(2)}) collective-permute-start(bf16[64,1280]{1,0:T(8,128)(2,1)S(1)} %collective-permute-done.refs_1_), channel_id=1, source_target_pairs={{0,2},{1,3},{2,4},{3,5},{4,6},{5,7},{6,8},{7,9},{8,10},{9,11},{10,... | collective-permute-start | bytes 491528 | tf_op jit(solution)/shard_map/ppermute | solution.py:31
  22.8 6.3 %collective-permute-start.6 = (bf16[64,1280]{1,0:T(8,128)(2,1)S(1)}, bf16[64,1280]{1,0:T(8,128)(2,1)S(1)}, u32[]{:S(2)}, u32[]{:S(2)}) collective-permute-start(bf16[64,1280]{1,0:T(8,128)(2,1)S(1)} %collective-permute-done.1.refs_2_), channel_id=1, source_target_pairs={{0,14},{1,15},{2,0},{3,1},{4,2},{5,3},{6,4},{7,5},{8,6},{9,7},{10,... | collective-permute-start | bytes 491528 | tf_op jit(solution)/shard_map/ppermute | solution.py:31
  29.1 6.1 %collective-permute-start.7 = (bf16[64,1280]{1,0:T(8,128)(2,1)S(1)}, bf16[64,1280]{1,0:T(8,128)(2,1)S(1)}, u32[]{:S(2)}, u32[]{:S(2)}) collective-permute-start(bf16[64,1280]{1,0:T(8,128)(2,1)S(1)} %collective-permute-done.5.refs_3_), channel_id=1, source_target_pairs={{0,2},{1,3},{2,4},{3,5},{4,6},{5,7},{6,8},{7,9},{8,10},{9,11},{10,... | collective-permute-start | bytes 491528 | tf_op jit(solution)/shard_map/ppermute | solution.py:31
  32.4 6.8 %collective-permute-start.8 = (bf16[64,1280]{1,0:T(8,128)(2,1)S(1)}, bf16[64,1280]{1,0:T(8,128)(2,1)S(1)}, u32[]{:S(2)}, u32[]{:S(2)}) collective-permute-start(bf16[64,1280]{1,0:T(8,128)(2,1)S(1)} %collective-permute-done.6.refs_4_), channel_id=1, source_target_pairs={{0,14},{1,15},{2,0},{3,1},{4,2},{5,3},{6,4},{7,5},{8,6},{9,7},{10,... | collective-permute-start | bytes 491528 | tf_op jit(solution)/shard_map/ppermute | solution.py:31
  35.2 6.7 %collective-permute-start.13 = (bf16[256,1280]{1,0:T(8,128)(2,1)S(1)}, bf16[256,1280]{1,0:T(8,128)(2,1)S(1)}, u32[]{:S(2)}, u32[]{:S(2)}) collective-permute-start(bf16[256,1280]{1,0:T(8,128)(2,1)S(1)} %shard_map.49.refs_8_), channel_id=1, source_target_pairs={{0,1},{1,0},{2,3},{3,2},{4,5},{5,4},{6,7},{7,6},{8,9},{9,8},{10,11... | collective-permute-start | bytes 1966088 | tf_op jit(solution)/shard_map/ppermute | solution.py:49
  39.2 7.2 %collective-permute-start.14 = (bf16[256,1280]{1,0:T(8,128)(2,1)S(1)}, bf16[256,1280]{1,0:T(8,128)(2,1)S(1)}, u32[]{:S(2)}, u32[]{:S(2)}) collective-permute-start(bf16[256,1280]{1,0:T(8,128)(2,1)S(1)} %collective-permute-done.9.refs_9_), channel_id=1, source_target_pairs={{0,1},{1,0},{2,3},{3,2},{4,5},{5,4},{6,7},{7,6},{8,9},{9,8},{10,11... | collective-permute-start | bytes 1966088 | tf_op jit(solution)/shard_map/ppermute | solution.py:49
  39.3 7.1 %collective-permute-start.15 = (bf16[256,1280]{1,0:T(8,128)(2,1)S(1)}, bf16[256,1280]{1,0:T(8,128)(2,1)S(1)}, u32[]{:S(2)}, u32[]{:S(2)}) collective-permute-start(bf16[256,1280]{1,0:T(8,128)(2,1)S(1)} %collective-permute-done.10.refs_10_), channel_id=1, source_target_pairs={{0,1},{1,0},{2,3},{3,2},{4,5},{5,4},{6,7},{7,6},{8,9},{9,8},{10,11... | collective-permute-start | bytes 1966088 | tf_op jit(solution)/shard_map/ppermute | solution.py:49
  39.8 6.6 %collective-permute-start.16 = (bf16[256,1280]{1,0:T(8,128)(2,1)S(1)}, bf16[256,1280]{1,0:T(8,128)(2,1)S(1)}, u32[]{:S(2)}, u32[]{:S(2)}) collective-permute-start(bf16[256,1280]{1,0:T(8,128)(2,1)S(1)} %collective-permute-done.11.refs_11_), channel_id=1, source_target_pairs={{0,1},{1,0},{2,3},{3,2},{4,5},{5,4},{6,7},{7,6},{8,9},{9,8},{10,11... | collective-permute-start | bytes 1966088 | tf_op jit(solution)/shard_map/ppermute | solution.py:49
  39.9 6.5 %collective-permute-start.12 = (bf16[64,1280]{1,0:T(8,128)(2,1)S(1)}, bf16[64,1280]{1,0:T(8,128)(2,1)S(1)}, u32[]{:S(2)}, u32[]{:S(2)}) collective-permute-start(bf16[64,1280]{1,0:T(8,128)(2,1)S(1)} %collective-permute-done.7.refs_5_), channel_id=1, source_target_pairs={{0,2},{1,3},{2,4},{3,5},{4,6},{5,7},{6,8},{7,9},{8,10},{9,11},{10,... | collective-permute-start | bytes 491528 | tf_op jit(solution)/shard_map/ppermute | solution.py:31
  53.0 1.2 collective-permute-start.20
  54.3 3.7 %collective-permute-start.21 = (f32[1,2176]{1,0:T(1,128)S(1)}, f32[1,2176]{1,0:T(1,128)S(1)}, u32[]{:S(2)}, u32[]{:S(2)}) collective-permute-start(f32[1,2176]{1,0:T(1,128)S(1)} %add_select_fusion.4), channel_id=1, source_target_pairs={{0,16},{1,17},{2,18},{3,19},{4,20},{5,21},{6,22},{7,23},{8,24},{9,... | collective-permute-start | bytes 26120 | tf_op jit(solution)/shard_map/ppermute | solution.py:49
  54.4 4.7 %collective-permute-start.17 = (f32[1,512]{1,0:T(1,128)S(1)}, f32[1,512]{1,0:T(1,128)S(1)}, u32[]{:S(2)}, u32[]{:S(2)}) collective-permute-start(f32[1,512]{1,0:T(1,128)S(1)} %get-tuple-element.63), channel_id=1, source_target_pairs={{0,2},{1,3},{2,0},{3,1},{4,6},{5,7},{6,4},{7,5},{8,10},{9,11},{10,... | collective-permute-start | bytes 6152 | tf_op jit(solution)/shard_map/ppermute | solution.py:49
  55.6 24.8 %collective-permute-start.32 = (bf16[512,1280]{1,0:T(8,128)(2,1)S(1)}, bf16[512,1280]{1,0:T(8,128)(2,1)S(1)}, u32[]{:S(2)}, u32[]{:S(2)}) collective-permute-start(bf16[512,1280]{1,0:T(8,128)(2,1)S(1)} %get-tuple-element.82.img), channel_id=1, source_target_pairs={{0,1},{1,0},{2,3},{3,2},{4,5},{5,4},{6,7},{7,6},{8,9},{9,8},{10,11... | collective-permute-start | bytes 3932168 | tf_op jit(solution)/shard_map/ppermute | solution.py:49
  58.1 5.2 %collective-permute-start.22 = (f32[1,2176]{1,0:T(1,128)S(1)}, f32[1,2176]{1,0:T(1,128)S(1)}, u32[]{:S(2)}, u32[]{:S(2)}) collective-permute-start(f32[1,2176]{1,0:T(1,128)S(1)} %add_select_fusion.3), channel_id=1, source_target_pairs={{0,32},{1,33},{2,34},{3,35},{4,36},{5,37},{6,38},{7,39},{8,40},{9,... | collective-permute-start | bytes 26120 | tf_op jit(solution)/shard_map/ppermute | solution.py:49
  59.2 6.1 %collective-permute-start.18 = (f32[1,512]{1,0:T(1,128)S(1)}, f32[1,512]{1,0:T(1,128)S(1)}, u32[]{:S(2)}, u32[]{:S(2)}) collective-permute-start(f32[1,512]{1,0:T(1,128)S(1)} %log_add_fusion.2), channel_id=1, source_target_pairs={{0,4},{1,5},{2,6},{3,7},{4,0},{5,1},{6,2},{7,3},{8,12},{9,13},{10,... | collective-permute-start | bytes 6152 | tf_op jit(solution)/shard_map/ppermute | solution.py:49
  63.4 4.6 %collective-permute-start.23 = (f32[1,2176]{1,0:T(1,128)S(1)}, f32[1,2176]{1,0:T(1,128)S(1)}, u32[]{:S(2)}, u32[]{:S(2)}) collective-permute-start(f32[1,2176]{1,0:T(1,128)S(1)} %add_select_fusion.2), channel_id=1, source_target_pairs={{0,64},{1,65},{2,66},{3,67},{4,68},{5,69},{6,70},{7,71},{8,72},{9,... | collective-permute-start | bytes 26120 | tf_op jit(solution)/shard_map/ppermute | solution.py:49
  65.3 7.6 %collective-permute-start.19 = (f32[1,512]{1,0:T(1,128)S(1)}, f32[1,512]{1,0:T(1,128)S(1)}, u32[]{:S(2)}, u32[]{:S(2)}) collective-permute-start(f32[1,512]{1,0:T(1,128)S(1)} %log_add_fusion.1), channel_id=1, source_target_pairs={{0,8},{1,9},{2,10},{3,11},{4,12},{5,13},{6,14},{7,15},{8,0},{9,1},... | collective-permute-start | bytes 6152 | tf_op jit(solution)/shard_map/ppermute | solution.py:49
  68.1 5.2 %collective-permute-start.24 = (f32[1,2176]{1,0:T(1,128)S(1)}, f32[1,2176]{1,0:T(1,128)S(1)}, u32[]{:S(2)}, u32[]{:S(2)}) collective-permute-start(f32[1,2176]{1,0:T(1,128)S(1)} %add_select_fusion.1), channel_id=1, source_target_pairs={{0,128},{1,129},{2,130},{3,131},{4,132},{5,133},{6,134},{7,135},{8... | collective-permute-start | bytes 26120 | tf_op jit(solution)/shard_map/ppermute | solution.py:49
  75.6 4.9 %collective-permute-start.29 = (bf16[512,1024]{1,0:T(8,128)(2,1)S(1)}, bf16[512,1024]{1,0:T(8,128)(2,1)S(1)}, u32[]{:S(2)}, u32[]{:S(2)}) collective-permute-start(bf16[512,1024]{1,0:T(8,128)(2,1)S(1)} %get-tuple-element.66.other), channel_id=1, source_target_pairs={{0,1},{1,0},{2,3},{3,2},{4,5},{5,4},{6,7},{7,6},{8,9},{9,8},{10,11... | collective-permute-start | bytes 3145736 | tf_op jit(solution)/shard_map/ppermute | solution.py:49
  75.6 4.9 %collective-permute-start.33 = (f32[1,128]{1,0:T(1,128)S(1)}, f32[1,128]{1,0:T(1,128)S(1)}, u32[]{:S(2)}, u32[]{:S(2)}) collective-permute-start(f32[1,128]{1,0:T(1,128)S(1)} %get-tuple-element.83.p_own), channel_id=1, source_target_pairs={{0,1},{1,0},{2,3},{3,2},{4,5},{5,4},{6,7},{7,6},{8,9},{9,8},{10,11... | collective-permute-start | bytes 1544 | tf_op jit(solution)/shard_map/ppermute | solution.py:49
  84.9 32.4 %collective-permute-start.34 = (bf16[272,1280]{1,0:T(8,128)(2,1)S(1)}, bf16[272,1280]{1,0:T(8,128)(2,1)S(1)}, u32[]{:S(2)}, u32[]{:S(2)}) collective-permute-start(bf16[272,1280]{1,0:T(8,128)(2,1)S(1)} %get-tuple-element.84), channel_id=1, source_target_pairs={{0,16},{1,65},{2,18},{3,67},{4,20},{5,69},{6,22},{7,71},{8,24},{9,... | collective-permute-start | bytes 2088968 | tf_op jit(solution)/shard_map/ppermute | solution.py:40
  86.3 31.0 %collective-permute-start.35 = (bf16[272,1280]{1,0:T(8,128)(2,1)S(1)}, bf16[272,1280]{1,0:T(8,128)(2,1)S(1)}, u32[]{:S(2)}, u32[]{:S(2)}) collective-permute-start(bf16[272,1280]{1,0:T(8,128)(2,1)S(1)} %get-tuple-element.85), channel_id=1, source_target_pairs={{0,32},{1,129},{2,34},{3,131},{4,36},{5,133},{6,38},{7,135},{8,40}... | collective-permute-start | bytes 2088968 | tf_op jit(solution)/shard_map/ppermute | solution.py:40
  87.9 29.4 %collective-permute-start.36 = (bf16[272,1280]{1,0:T(8,128)(2,1)S(1)}, bf16[272,1280]{1,0:T(8,128)(2,1)S(1)}, u32[]{:S(2)}, u32[]{:S(2)}) collective-permute-start(bf16[272,1280]{1,0:T(8,128)(2,1)S(1)} %get-tuple-element.86), channel_id=1, source_target_pairs={{0,48},{1,193},{2,50},{3,195},{4,52},{5,197},{6,54},{7,199},{8,56}... | collective-permute-start | bytes 2088968 | tf_op jit(solution)/shard_map/ppermute | solution.py:40
  89.7 8.5 %collective-permute-start.27 = (bf16[48,1280]{1,0:T(8,128)(2,1)S(1)}, bf16[48,1280]{1,0:T(8,128)(2,1)S(1)}, u32[]{:S(2)}, u32[]{:S(2)}) collective-permute-start(bf16[48,1280]{1,0:T(8,128)(2,1)S(1)} %get-tuple-element.71), channel_id=1, source_target_pairs={{0,4},{1,5},{2,6},{3,7},{4,8},{5,9},{6,10},{7,11},{8,12},{9,13},{1... | collective-permute-start | bytes 368648 | tf_op jit(solution)/shard_map/ppermute | solution.py:31
  91.1 9.2 %collective-permute-start.28 = (bf16[48,1280]{1,0:T(8,128)(2,1)S(1)}, bf16[48,1280]{1,0:T(8,128)(2,1)S(1)}, u32[]{:S(2)}, u32[]{:S(2)}) collective-permute-start(bf16[48,1280]{1,0:T(8,128)(2,1)S(1)} %get-tuple-element.72), channel_id=1, source_target_pairs={{0,12},{1,13},{2,14},{3,15},{4,0},{5,1},{6,2},{7,3},{8,4},{9,5},{1... | collective-permute-start | bytes 368648 | tf_op jit(solution)/shard_map/ppermute | solution.py:31
  98.2 12.9 %collective-permute-start.25 = (bf16[144,1280]{1,0:T(8,128)(2,1)S(1)}, bf16[144,1280]{1,0:T(8,128)(2,1)S(1)}, u32[]{:S(2)}, u32[]{:S(2)}) collective-permute-start(bf16[144,1280]{1,0:T(8,128)(2,1)S(1)} %get-tuple-element.69), channel_id=1, source_target_pairs={{0,2},{1,3},{2,4},{3,5},{4,6},{5,7},{6,8},{7,9},{8,10},{9,11},{10,... | collective-permute-start | bytes 1105928 | tf_op jit(solution)/shard_map/ppermute | solution.py:31
  100.3 11.9 %collective-permute-start.26 = (bf16[144,1280]{1,0:T(8,128)(2,1)S(1)}, bf16[144,1280]{1,0:T(8,128)(2,1)S(1)}, u32[]{:S(2)}, u32[]{:S(2)}) collective-permute-start(bf16[144,1280]{1,0:T(8,128)(2,1)S(1)} %get-tuple-element.70), channel_id=1, source_target_pairs={{0,14},{1,15},{2,0},{3,1},{4,2},{5,3},{6,4},{7,5},{8,6},{9,7},{10,... | collective-permute-start | bytes 1105928 | tf_op jit(solution)/shard_map/ppermute | solution.py:31
  112.9 13.0 %collective-permute-start.30 = (bf16[80,1280]{1,0:T(8,128)(2,1)S(1)}, bf16[80,1280]{1,0:T(8,128)(2,1)S(1)}, u32[]{:S(2)}, u32[]{:S(2)}) collective-permute-start(bf16[80,1280]{1,0:T(8,128)(2,1)S(1)} %get-tuple-element.77), channel_id=1, source_target_pairs={{0,4},{1,5},{2,6},{3,7},{4,8},{5,9},{6,10},{7,11},{8,12},{9,13},{1... | collective-permute-start | bytes 614408 | tf_op jit(solution)/shard_map/ppermute | solution.py:31
  115.8 11.0 %collective-permute-start.31 = (bf16[80,1280]{1,0:T(8,128)(2,1)S(1)}, bf16[80,1280]{1,0:T(8,128)(2,1)S(1)}, u32[]{:S(2)}, u32[]{:S(2)}) collective-permute-start(bf16[80,1280]{1,0:T(8,128)(2,1)S(1)} %get-tuple-element.78), channel_id=1, source_target_pairs={{0,12},{1,13},{2,14},{3,15},{4,0},{5,1},{6,2},{7,3},{8,4},{9,5},{1... | collective-permute-start | bytes 614408 | tf_op jit(solution)/shard_map/ppermute | solution.py:31
  118.2 9.2 %collective-permute-start.37 = (bf16[80,1280]{1,0:T(8,128)(2,1)S(1)}, bf16[80,1280]{1,0:T(8,128)(2,1)S(1)}, u32[]{:S(2)}, u32[]{:S(2)}) collective-permute-start(bf16[80,1280]{1,0:T(8,128)(2,1)S(1)} %get-tuple-element.89), channel_id=1, source_target_pairs={{0,64},{1,17},{2,66},{3,19},{4,68},{5,21},{6,70},{7,23},{8,72},{9,... | collective-permute-start | bytes 614408 | tf_op jit(solution)/shard_map/ppermute | solution.py:40
  118.6 8.8 %collective-permute-start.38 = (bf16[80,1280]{1,0:T(8,128)(2,1)S(1)}, bf16[80,1280]{1,0:T(8,128)(2,1)S(1)}, u32[]{:S(2)}, u32[]{:S(2)}) collective-permute-start(bf16[80,1280]{1,0:T(8,128)(2,1)S(1)} %get-tuple-element.90), channel_id=1, source_target_pairs={{0,128},{1,33},{2,130},{3,35},{4,132},{5,37},{6,134},{7,39},{8,136... | collective-permute-start | bytes 614408 | tf_op jit(solution)/shard_map/ppermute | solution.py:40
  118.6 9.7 %collective-permute-start.39 = (bf16[80,1280]{1,0:T(8,128)(2,1)S(1)}, bf16[80,1280]{1,0:T(8,128)(2,1)S(1)}, u32[]{:S(2)}, u32[]{:S(2)}) collective-permute-start(bf16[80,1280]{1,0:T(8,128)(2,1)S(1)} %get-tuple-element.91), channel_id=1, source_target_pairs={{0,192},{1,49},{2,194},{3,51},{4,196},{5,53},{6,198},{7,55},{8,200... | collective-permute-start | bytes 614408 | tf_op jit(solution)/shard_map/ppermute | solution.py:40

commit v2 on v1

v2 whole, which is shorter than its diff:
```python
import functools
import math

import jax
import jax.numpy as jnp
from jax import lax
from jax.experimental import pallas as pl
from jax.experimental.pallas import tpu as pltpu
from jax.sharding import PartitionSpec as P

NX, NY, NZ, NC = 4, 4, 8, 2
AXES = ("img", "txt")
SHARD = 64
HALF = SHARD // 2
ROWS = NZ * SHARD
PLANE = NX * NY * SHARD
COLS = NC * PLANE
NOTE = 16
BF16, F32 = jnp.bfloat16, jnp.float32


def device_id(x, y, z, c):
    return (((x % NX) * NY + y % NY) * NZ + z % NZ) * NC + c % NC


COORDINATES = [(x, y, z, c) for x in range(NX) for y in range(NY) for z in range(NZ) for c in range(NC)]


def shift_z(value, by):
    pairs = [(device_id(x, y, z, c), device_id(x, y, z + by, c)) for x, y, z, c in COORDINATES]
    return lax.ppermute(value, AXES, pairs)


def shift_plane(value, by, first):
    pairs = []
    for x, y, z, c in COORDINATES:
        along_y = (c == 0) == first
        to = (x, y + by) if along_y else (x + by, y)
        pairs.append((device_id(x, y, z, c), device_id(*to, z, c)))
    return lax.ppermute(value, AXES, pairs)


def shift_far(value):
    pairs = [(device_id(x, y, z, c), device_id(x, y, z + 2 - 4 * c, c)) for x, y, z, c in COORDINATES]
    return lax.ppermute(value, AXES, pairs)


def swap(value, axis, bit):
    pairs = []
    for at in COORDINATES:
        to = list(at)
        to[axis] ^= bit
        pairs.append((device_id(*at), device_id(*to)))
    return lax.ppermute(value, AXES, pairs)


def swap_core(value):
    return swap(value, 3, 1)


def merge(*parts):
    top = functools.reduce(jnp.maximum, parts)
    return top + jnp.log(sum(jnp.exp(part - top) for part in parts))


def merge_columns(*parts):
    lanes = lax.broadcasted_iota(jnp.int32, parts[0].shape, 1)
    return jnp.where(lanes < COLS, merge(*parts), sum(parts))


def shift_one(value, axis, by):
    pairs = []
    for at in COORDINATES:
        to = list(at)
        to[axis] += by
        pairs.append((device_id(*at), device_id(*to)))
    return lax.ppermute(value, AXES, pairs)


def position():
    img, txt = lax.axis_index("img"), lax.axis_index("txt")
    y = lax.rem(img, 2) * 2 + txt // (NZ * NC)
    return img // 2, y, lax.rem(txt // NC, NZ), lax.rem(txt, NC)


def call(kernel, outs, args, scratch, flops, transcendentals, moved, vmem_mib):
    vmem = pl.BlockSpec(memory_space=pltpu.VMEM)
    return pl.pallas_call(
        lambda *refs: kernel(position(), *refs),
        out_shape=[jax.ShapeDtypeStruct(shape, dtype) for shape, dtype in outs],
        in_specs=[vmem] * len(args),
        out_specs=[vmem] * len(outs),
        scratch_shapes=scratch,
        cost_estimate=pl.CostEstimate(flops=flops, transcendentals=transcendentals, bytes_accessed=moved),
        compiler_params=pltpu.CompilerParams(vmem_limit_bytes=vmem_mib << 20),
    )(*args)


def diagonal_blocks(c):
    for zz in range(NZ):
        col = (zz // 4) * PLANE + (zz % 4) * NY * SHARD + c * 2 * SHARD
        yield zz * SHARD, pl.multiple_of(col, 128)


def on_diagonal(x):
    rows = lax.broadcasted_iota(jnp.int32, (SHARD, 128), 0)
    lanes = lax.broadcasted_iota(jnp.int32, (SHARD, 128), 1)
    return lanes == rows + (x // 2) * SHARD


def has_diagonal(x, y, z):
    return z == (x % 2) * 4 + y


def block_row(xx, yy):
    return pl.multiple_of((lax.rem(xx + NX, NX) * NY + lax.rem(yy + NY, NY)) * SHARD, SHARD)


def write_note(ref, value):
    high = value.astype(BF16).astype(F32)
    middle = (value - high).astype(BF16).astype(F32)
    low = value - high - middle
    which = lax.broadcasted_iota(jnp.int32, (NOTE, 128), 0)
    rows = jnp.where(which == 0, high, jnp.where(which == 1, middle, jnp.where(which == 2, low, 0.0)))
    ref[ref.shape[0] - NOTE :, :] = rows.astype(BF16)


def read_note(ref):
    terms = [ref[ref.shape[0] - NOTE + i : ref.shape[0] - NOTE + i + 1, :].astype(F32) for i in range(3)]
    return terms[0] + terms[1] + terms[2]


def part_of(ref, index, strip, strips):
    start = (index * strips + strip) * SHARD
    return slice(start, start + SHARD)


def columns(strip):
    return slice(strip * 128, (strip + 1) * 128)


STEPS = (0, 1, -1, 2)


def scores_kernel(scale, at, *refs):
    image_in, text_in = refs[:8], refs[8:16]
    scores, img, txt, row_out, col_out, row_top, row_part = refs[16:]
    x, y, z, c = at[0], at[1], at[2], at[3]
    for ref, step in zip(image_in, (0, -1, 1, -2, 2, -3, 3, -4)):
        where = lax.rem(z + step + NZ, NZ) * SHARD
        img[pl.ds(pl.multiple_of(where, SHARD), SHARD), :] = ref[...]
    for own in range(2):
        core = c if own == 0 else 1 - c
        for i, d in enumerate(STEPS):
            for j, e in enumerate(STEPS):
                dx, dy = jnp.where(core == 0, d, e), jnp.where(core == 0, e, d)
                where = pl.multiple_of(core * PLANE + block_row(x - dx, y - dy), SHARD)
                txt[pl.ds(where, SHARD), :] = text_in[own * 4 + i][j * SHARD : (j + 1) * SHARD, :]

    chunk = 512
    row_part[...] = jnp.full((ROWS, 128), -jnp.inf, F32)

    @pl.loop(0, COLS // chunk)
    def _(i):
        cols = pl.ds(pl.multiple_of(i * chunk, chunk), chunk)
        s = scale * lax.dot_general(
            img[...], txt[cols, :], (((1,), (1,)), ((), ())), preferred_element_type=F32
        )
        scores[:, cols] = s
        tops = row_part[...]
        for j in range(chunk // 128):
            tops = jnp.maximum(tops, s[:, j * 128 : (j + 1) * 128])
        row_part[...] = tops
        top = jnp.max(s, axis=0, keepdims=True)
        col_out[:, cols] = top + jnp.log(jnp.sum(jnp.exp(s - top), axis=0, keepdims=True))

    row_top[...] = jnp.broadcast_to(jnp.max(row_part[...], axis=1, keepdims=True), (ROWS, 128))
    row_part[...] = jnp.zeros((ROWS, 128), F32)

    @pl.loop(0, COLS // chunk)
    def _(i):
        for j in range(chunk // 128):
            cols = pl.ds(pl.multiple_of(i * chunk + j * 128, 128), 128)
            row_part[...] += jnp.exp(scores[:, cols] - row_top[...])

    row = row_top[...] + jnp.log(jnp.sum(row_part[...], axis=1, keepdims=True))
    row_out[...] = jnp.transpose(row)[0:1, :]
    col_out[:, COLS:] = jnp.zeros((1, 128), F32)

    @pl.when(has_diagonal(x, y, z))
    def _():
        mask = on_diagonal(x)
        total = jnp.zeros((1, 128), F32)
        for row, col in diagonal_blocks(c):
            block = scores[row : row + SHARD, pl.ds(col, 128)]
            total += jnp.sum(jnp.where(mask, block, 0.0), axis=0, keepdims=True)
        total = jnp.sum(total, axis=1, keepdims=True)
        col_out[:, COLS:] = jnp.broadcast_to(total, (1, 128))


def line_kernel(text, *refs):
    near, line, sem = refs[:3], refs[3], refs[4]
    copy = pltpu.make_async_copy(text, line.at[pl.ds(0, SHARD)], sem)
    copy.start()
    for i, ref in enumerate(near, 1):
        line[i * SHARD : (i + 1) * SHARD, :] = ref[...]
    copy.wait()


def weights_kernel(own, at, scores, row_lse, col_lse, out, *refs):
    x, y, z, c = at
    sums, row_col = refs[:-1], refs[-1]
    row_col[...] = jnp.transpose(jnp.broadcast_to(row_lse[...], (128, ROWS)))
    half = c if own else 1 - c

    def weigh(s, rows, cols):
        return 0.5 * (jnp.exp(s - rows) + jnp.exp(s - cols))

    chunk = 128

    @pl.loop(0, PLANE // chunk)
    def _(i):
        cols = pl.ds(pl.multiple_of(half * PLANE + i * chunk, chunk), chunk)
        out[:, pl.ds(pl.multiple_of(i * chunk, chunk), chunk)] = weigh(
            scores[:, cols], row_col[...], col_lse[:, cols]
        ).astype(BF16)

    @pl.when(has_diagonal(x, y, z))
    def _():
        mask = on_diagonal(x).astype(F32)
        for zz, (row, col) in enumerate(diagonal_blocks(c)):
            core = zz // 4

            @pl.when(half == core)
            def _(row=row, col=col, core=core):
                rows, cols = pl.ds(row, SHARD), pl.ds(col, 128)
                block = weigh(scores[rows, cols], row_col[rows, :], col_lse[:, cols]) - mask
                out[rows, pl.ds(pl.multiple_of(col - core * PLANE, 128), 128)] = block.astype(BF16)

    if own:
        p_out, q_out = sums
        row_sum = 0.5 * jnp.sum(row_lse[...], axis=1, keepdims=True)
        p_out[...] = jnp.broadcast_to(row_sum, (1, 128))
        col_sum = 0.5 * jnp.sum(col_lse[:, :COLS], axis=1, keepdims=True)
        q_out[...] = jnp.broadcast_to(col_sum, (1, 128)) - col_lse[:, COLS:]


def image_kernel(at, own, other, txt, q, up, down, far, here, up_two, down_two, total):
    _, _, z, c = at
    mine = pl.ds(pl.multiple_of(c * PLANE, PLANE), PLANE)
    theirs = pl.ds(pl.multiple_of((1 - c) * PLANE, PLANE), PLANE)
    chunk = 256

    @pl.loop(0, total.shape[1] // chunk)
    def _(i):
        cols = pl.ds(pl.multiple_of(i * chunk, chunk), chunk)
        total[:, cols] = jnp.dot(own[...], txt[mine, cols], preferred_element_type=F32) + jnp.dot(
            other[...], txt[theirs, cols], preferred_element_type=F32
        )

    strips = total.shape[1] // 128

    def block(dz, strip):
        return total[pl.ds(pl.multiple_of(lax.rem(z + dz + NZ, NZ) * SHARD, SHARD), SHARD), columns(strip)]

    for i in range(strips):
        for ref, index, dz in ((up, 0, 1), (up, 1, 3), (down, 0, -1), (down, 1, -3), (far, 0, 4)):
            ref[part_of(ref, index, i, strips), :] = block(dz, i).astype(BF16)
        for ref, dz in ((here, 0), (up_two, 2), (down_two, -2)):
            ref[:, columns(i)] = block(dz, i)
    for ref in (up, down, far):
        write_note(ref, q[...])


def text_kernel(at, own, received, img, img_other, p_own, p_other, *refs):
    sent, kept, p_out, total = refs[:3], refs[3], refs[4], refs[5]
    x, y, _, c = at
    p = p_own[...] + p_other[...]
    p_out[...] = p
    chunk = 256

    @pl.loop(0, PLANE // chunk)
    def _(i):
        cols = pl.ds(pl.multiple_of(i * chunk, chunk), chunk)
        total[cols, :] = lax.dot_general(
            own[:, cols], img[...], (((0,), (0,)), ((), ())), preferred_element_type=F32
        ) + lax.dot_general(
            received[:, cols], img_other[...], (((0,), (0,)), ((), ())), preferred_element_type=F32
        )

    strips = total.shape[1] // 128
    for d in range(4):
        for e in range(4):
            dx, dy = jnp.where(c == 0, e, d), jnp.where(c == 0, d, e)
            rows = pl.ds(block_row(x + dx, y + dy), SHARD)
            for i in range(strips):
                part = total[rows, columns(i)]
                if d == 0:
                    kept[e * SHARD : (e + 1) * SHARD, columns(i)] = part
                else:
                    sent[d - 1][part_of(sent[d - 1], e, i, strips), :] = part.astype(BF16)
        if d:
            write_note(sent[d - 1], p)


def image_middle_kernel(at, up, down, far, here, up_two, down_two, q, up_out, down_out, here_out, q_out):
    first_core = at[3] == 0
    strips = here.shape[1] // 128
    for i in range(strips):
        near, rest, cols = part_of(up, 0, i, strips), part_of(up, 1, i, strips), columns(i)
        here_out[:, cols] = here[:, cols] + up[near, :].astype(F32) + down[near, :].astype(F32)
        far_rows = far[near, :].astype(F32)
        above = up_two[:, cols] + up[rest, :].astype(F32) + jnp.where(first_core, far_rows, 0.0)
        below = down_two[:, cols] + down[rest, :].astype(F32) + jnp.where(first_core, 0.0, far_rows)
        up_out[near, :] = above.astype(BF16)
        down_out[near, :] = below.astype(BF16)
    note_up, note_down, note_far = read_note(up), read_note(down), read_note(far)
    write_note(up_out, q[...] + note_up + jnp.where(first_core, note_far, 0.0))
    write_note(down_out, q[...] + note_down + jnp.where(first_core, 0.0, note_far))
    q_out[...] = q[...] + note_up + note_down


def text_middle_kernel(at, first, second, third, kept, p, *refs):
    sent, kept_out, p_out = refs[:3], refs[3], refs[4]
    total = p[...] + read_note(first) + read_note(second) + read_note(third)
    p_out[...] = total
    strips = kept.shape[1] // 128
    for e in range(4):
        for i in range(strips):
            rows, cols = part_of(first, e, i, strips), columns(i)
            part = kept[e * SHARD : (e + 1) * SHARD, cols] + first[rows, :].astype(F32)
            part += second[rows, :].astype(F32) + third[rows, :].astype(F32)
            if e == 0:
                kept_out[:, cols] = part
            else:
                sent[e - 1][part_of(first, 0, i, strips), :] = part.astype(BF16)
        if e:
            write_note(sent[e - 1], total)


def last_kernel(at, up, down, here, q, first, second, third, kept, p, image_out, text_out, loss_out):
    strips = kept.shape[1] // 128
    for i in range(strips):
        rows, cols = part_of(up, 0, i, strips), columns(i)
        image = here[:, cols] + up[rows, :].astype(F32) + down[rows, :].astype(F32)
        image_out[:, cols] = image.astype(BF16)
        text = kept[:, cols] + first[rows, :].astype(F32) + second[rows, :].astype(F32) + third[rows, :].astype(F32)
        text_out[:, cols] = text.astype(BF16)
    loss = q[...] + p[...]
    for message in (up, down, first, second, third):
        loss += read_note(message)
    loss_out[...] = loss / (ROWS * NC * NX * NY)


def shards(image, text):
    embed = image.shape[1]
    scale = 4.0 / math.sqrt(embed)
    up, down = shift_z(image, 1), shift_z(image, -1)
    near = [shift_plane(text, d, True) for d in STEPS[1:]]
    line = pl.pallas_call(
        line_kernel,
        out_shape=jax.ShapeDtypeStruct((4 * SHARD, embed), BF16),
        in_specs=[pl.BlockSpec(memory_space=pltpu.HBM)] + [pl.BlockSpec(memory_space=pltpu.VMEM)] * 3,
        out_specs=pl.BlockSpec(memory_space=pltpu.VMEM),
        scratch_shapes=[pltpu.SemaphoreType.DMA],
        cost_estimate=pl.CostEstimate(flops=0, transcendentals=0, bytes_accessed=1 << 20),
        compiler_params=pltpu.CompilerParams(vmem_limit_bytes=4 << 20),
    )(text, *near)
    image_in = [image, up, down]
    up, down, line = lax.optimization_barrier((shift_z(up, 1), shift_z(down, -1), line))
    image_in += [up, down]
    far = [shift_plane(line, d, False) for d in STEPS[1:]]
    up, down = lax.optimization_barrier((shift_z(up, 1), shift_z(down, -1)))
    image_in += [up, down]
    last, line, *far = lax.optimization_barrier((shift_z(up, 1), line, *far))
    image_in.append(last)
    text_in = [line, *far]
    text_in += [swap_core(part) for part in text_in]

    tile = 2 * ROWS * COLS * embed
    scores, img, txt, row_lse, col_lse = call(
        functools.partial(scores_kernel, scale),
        [
            ((ROWS, COLS), F32),
            ((ROWS, embed), BF16),
            ((COLS, embed), BF16),
            ((1, ROWS), F32),
            ((1, COLS + 128), F32),
        ],
        image_in + text_in,
        [pltpu.VMEM((ROWS, 128), F32), pltpu.VMEM((ROWS, 128), F32)],
        tile,
        2 * ROWS * COLS,
        14 << 20,
        16,
    )
    img_other = swap_core(img)
    col_lse = merge_columns(col_lse, swap_core(col_lse))
    for axis in (1, 0):
        col_lse = merge_columns(col_lse, *[shift_one(col_lse, axis, by) for by in STEPS[1:]])
    for bit in (1, 2, 4):
        row_lse = merge(row_lse, swap(row_lse, 2, bit))

    half = ((ROWS, PLANE), BF16)
    scalar = ((1, 128), F32)
    weights = lambda own, outs, scores: call(
        functools.partial(weights_kernel, own),
        [half, *outs],
        (scores, row_lse, col_lse),
        [pltpu.VMEM((ROWS, 128), F32)],
        4 * ROWS * COLS,
        ROWS * COLS,
        3 << 20,
        12,
    )
    (other,) = weights(False, [], scores)
    scores, other = lax.optimization_barrier((scores, other))
    received = swap_core(other)
    own, p, q = weights(True, [scalar, scalar], scores)
    p_other = swap_core(p)
    message = lambda rows: ((rows * embed // 128 + NOTE, 128), BF16)
    *sent, kept, p = call(
        text_kernel,
        [message(4 * SHARD)] * 3 + [((4 * SHARD, embed), F32), scalar],
        (own, received, img, img_other, p, p_other),
        [pltpu.VMEM((PLANE, embed), F32)],
        tile // 2,
        0,
        12 << 20,
        24,
    )
    other, kept = lax.optimization_barrier((other, kept))
    up, down, far, here, up_two, down_two = call(
        image_kernel,
        [message(2 * SHARD)] * 2 + [message(SHARD)] + [((SHARD, embed), F32)] * 3,
        (own, other, txt, q),
        [pltpu.VMEM((ROWS, embed), F32)],
        tile,
        0,
        10 << 20,
        16,
    )
    up, down = shift_z(up, 1), shift_z(down, -1)
    sent = [shift_plane(part, d, True) for d, part in enumerate(sent, 1)]
    far, sent[0] = lax.optimization_barrier((far, sent[0]))
    far = shift_far(far)
    up, down, here, q = call(
        image_middle_kernel,
        [message(SHARD)] * 2 + [((SHARD, embed), F32), scalar],
        (up, down, far, here, up_two, down_two, q),
        [],
        1 << 20,
        0,
        2 << 20,
        12,
    )
    up, down = shift_z(up, 2), shift_z(down, -2)
    *sent, kept, p = call(
        text_middle_kernel,
        [message(SHARD)] * 3 + [((SHARD, embed), F32), scalar],
        (*sent, kept, p),
        [],
        1 << 20,
        0,
        4 << 20,
        12,
    )
    sent = [shift_plane(part, d, False) for d, part in enumerate(sent, 1)]
    image_grad, text_grad, loss = call(
        last_kernel,
        [((SHARD, embed), BF16)] * 2 + [scalar],
        (up, down, here, q, *sent, kept, p),
        [],
        1 << 20,
        0,
        2 << 20,
        12,
    )
    return image_grad, text_grad, loss[0, 0]


def solution(mesh):
    return jax.shard_map(
        shards,
        mesh=mesh,
        in_specs=(P(("img", "txt"), None), P(("txt", "img"), None)),
        out_specs=(P(("img", "txt"), None), P(("txt", "img"), None), P()),
        check_vma=False,
    )
```

time: 131 us -> 120 us (0.916); the launches traced: 130 us -> 120 us
  waiting for transfers between devices: 50.2 us -> 45.7 us
  Pallas kernels: 21 us -> 17.2 us
    ppermute x13 -> x11, waiting for transfers between devices: 36 us -> 15 us  [shift_z(): return lax.ppermute(value, AXES, pairs)]
    ppermute x0 -> x7, waiting for transfers between devices: none -> 11.7 us  [the longest x6 7.32 us: shift_one(): return lax.ppermute(value, AXES, pairs)]
    ppermute x0 -> x7, starting transfers between devices: none -> 9.68 us  [the longest x6 9.66 us: shift_one(): return lax.ppermute(value, AXES, pairs)]
    ppermute x13 -> x11, starting transfers between devices: 23.9 us -> 17.9 us  [shift_z(): return lax.ppermute(value, AXES, pairs)]
    ppermute x12, waiting for transfers between devices: 6.98 us -> 12.8 us  [shift_plane(): return lax.ppermute(value, AXES, pairs)]
    pallas_call x8 -> x9, Pallas kernels: 21 us -> 17.2 us  [the longest x8 16.9 us: call(): pl.pallas_call(lambda *refs: kernel(position(), *refs), out_shape=[jax.Sh...]
    ppermute x15 -> x11, starting transfers between devices: 14 us -> 10.8 us  [swap(): return lax.ppermute(value, AXES, pairs)]
    ppermute x12, starting transfers between devices: 18.5 us -> 17.1 us  [shift_plane(): return lax.ppermute(value, AXES, pairs)]
  transfers between devices with their start and end apart: 40 -> 41, of which waited for: 20 -> 19; matrix products, arithmetic and copies ran while one was open for 0% -> 0% of each run, Pallas kernels for 6% -> 5%
where the time goes in v2:
time: 120 us
  starting transfers between devices  55.5 us (46%)
  waiting for transfers between devices  45.7 us (38%)
  Pallas kernels  17.2 us (14%)
    ppermute x11, starting transfers between devices, shift_z(): return lax.ppermute(value, AXES, pairs)  17.9 us
    ppermute x12, starting transfers between devices, shift_plane(): return lax.ppermute(value, AXES, pairs)  17.1 us
    pallas_call x8, Pallas kernels, call(): pl.pallas_call(lambda *refs: kernel(position(), *refs), out_shape=[jax.Sh...  16.9 us
    ppermute x11, waiting for transfers between devices, shift_z(): return lax.ppermute(value, AXES, pairs)  15 us
    ppermute x12, waiting for transfers between devices, shift_plane(): return lax.ppermute(value, AXES, pairs)  12.8 us
    ppermute x11, starting transfers between devices, swap(): return lax.ppermute(value, AXES, pairs)  10.8 us
    ppermute x6, starting transfers between devices, shift_one(): return lax.ppermute(value, AXES, pairs)  9.66 us
    ppermute x6, waiting for transfers between devices, shift_one(): return lax.ppermute(value, AXES, pairs)  7.32 us
  transfers between devices with their start and end apart: 41, of which 19 were waited for; matrix products, arithmetic and copies ran while one was open for 0% of the time, Pallas kernels for 5%

profile of v2, /device:TPU:32, one launch (start us, length us, event | category | flops | bytes accessed | tf_op | source)
XLA Modules:
  0.0 120.3 jit_solution(6886337103630651744)
XLA Ops:
  0.6 2.0 %collective-permute-start = (bf16[64,1280]{1,0:T(8,128)(2,1)}, bf16[64,1280]{1,0:T(8,128)(2,1)S(1)}, u32[]{:S(2)}, u32[]{:S(2)}) collective-permute-start(bf16[64,1280]{1,0:T(8,128)(2,1)} %refs_0_.1), channel_id=1, source_target_pairs={{0,2},{1,3},{2,4},{3,5},{4,6},{5,7},{6,8},{7,9},{8,10},{9,11},{10,... | collective-permute-start | bytes 491528 | tf_op jit(solution)/shard_map/ppermute | solution.py:31
  2.7 3.0 %collective-permute-start.5 = (bf16[64,1280]{1,0:T(8,128)(2,1)}, bf16[64,1280]{1,0:T(8,128)(2,1)S(1)}, u32[]{:S(2)}, u32[]{:S(2)}) collective-permute-start(bf16[64,1280]{1,0:T(8,128)(2,1)} %text.1), channel_id=1, source_target_pairs={{0,48},{1,193},{2,50},{3,195},{4,52},{5,197},{6,54},{7,199},{8,56}... | collective-permute-start | bytes 491528 | tf_op jit(solution)/shard_map/ppermute | solution.py:40
  5.8 2.2 %collective-permute-start.6 = (bf16[64,1280]{1,0:T(8,128)(2,1)}, bf16[64,1280]{1,0:T(8,128)(2,1)S(1)}, u32[]{:S(2)}, u32[]{:S(2)}) collective-permute-start(bf16[64,1280]{1,0:T(8,128)(2,1)} %text.1), channel_id=1, source_target_pairs={{0,32},{1,129},{2,34},{3,131},{4,36},{5,133},{6,38},{7,135},{8,40}... | collective-permute-start | bytes 491528 | tf_op jit(solution)/shard_map/ppermute | solution.py:40
  8.0 1.9 %collective-permute-start.2 = (bf16[64,1280]{1,0:T(8,128)(2,1)S(1)}, bf16[64,1280]{1,0:T(8,128)(2,1)S(1)}, u32[]{:S(2)}, u32[]{:S(2)}) collective-permute-start(bf16[64,1280]{1,0:T(8,128)(2,1)S(1)} %collective-permute-done.refs_1_), channel_id=1, source_target_pairs={{0,2},{1,3},{2,4},{3,5},{4,6},{5,7},{6,8},{7,9},{8,10},{9,11},{10,... | collective-permute-start | bytes 491528 | tf_op jit(solution)/shard_map/ppermute | solution.py:31
  9.9 2.2 %collective-permute-start.3 = (bf16[64,1280]{1,0:T(8,128)(2,1)S(1)}, bf16[64,1280]{1,0:T(8,128)(2,1)S(1)}, u32[]{:S(2)}, u32[]{:S(2)}) collective-permute-start(bf16[64,1280]{1,0:T(8,128)(2,1)S(1)} %collective-permute-done.1.refs_2_), channel_id=1, source_target_pairs={{0,14},{1,15},{2,0},{3,1},{4,2},{5,3},{6,4},{7,5},{8,6},{9,7},{10,... | collective-permute-start | bytes 491528 | tf_op jit(solution)/shard_map/ppermute | solution.py:31
  12.1 2.2 %collective-permute-done.4.refs_0_ = bf16[64,1280]{1,0:T(8,128)(2,1)S(1)} collective-permute-done((bf16[64,1280]{1,0:T(8,128)(2,1)}, bf16[64,1280]{1,0:T(8,128)(2,1)S(1)}, u32[]{:S(2)}, u32[]{:S(2)}) %collective-permute-start.4) | collective-permute-done | bytes 163872 | tf_op jit(solution)/shard_map/ppermute | solution.py:40
  14.2 0.9 copy-done
  16.2 3.0 %collective-permute-start.12 = (bf16[256,1280]{1,0:T(8,128)(2,1)S(1)}, bf16[256,1280]{1,0:T(8,128)(2,1)S(1)}, u32[]{:S(2)}, u32[]{:S(2)}) collective-permute-start(bf16[256,1280]{1,0:T(8,128)(2,1)S(1)} %shard_map.49.refs_8_), channel_id=1, source_target_pairs={{0,128},{1,33},{2,130},{3,35},{4,132},{5,37},{6,134},{7,39},{8,136... | collective-permute-start | bytes 1966088 | tf_op jit(solution)/shard_map/ppermute | solution.py:40
  19.2 1.1 collective-permute-start.11
  20.4 0.9 collective-permute-start.10
  21.3 3.2 %collective-permute-start.7 = (bf16[64,1280]{1,0:T(8,128)(2,1)S(1)}, bf16[64,1280]{1,0:T(8,128)(2,1)S(1)}, u32[]{:S(2)}, u32[]{:S(2)}) collective-permute-start(bf16[64,1280]{1,0:T(8,128)(2,1)S(1)} %collective-permute-done.2.refs_3_), channel_id=1, source_target_pairs={{0,2},{1,3},{2,4},{3,5},{4,6},{5,7},{6,8},{7,9},{8,10},{9,11},{10,... | collective-permute-start | bytes 491528 | tf_op jit(solution)/shard_map/ppermute | solution.py:31
  24.6 3.3 %collective-permute-done.7.refs_5_ = bf16[64,1280]{1,0:T(8,128)(2,1)S(1)} collective-permute-done((bf16[64,1280]{1,0:T(8,128)(2,1)S(1)}, bf16[64,1280]{1,0:T(8,128)(2,1)S(1)}, u32[]{:S(2)}, u32[]{:S(2)}) %collective-permute-start.7) | collective-permute-done | bytes 163872 | tf_op jit(solution)/shard_map/ppermute | solution.py:31
  27.9 3.1 %collective-permute-done.8.refs_6_ = bf16[64,1280]{1,0:T(8,128)(2,1)S(1)} collective-permute-done((bf16[64,1280]{1,0:T(8,128)(2,1)S(1)}, bf16[64,1280]{1,0:T(8,128)(2,1)S(1)}, u32[]{:S(2)}, u32[]{:S(2)}) %collective-permute-start.8) | collective-permute-done | bytes 163872 | tf_op jit(solution)/shard_map/ppermute | solution.py:31
  31.0 2.0 %collective-permute-start.9 = (bf16[64,1280]{1,0:T(8,128)(2,1)S(1)}, bf16[64,1280]{1,0:T(8,128)(2,1)S(1)}, u32[]{:S(2)}, u32[]{:S(2)}) collective-permute-start(bf16[64,1280]{1,0:T(8,128)(2,1)S(1)} %collective-permute-done.7.refs_5_), channel_id=1, source_target_pairs={{0,2},{1,3},{2,4},{3,5},{4,6},{5,7},{6,8},{7,9},{8,10},{9,11},{10,... | collective-permute-start | bytes 491528 | tf_op jit(solution)/shard_map/ppermute | solution.py:31
  33.0 3.3 %collective-permute-done.9.refs_7_ = bf16[64,1280]{1,0:T(8,128)(2,1)S(1)} collective-permute-done((bf16[64,1280]{1,0:T(8,128)(2,1)S(1)}, bf16[64,1280]{1,0:T(8,128)(2,1)S(1)}, u32[]{:S(2)}, u32[]{:S(2)}) %collective-permute-start.9) | collective-permute-done | bytes 163872 | tf_op jit(solution)/shard_map/ppermute | solution.py:31
  37.5 1.1 collective-permute-done.13.refs_12_
  38.5 0.9 collective-permute-done.14.refs_13_
  39.5 0.9 collective-permute-done.15.refs_14_
  40.4 0.9 collective-permute-done.16.refs_15_
  41.3 6.2 %shard_map.50 = (f32[512,2048]{1,0:T(8,128)S(1)}, bf16[512,1280]{1,0:T(8,128)(2,1)S(1)}, bf16[2048,1280]{1,0:T(8,128)(2,1)S(1)}, f32[1,512]{1,0:T(1,128)S(1)}, f32[1,2176]{1,0:T(1,128)S(1)}) custom-call(bf16[64,1280]{1,0:T(8,128)(2,1)S(1)} %copy-done.1, bf16[64,1280]{1,0:T(8,128)(2,1)S(1)} %collective-permute-done.refs_1_, ...), custom_call_target="tpu_custom_call" | custom-call | flops 2684354560 | bytes 14680064 | tf_op jit(solution)/shard_map/pallas_call | solution.py:88
  47.6 2.5 %collective-permute-start.17 = (f32[1,512]{1,0:T(1,128)S(1)}, f32[1,512]{1,0:T(1,128)S(1)}, u32[]{:S(2)}, u32[]{:S(2)}) collective-permute-start(f32[1,512]{1,0:T(1,128)S(1)} %get-tuple-element.61), channel_id=1, source_target_pairs={{0,2},{1,3},{2,0},{3,1},{4,6},{5,7},{6,4},{7,5},{8,10},{9,11},{10,... | collective-permute-start | bytes 6152 | tf_op jit(solution)/shard_map/ppermute | solution.py:54
  50.6 1.1 collective-permute-done.17
  51.7 4.6 %collective-permute-start.18 = (f32[1,512]{1,0:T(1,128)S(1)}, f32[1,512]{1,0:T(1,128)S(1)}, u32[]{:S(2)}, u32[]{:S(2)}) collective-permute-start(f32[1,512]{1,0:T(1,128)S(1)} %log_add_fusion.2), channel_id=1, source_target_pairs={{0,4},{1,5},{2,6},{3,7},{4,0},{5,1},{6,2},{7,3},{8,12},{9,13},{10,... | collective-permute-start | bytes 6152 | tf_op jit(solution)/shard_map/ppermute | solution.py:54
  56.3 2.2 %collective-permute-start.23 = (f32[1,2176]{1,0:T(1,128)S(1)}, f32[1,2176]{1,0:T(1,128)S(1)}, u32[]{:S(2)}, u32[]{:S(2)}) collective-permute-start(f32[1,2176]{1,0:T(1,128)S(1)} %add_select_fusion.2), channel_id=1, source_target_pairs={{0,32},{1,33},{2,34},{3,35},{4,36},{5,37},{6,38},{7,39},{8,40},{9,... | collective-permute-start | bytes 26120 | tf_op jit(solution)/shard_map/ppermute | solution.py:77
  58.5 2.5 %collective-permute-start.22 = (f32[1,2176]{1,0:T(1,128)S(1)}, f32[1,2176]{1,0:T(1,128)S(1)}, u32[]{:S(2)}, u32[]{:S(2)}) collective-permute-start(f32[1,2176]{1,0:T(1,128)S(1)} %add_select_fusion.2), channel_id=1, source_target_pairs={{0,48},{1,49},{2,50},{3,51},{4,52},{5,53},{6,54},{7,55},{8,56},{9,... | collective-permute-start | bytes 26120 | tf_op jit(solution)/shard_map/ppermute | solution.py:77
  61.0 1.5 %collective-permute-start.19 = (f32[1,512]{1,0:T(1,128)S(1)}, f32[1,512]{1,0:T(1,128)S(1)}, u32[]{:S(2)}, u32[]{:S(2)}) collective-permute-start(f32[1,512]{1,0:T(1,128)S(1)} %log_add_fusion.1), channel_id=1, source_target_pairs={{0,8},{1,9},{2,10},{3,11},{4,12},{5,13},{6,14},{7,15},{8,0},{9,1},... | collective-permute-start | bytes 6152 | tf_op jit(solution)/shard_map/ppermute | solution.py:54
  62.5 3.3 %collective-permute-done.21 = f32[1,2176]{1,0:T(1,128)S(1)} collective-permute-done((f32[1,2176]{1,0:T(1,128)S(1)}, f32[1,2176]{1,0:T(1,128)S(1)}, u32[]{:S(2)}, u32[]{:S(2)}) %collective-permute-start.21) | collective-permute-done | bytes 8736 | tf_op jit(solution)/shard_map/ppermute | solution.py:77
  65.9 3.0 %collective-permute-start.26 = (f32[1,2176]{1,0:T(1,128)S(1)}, f32[1,2176]{1,0:T(1,128)S(1)}, u32[]{:S(2)}, u32[]{:S(2)}) collective-permute-start(f32[1,2176]{1,0:T(1,128)S(1)} %add_select_fusion.1), channel_id=1, source_target_pairs={{0,128},{1,129},{2,130},{3,131},{4,132},{5,133},{6,134},{7,135},{8... | collective-permute-start | bytes 26120 | tf_op jit(solution)/shard_map/ppermute | solution.py:77
  68.9 1.2 %collective-permute-start.25 = (f32[1,2176]{1,0:T(1,128)S(1)}, f32[1,2176]{1,0:T(1,128)S(1)}, u32[]{:S(2)}, u32[]{:S(2)}) collective-permute-start(f32[1,2176]{1,0:T(1,128)S(1)} %add_select_fusion.1), channel_id=1, source_target_pairs={{0,192},{1,193},{2,194},{3,195},{4,196},{5,197},{6,198},{7,199},{8... | collective-permute-start | bytes 26120 | tf_op jit(solution)/shard_map/ppermute | solution.py:77
  70.1 0.8 collective-permute-start.24
  71.1 1.4 %collective-permute-done.25 = f32[1,2176]{1,0:T(1,128)S(1)} collective-permute-done((f32[1,2176]{1,0:T(1,128)S(1)}, f32[1,2176]{1,0:T(1,128)S(1)}, u32[]{:S(2)}, u32[]{:S(2)}) %collective-permute-start.25) | collective-permute-done | bytes 8736 | tf_op jit(solution)/shard_map/ppermute | solution.py:77
  72.5 2.4 %collective-permute-done.24 = f32[1,2176]{1,0:T(1,128)S(1)} collective-permute-done((f32[1,2176]{1,0:T(1,128)S(1)}, f32[1,2176]{1,0:T(1,128)S(1)}, u32[]{:S(2)}, u32[]{:S(2)}) %collective-permute-start.24) | collective-permute-done | bytes 8736 | tf_op jit(solution)/shard_map/ppermute | solution.py:77
  75.0 0.9 shard_map.51.refs_1_
  76.0 1.0 shard_map.52
  77.4 1.2 collective-permute-done.29.refs_5_
  78.6 3.8 %shard_map.53 = (bf16[2576,128]{1,0:T(8,128)(2,1)S(1)}, bf16[2576,128]{1,0:T(8,128)(2,1)S(1)}, bf16[2576,128]{1,0:T(8,128)(2,1)S(1)}, f32[256,1280]{1,0:T(8,128)S(1)}, f32[1,128]{1,0:T(1,128)S(1)}) custom-call(bf16[512,1024]{1,0:T(8,128)(2,1)S(1)} %get-tuple-element.64.refs_0_, bf16[512,1024]{1,0:T(8,128)(2,1)S(1)} %collective-permute-done.27.refs_1_, ...), custom_call_target="tpu_custom_call" | custom-call | flops 1342177280 | bytes 12582912 | tf_op jit(solution)/shard_map/pallas_call | solution.py:88
  82.8 1.5 %collective-permute-start.36 = (bf16[2576,128]{1,0:T(8,128)(2,1)S(1)}, bf16[2576,128]{1,0:T(8,128)(2,1)S(1)}, u32[]{:S(2)}, u32[]{:S(2)}) collective-permute-start(bf16[2576,128]{1,0:T(8,128)(2,1)S(1)} %get-tuple-element.85), channel_id=1, source_target_pairs={{0,32},{1,129},{2,34},{3,131},{4,36},{5,133},{6,38},{7,135},{8,40}... | collective-permute-start | bytes 1978376 | tf_op jit(solution)/shard_map/ppermute | solution.py:40
  84.2 1.8 %collective-permute-start.37 = (bf16[2576,128]{1,0:T(8,128)(2,1)S(1)}, bf16[2576,128]{1,0:T(8,128)(2,1)S(1)}, u32[]{:S(2)}, u32[]{:S(2)}) collective-permute-start(bf16[2576,128]{1,0:T(8,128)(2,1)S(1)} %get-tuple-element.86), channel_id=1, source_target_pairs={{0,48},{1,193},{2,50},{3,195},{4,52},{5,197},{6,54},{7,199},{8,56}... | collective-permute-start | bytes 1978376 | tf_op jit(solution)/shard_map/ppermute | solution.py:40
  86.0 3.8 %shard_map.54 = (bf16[1296,128]{1,0:T(8,128)(2,1)S(1)}, bf16[1296,128]{1,0:T(8,128)(2,1)S(1)}, bf16[656,128]{1,0:T(8,128)(2,1)S(1)}, f32[64,1280]{1,0:T(8,128)S(...) custom-call(bf16[512,1024]{1,0:T(8,128)(2,1)S(1)} %get-tuple-element.64.refs_0_, ...), custom_call_target="tpu_custom_call" | custom-call | flops 2684354560 | bytes 10485760 | tf_op jit(solution)/shard_map/pallas_call | solution.py:88
  89.9 2.0 %collective-permute-start.31 = (bf16[1296,128]{1,0:T(8,128)(2,1)S(1)}, bf16[1296,128]{1,0:T(8,128)(2,1)S(1)}, u32[]{:S(2)}, u32[]{:S(2)}) collective-permute-start(bf16[1296,128]{1,0:T(8,128)(2,1)S(1)} %get-tuple-element.73), channel_id=1, source_target_pairs={{0,14},{1,15},{2,0},{3,1},{4,2},{5,3},{6,4},{7,5},{8,6},{9,7},{10,... | collective-permute-start | bytes 995336 | tf_op jit(solution)/shard_map/ppermute | solution.py:31
  91.9 9.8 %collective-permute-done.32.refs_0_ = bf16[2576,128]{1,0:T(8,128)(2,1)S(1)} collective-permute-done((bf16[2576,128]{1,0:T(8,128)(2,1)S(1)}, bf16[2576,128]{1,0:T(8,128)(2,1)S(1)}, u32[]{:S(2)}, u32[]{:S(2)}) %collective-permute-start.32) | collective-permute-done | bytes 659488 | tf_op jit(solution)/shard_map/ppermute | solution.py:40
  101.7 0.9 collective-permute-done.37.refs_2_
  102.9 1.5 %collective-permute-start.39 = (bf16[656,128]{1,0:T(8,128)(2,1)S(1)}, bf16[656,128]{1,0:T(8,128)(2,1)S(1)}, u32[]{:S(2)}, u32[]{:S(2)}) collective-permute-start(bf16[656,128]{1,0:T(8,128)(2,1)S(1)} %get-tuple-element.90), channel_id=1, source_target_pairs={{0,128},{1,33},{2,130},{3,35},{4,132},{5,37},{6,134},{7,39},{8,136... | collective-permute-start | bytes 503816 | tf_op jit(solution)/shard_map/ppermute | solution.py:40
  104.4 1.8 %collective-permute-start.40 = (bf16[656,128]{1,0:T(8,128)(2,1)S(1)}, bf16[656,128]{1,0:T(8,128)(2,1)S(1)}, u32[]{:S(2)}, u32[]{:S(2)}) collective-permute-start(bf16[656,128]{1,0:T(8,128)(2,1)S(1)} %get-tuple-element.91), channel_id=1, source_target_pairs={{0,192},{1,49},{2,194},{3,51},{4,196},{5,53},{6,198},{7,55},{8,200... | collective-permute-start | bytes 503816 | tf_op jit(solution)/shard_map/ppermute | solution.py:40
  106.2 4.4 %collective-permute-done.33.refs_2_ = bf16[656,128]{1,0:T(8,128)(2,1)S(1)} collective-permute-done((bf16[656,128]{1,0:T(8,128)(2,1)S(1)}, bf16[656,128]{1,0:T(8,128)(2,1)S(1)}, u32[]{:S(2)}, u32[]{:S(2)}) %collective-permute-start.33) | collective-permute-done | bytes 167968 | tf_op jit(solution)/shard_map/ppermute | solution.py:45
  110.8 4.1 %collective-permute-start.35 = (bf16[656,128]{1,0:T(8,128)(2,1)S(1)}, bf16[656,128]{1,0:T(8,128)(2,1)S(1)}, u32[]{:S(2)}, u32[]{:S(2)}) collective-permute-start(bf16[656,128]{1,0:T(8,128)(2,1)S(1)} %get-tuple-element.81), channel_id=1, source_target_pairs={{0,12},{1,13},{2,14},{3,15},{4,0},{5,1},{6,2},{7,3},{8,4},{9,5},{1... | collective-permute-start | bytes 503816 | tf_op jit(solution)/shard_map/ppermute | solution.py:31
  115.0 4.5 %collective-permute-done.34.refs_0_ = bf16[656,128]{1,0:T(8,128)(2,1)S(1)} collective-permute-done((bf16[656,128]{1,0:T(8,128)(2,1)S(1)}, bf16[656,128]{1,0:T(8,128)(2,1)S(1)}, u32[]{:S(2)}, u32[]{:S(2)}) %collective-permute-start.34) | collective-permute-done | bytes 167968 | tf_op jit(solution)/shard_map/ppermute | solution.py:31
  119.4 0.8 shard_map.57
  (53 shorter events, 5.0 us)
Async XLA Ops:
  0.6 7.3 %collective-permute-start = (bf16[64,1280]{1,0:T(8,128)(2,1)}, bf16[64,1280]{1,0:T(8,128)(2,1)S(1)}, u32[]{:S(2)}, u32[]{:S(2)}) collective-permute-start(bf16[64,1280]{1,0:T(8,128)(2,1)} %refs_0_.1), channel_id=1, source_target_pairs={{0,2},{1,3},{2,4},{3,5},{4,6},{5,7},{6,8},{7,9},{8,10},{9,11},{10,... | collective-permute-start | bytes 491528 | tf_op jit(solution)/shard_map/ppermute | solution.py:31
  2.6 7.3 %collective-permute-start.1 = (bf16[64,1280]{1,0:T(8,128)(2,1)}, bf16[64,1280]{1,0:T(8,128)(2,1)S(1)}, u32[]{:S(2)}, u32[]{:S(2)}) collective-permute-start(bf16[64,1280]{1,0:T(8,128)(2,1)} %refs_0_.1), channel_id=1, source_target_pairs={{0,14},{1,15},{2,0},{3,1},{4,2},{5,3},{6,4},{7,5},{8,6},{9,7},{10,... | collective-permute-start | bytes 491528 | tf_op jit(solution)/shard_map/ppermute | solution.py:31
  2.7 9.3 %collective-permute-start.5 = (bf16[64,1280]{1,0:T(8,128)(2,1)}, bf16[64,1280]{1,0:T(8,128)(2,1)S(1)}, u32[]{:S(2)}, u32[]{:S(2)}) collective-permute-start(bf16[64,1280]{1,0:T(8,128)(2,1)} %text.1), channel_id=1, source_target_pairs={{0,48},{1,193},{2,50},{3,195},{4,52},{5,197},{6,54},{7,199},{8,56}... | collective-permute-start | bytes 491528 | tf_op jit(solution)/shard_map/ppermute | solution.py:40
  5.7 8.5 %collective-permute-start.4 = (bf16[64,1280]{1,0:T(8,128)(2,1)}, bf16[64,1280]{1,0:T(8,128)(2,1)S(1)}, u32[]{:S(2)}, u32[]{:S(2)}) collective-permute-start(bf16[64,1280]{1,0:T(8,128)(2,1)} %text.1), channel_id=1, source_target_pairs={{0,16},{1,65},{2,18},{3,67},{4,20},{5,69},{6,22},{7,71},{8,24},{9,... | collective-permute-start | bytes 491528 | tf_op jit(solution)/shard_map/ppermute | solution.py:40
  5.8 8.5 %collective-permute-start.6 = (bf16[64,1280]{1,0:T(8,128)(2,1)}, bf16[64,1280]{1,0:T(8,128)(2,1)S(1)}, u32[]{:S(2)}, u32[]{:S(2)}) collective-permute-start(bf16[64,1280]{1,0:T(8,128)(2,1)} %text.1), channel_id=1, source_target_pairs={{0,32},{1,129},{2,34},{3,131},{4,36},{5,133},{6,38},{7,135},{8,40}... | collective-permute-start | bytes 491528 | tf_op jit(solution)/shard_map/ppermute | solution.py:40
  8.0 7.4 %collective-permute-start.2 = (bf16[64,1280]{1,0:T(8,128)(2,1)S(1)}, bf16[64,1280]{1,0:T(8,128)(2,1)S(1)}, u32[]{:S(2)}, u32[]{:S(2)}) collective-permute-start(bf16[64,1280]{1,0:T(8,128)(2,1)S(1)} %collective-permute-done.refs_1_), channel_id=1, source_target_pairs={{0,2},{1,3},{2,4},{3,5},{4,6},{5,7},{6,8},{7,9},{8,10},{9,11},{10,... | collective-permute-start | bytes 491528 | tf_op jit(solution)/shard_map/ppermute | solution.py:31
  9.9 6.3 %collective-permute-start.3 = (bf16[64,1280]{1,0:T(8,128)(2,1)S(1)}, bf16[64,1280]{1,0:T(8,128)(2,1)S(1)}, u32[]{:S(2)}, u32[]{:S(2)}) collective-permute-start(bf16[64,1280]{1,0:T(8,128)(2,1)S(1)} %collective-permute-done.1.refs_2_), channel_id=1, source_target_pairs={{0,14},{1,15},{2,0},{3,1},{4,2},{5,3},{6,4},{7,5},{8,6},{9,7},{10,... | collective-permute-start | bytes 491528 | tf_op jit(solution)/shard_map/ppermute | solution.py:31
  14.2 0.9 copy-start
  15.2 26.2 %copy-start.1 = (bf16[64,1280]{1,0:T(8,128)(2,1)S(1)}, bf16[64,1280]{1,0:T(8,128)(2,1)}, u32[]{:S(2)}) copy-start(bf16[64,1280]{1,0:T(8,128)(2,1)} %refs_0_.1) | copy-start | bytes 491524
  16.2 20.1 %collective-permute-start.12 = (bf16[256,1280]{1,0:T(8,128)(2,1)S(1)}, bf16[256,1280]{1,0:T(8,128)(2,1)S(1)}, u32[]{:S(2)}, u32[]{:S(2)}) collective-permute-start(bf16[256,1280]{1,0:T(8,128)(2,1)S(1)} %shard_map.49.refs_8_), channel_id=1, source_target_pairs={{0,128},{1,33},{2,130},{3,35},{4,132},{5,37},{6,134},{7,39},{8,136... | collective-permute-start | bytes 1966088 | tf_op jit(solution)/shard_map/ppermute | solution.py:40
  19.2 17.1 %collective-permute-start.11 = (bf16[256,1280]{1,0:T(8,128)(2,1)S(1)}, bf16[256,1280]{1,0:T(8,128)(2,1)S(1)}, u32[]{:S(2)}, u32[]{:S(2)}) collective-permute-start(bf16[256,1280]{1,0:T(8,128)(2,1)S(1)} %shard_map.49.refs_8_), channel_id=1, source_target_pairs={{0,192},{1,49},{2,194},{3,51},{4,196},{5,53},{6,198},{7,55},{8,200... | collective-permute-start | bytes 1966088 | tf_op jit(solution)/shard_map/ppermute | solution.py:40
  20.4 16.0 %collective-permute-start.10 = (bf16[256,1280]{1,0:T(8,128)(2,1)S(1)}, bf16[256,1280]{1,0:T(8,128)(2,1)S(1)}, u32[]{:S(2)}, u32[]{:S(2)}) collective-permute-start(bf16[256,1280]{1,0:T(8,128)(2,1)S(1)} %shard_map.49.refs_8_), channel_id=1, source_target_pairs={{0,64},{1,17},{2,66},{3,19},{4,68},{5,21},{6,70},{7,23},{8,72},{9,... | collective-permute-start | bytes 1966088 | tf_op jit(solution)/shard_map/ppermute | solution.py:40
  21.3 6.6 %collective-permute-start.7 = (bf16[64,1280]{1,0:T(8,128)(2,1)S(1)}, bf16[64,1280]{1,0:T(8,128)(2,1)S(1)}, u32[]{:S(2)}, u32[]{:S(2)}) collective-permute-start(bf16[64,1280]{1,0:T(8,128)(2,1)S(1)} %collective-permute-done.2.refs_3_), channel_id=1, source_target_pairs={{0,2},{1,3},{2,4},{3,5},{4,6},{5,7},{6,8},{7,9},{8,10},{9,11},{10,... | collective-permute-start | bytes 491528 | tf_op jit(solution)/shard_map/ppermute | solution.py:31
  24.5 6.5 %collective-permute-start.8 = (bf16[64,1280]{1,0:T(8,128)(2,1)S(1)}, bf16[64,1280]{1,0:T(8,128)(2,1)S(1)}, u32[]{:S(2)}, u32[]{:S(2)}) collective-permute-start(bf16[64,1280]{1,0:T(8,128)(2,1)S(1)} %collective-permute-done.3.refs_4_), channel_id=1, source_target_pairs={{0,14},{1,15},{2,0},{3,1},{4,2},{5,3},{6,4},{7,5},{8,6},{9,7},{10,... | collective-permute-start | bytes 491528 | tf_op jit(solution)/shard_map/ppermute | solution.py:31
  31.0 5.3 %collective-permute-start.9 = (bf16[64,1280]{1,0:T(8,128)(2,1)S(1)}, bf16[64,1280]{1,0:T(8,128)(2,1)S(1)}, u32[]{:S(2)}, u32[]{:S(2)}) collective-permute-start(bf16[64,1280]{1,0:T(8,128)(2,1)S(1)} %collective-permute-done.7.refs_5_), channel_id=1, source_target_pairs={{0,2},{1,3},{2,4},{3,5},{4,6},{5,7},{6,8},{7,9},{8,10},{9,11},{10,... | collective-permute-start | bytes 491528 | tf_op jit(solution)/shard_map/ppermute | solution.py:31
  36.3 2.2 %collective-permute-start.13 = (bf16[256,1280]{1,0:T(8,128)(2,1)S(1)}, bf16[256,1280]{1,0:T(8,128)(2,1)S(1)}, u32[]{:S(2)}, u32[]{:S(2)}) collective-permute-start(bf16[256,1280]{1,0:T(8,128)(2,1)S(1)} %shard_map.49.refs_8_), channel_id=1, source_target_pairs={{0,1},{1,0},{2,3},{3,2},{4,5},{5,4},{6,7},{7,6},{8,9},{9,8},{10,11... | collective-permute-start | bytes 1966088 | tf_op jit(solution)/shard_map/ppermute | solution.py:54
  36.4 3.0 %collective-permute-start.14 = (bf16[256,1280]{1,0:T(8,128)(2,1)S(1)}, bf16[256,1280]{1,0:T(8,128)(2,1)S(1)}, u32[]{:S(2)}, u32[]{:S(2)}) collective-permute-start(bf16[256,1280]{1,0:T(8,128)(2,1)S(1)} %collective-permute-done.10.refs_9_), channel_id=1, source_target_pairs={{0,1},{1,0},{2,3},{3,2},{4,5},{5,4},{6,7},{7,6},{8,9},{9,8},{10,11... | collective-permute-start | bytes 1966088 | tf_op jit(solution)/shard_map/ppermute | solution.py:54
  36.9 3.5 %collective-permute-start.15 = (bf16[256,1280]{1,0:T(8,128)(2,1)S(1)}, bf16[256,1280]{1,0:T(8,128)(2,1)S(1)}, u32[]{:S(2)}, u32[]{:S(2)}) collective-permute-start(bf16[256,1280]{1,0:T(8,128)(2,1)S(1)} %collective-permute-done.11.refs_10_), channel_id=1, source_target_pairs={{0,1},{1,0},{2,3},{3,2},{4,5},{5,4},{6,7},{7,6},{8,9},{9,8},{10,11... | collective-permute-start | bytes 1966088 | tf_op jit(solution)/shard_map/ppermute | solution.py:54
  37.0 4.3 %collective-permute-start.16 = (bf16[256,1280]{1,0:T(8,128)(2,1)S(1)}, bf16[256,1280]{1,0:T(8,128)(2,1)S(1)}, u32[]{:S(2)}, u32[]{:S(2)}) collective-permute-start(bf16[256,1280]{1,0:T(8,128)(2,1)S(1)} %collective-permute-done.12.refs_11_), channel_id=1, source_target_pairs={{0,1},{1,0},{2,3},{3,2},{4,5},{5,4},{6,7},{7,6},{8,9},{9,8},{10,11... | collective-permute-start | bytes 1966088 | tf_op jit(solution)/shard_map/ppermute | solution.py:54
  47.6 4.1 %collective-permute-start.17 = (f32[1,512]{1,0:T(1,128)S(1)}, f32[1,512]{1,0:T(1,128)S(1)}, u32[]{:S(2)}, u32[]{:S(2)}) collective-permute-start(f32[1,512]{1,0:T(1,128)S(1)} %get-tuple-element.61), channel_id=1, source_target_pairs={{0,2},{1,3},{2,0},{3,1},{4,6},{5,7},{6,4},{7,5},{8,10},{9,11},{10,... | collective-permute-start | bytes 6152 | tf_op jit(solution)/shard_map/ppermute | solution.py:54
  50.1 6.2 %collective-permute-start.20 = (f32[1,2176]{1,0:T(1,128)S(1)}, f32[1,2176]{1,0:T(1,128)S(1)}, u32[]{:S(2)}, u32[]{:S(2)}) collective-permute-start(f32[1,2176]{1,0:T(1,128)S(1)} %get-tuple-element.62), channel_id=1, source_target_pairs={{0,1},{1,0},{2,3},{3,2},{4,5},{5,4},{6,7},{7,6},{8,9},{9,8},{10,11... | collective-permute-start | bytes 26120 | tf_op jit(solution)/shard_map/ppermute | solution.py:54
  50.1 28.6 %collective-permute-start.28 = (bf16[512,1280]{1,0:T(8,128)(2,1)S(1)}, bf16[512,1280]{1,0:T(8,128)(2,1)S(1)}, u32[]{:S(2)}, u32[]{:S(2)}) collective-permute-start(bf16[512,1280]{1,0:T(8,128)(2,1)S(1)} %get-tuple-element.66.refs_2_), channel_id=1, source_target_pairs={{0,1},{1,0},{2,3},{3,2},{4,5},{5,4},{6,7},{7,6},{8,9},{9,8},{10,11... | collective-permute-start | bytes 3932168 | tf_op jit(solution)/shard_map/ppermute | solution.py:54
  51.7 9.3 %collective-permute-start.18 = (f32[1,512]{1,0:T(1,128)S(1)}, f32[1,512]{1,0:T(1,128)S(1)}, u32[]{:S(2)}, u32[]{:S(2)}) collective-permute-start(f32[1,512]{1,0:T(1,128)S(1)} %log_add_fusion.2), channel_id=1, source_target_pairs={{0,4},{1,5},{2,6},{3,7},{4,0},{5,1},{6,2},{7,3},{8,12},{9,13},{10,... | collective-permute-start | bytes 6152 | tf_op jit(solution)/shard_map/ppermute | solution.py:54
  56.3 6.2 %collective-permute-start.23 = (f32[1,2176]{1,0:T(1,128)S(1)}, f32[1,2176]{1,0:T(1,128)S(1)}, u32[]{:S(2)}, u32[]{:S(2)}) collective-permute-start(f32[1,2176]{1,0:T(1,128)S(1)} %add_select_fusion.2), channel_id=1, source_target_pairs={{0,32},{1,33},{2,34},{3,35},{4,36},{5,37},{6,38},{7,39},{8,40},{9,... | collective-permute-start | bytes 26120 | tf_op jit(solution)/shard_map/ppermute | solution.py:77
  58.5 4.0 %collective-permute-start.22 = (f32[1,2176]{1,0:T(1,128)S(1)}, f32[1,2176]{1,0:T(1,128)S(1)}, u32[]{:S(2)}, u32[]{:S(2)}) collective-permute-start(f32[1,2176]{1,0:T(1,128)S(1)} %add_select_fusion.2), channel_id=1, source_target_pairs={{0,48},{1,49},{2,50},{3,51},{4,52},{5,53},{6,54},{7,55},{8,56},{9,... | collective-permute-start | bytes 26120 | tf_op jit(solution)/shard_map/ppermute | solution.py:77
  60.9 4.9 %collective-permute-start.21 = (f32[1,2176]{1,0:T(1,128)S(1)}, f32[1,2176]{1,0:T(1,128)S(1)}, u32[]{:S(2)}, u32[]{:S(2)}) collective-permute-start(f32[1,2176]{1,0:T(1,128)S(1)} %add_select_fusion.2), channel_id=1, source_target_pairs={{0,16},{1,17},{2,18},{3,19},{4,20},{5,21},{6,22},{7,23},{8,24},{9,... | collective-permute-start | bytes 26120 | tf_op jit(solution)/shard_map/ppermute | solution.py:77
  61.0 9.9 %collective-permute-start.19 = (f32[1,512]{1,0:T(1,128)S(1)}, f32[1,512]{1,0:T(1,128)S(1)}, u32[]{:S(2)}, u32[]{:S(2)}) collective-permute-start(f32[1,512]{1,0:T(1,128)S(1)} %log_add_fusion.1), channel_id=1, source_target_pairs={{0,8},{1,9},{2,10},{3,11},{4,12},{5,13},{6,14},{7,15},{8,0},{9,1},... | collective-permute-start | bytes 6152 | tf_op jit(solution)/shard_map/ppermute | solution.py:54
  65.9 5.2 %collective-permute-start.26 = (f32[1,2176]{1,0:T(1,128)S(1)}, f32[1,2176]{1,0:T(1,128)S(1)}, u32[]{:S(2)}, u32[]{:S(2)}) collective-permute-start(f32[1,2176]{1,0:T(1,128)S(1)} %add_select_fusion.1), channel_id=1, source_target_pairs={{0,128},{1,129},{2,130},{3,131},{4,132},{5,133},{6,134},{7,135},{8... | collective-permute-start | bytes 26120 | tf_op jit(solution)/shard_map/ppermute | solution.py:77
  68.9 3.7 %collective-permute-start.25 = (f32[1,2176]{1,0:T(1,128)S(1)}, f32[1,2176]{1,0:T(1,128)S(1)}, u32[]{:S(2)}, u32[]{:S(2)}) collective-permute-start(f32[1,2176]{1,0:T(1,128)S(1)} %add_select_fusion.1), channel_id=1, source_target_pairs={{0,192},{1,193},{2,194},{3,195},{4,196},{5,197},{6,198},{7,199},{8... | collective-permute-start | bytes 26120 | tf_op jit(solution)/shard_map/ppermute | solution.py:77
  70.1 4.9 %collective-permute-start.24 = (f32[1,2176]{1,0:T(1,128)S(1)}, f32[1,2176]{1,0:T(1,128)S(1)}, u32[]{:S(2)}, u32[]{:S(2)}) collective-permute-start(f32[1,2176]{1,0:T(1,128)S(1)} %add_select_fusion.1), channel_id=1, source_target_pairs={{0,64},{1,65},{2,66},{3,67},{4,68},{5,69},{6,70},{7,71},{8,72},{9,... | collective-permute-start | bytes 26120 | tf_op jit(solution)/shard_map/ppermute | solution.py:77
  75.9 2.8 %collective-permute-start.27 = (bf16[512,1024]{1,0:T(8,128)(2,1)S(1)}, bf16[512,1024]{1,0:T(8,128)(2,1)S(1)}, u32[]{:S(2)}, u32[]{:S(2)}) collective-permute-start(bf16[512,1024]{1,0:T(8,128)(2,1)S(1)} %shard_map.51.refs_1_), channel_id=1, source_target_pairs={{0,1},{1,0},{2,3},{3,2},{4,5},{5,4},{6,7},{7,6},{8,9},{9,8},{10,11... | collective-permute-start | bytes 3145736 | tf_op jit(solution)/shard_map/ppermute | solution.py:54
  76.9 1.7 %collective-permute-start.29 = (f32[1,128]{1,0:T(1,128)S(1)}, f32[1,128]{1,0:T(1,128)S(1)}, u32[]{:S(2)}, u32[]{:S(2)}) collective-permute-start(f32[1,128]{1,0:T(1,128)S(1)} %get-tuple-element.67.refs_4_), channel_id=1, source_target_pairs={{0,1},{1,0},{2,3},{3,2},{4,5},{5,4},{6,7},{7,6},{8,9},{9,8},{10,11... | collective-permute-start | bytes 1544 | tf_op jit(solution)/shard_map/ppermute | solution.py:54
  82.4 19.2 %collective-permute-start.32 = (bf16[2576,128]{1,0:T(8,128)(2,1)S(1)}, bf16[2576,128]{1,0:T(8,128)(2,1)S(1)}, u32[]{:S(2)}, u32[]{:S(2)}) collective-permute-start(bf16[2576,128]{1,0:T(8,128)(2,1)S(1)} %get-tuple-element.75), channel_id=1, source_target_pairs={{0,16},{1,65},{2,18},{3,67},{4,20},{5,69},{6,22},{7,71},{8,24},{9,... | collective-permute-start | bytes 1978376 | tf_op jit(solution)/shard_map/ppermute | solution.py:40
  82.8 18.9 %collective-permute-start.36 = (bf16[2576,128]{1,0:T(8,128)(2,1)S(1)}, bf16[2576,128]{1,0:T(8,128)(2,1)S(1)}, u32[]{:S(2)}, u32[]{:S(2)}) collective-permute-start(bf16[2576,128]{1,0:T(8,128)(2,1)S(1)} %get-tuple-element.85), channel_id=1, source_target_pairs={{0,32},{1,129},{2,34},{3,131},{4,36},{5,133},{6,38},{7,135},{8,40}... | collective-permute-start | bytes 1978376 | tf_op jit(solution)/shard_map/ppermute | solution.py:40
  84.2 18.3 %collective-permute-start.37 = (bf16[2576,128]{1,0:T(8,128)(2,1)S(1)}, bf16[2576,128]{1,0:T(8,128)(2,1)S(1)}, u32[]{:S(2)}, u32[]{:S(2)}) collective-permute-start(bf16[2576,128]{1,0:T(8,128)(2,1)S(1)} %get-tuple-element.86), channel_id=1, source_target_pairs={{0,48},{1,193},{2,50},{3,195},{4,52},{5,197},{6,54},{7,199},{8,56}... | collective-permute-start | bytes 1978376 | tf_op jit(solution)/shard_map/ppermute | solution.py:40
  89.8 14.6 %collective-permute-start.30 = (bf16[1296,128]{1,0:T(8,128)(2,1)S(1)}, bf16[1296,128]{1,0:T(8,128)(2,1)S(1)}, u32[]{:S(2)}, u32[]{:S(2)}) collective-permute-start(bf16[1296,128]{1,0:T(8,128)(2,1)S(1)} %get-tuple-element.72), channel_id=1, source_target_pairs={{0,2},{1,3},{2,4},{3,5},{4,6},{5,7},{6,8},{7,9},{8,10},{9,11},{10,... | collective-permute-start | bytes 995336 | tf_op jit(solution)/shard_map/ppermute | solution.py:31
  89.9 16.3 %collective-permute-start.31 = (bf16[1296,128]{1,0:T(8,128)(2,1)S(1)}, bf16[1296,128]{1,0:T(8,128)(2,1)S(1)}, u32[]{:S(2)}, u32[]{:S(2)}) collective-permute-start(bf16[1296,128]{1,0:T(8,128)(2,1)S(1)} %get-tuple-element.73), channel_id=1, source_target_pairs={{0,14},{1,15},{2,0},{3,1},{4,2},{5,3},{6,4},{7,5},{8,6},{9,7},{10,... | collective-permute-start | bytes 995336 | tf_op jit(solution)/shard_map/ppermute | solution.py:31
  101.6 8.9 %collective-permute-start.33 = (bf16[656,128]{1,0:T(8,128)(2,1)S(1)}, bf16[656,128]{1,0:T(8,128)(2,1)S(1)}, u32[]{:S(2)}, u32[]{:S(2)}) collective-permute-start(bf16[656,128]{1,0:T(8,128)(2,1)S(1)} %get-tuple-element.76), channel_id=1, source_target_pairs={{0,4},{1,13},{2,6},{3,15},{4,8},{5,1},{6,10},{7,3},{8,12},{9,5},{1... | collective-permute-start | bytes 503816 | tf_op jit(solution)/shard_map/ppermute | solution.py:45
  102.9 12.1 %collective-permute-start.38 = (bf16[656,128]{1,0:T(8,128)(2,1)S(1)}, bf16[656,128]{1,0:T(8,128)(2,1)S(1)}, u32[]{:S(2)}, u32[]{:S(2)}) collective-permute-start(bf16[656,128]{1,0:T(8,128)(2,1)S(1)} %get-tuple-element.89), channel_id=1, source_target_pairs={{0,64},{1,17},{2,66},{3,19},{4,68},{5,21},{6,70},{7,23},{8,72},{9,... | collective-permute-start | bytes 503816 | tf_op jit(solution)/shard_map/ppermute | solution.py:40
  102.9 12.0 %collective-permute-start.39 = (bf16[656,128]{1,0:T(8,128)(2,1)S(1)}, bf16[656,128]{1,0:T(8,128)(2,1)S(1)}, u32[]{:S(2)}, u32[]{:S(2)}) collective-permute-start(bf16[656,128]{1,0:T(8,128)(2,1)S(1)} %get-tuple-element.90), channel_id=1, source_target_pairs={{0,128},{1,33},{2,130},{3,35},{4,132},{5,37},{6,134},{7,39},{8,136... | collective-permute-start | bytes 503816 | tf_op jit(solution)/shard_map/ppermute | solution.py:40
  104.4 10.6 %collective-permute-start.40 = (bf16[656,128]{1,0:T(8,128)(2,1)S(1)}, bf16[656,128]{1,0:T(8,128)(2,1)S(1)}, u32[]{:S(2)}, u32[]{:S(2)}) collective-permute-start(bf16[656,128]{1,0:T(8,128)(2,1)S(1)} %get-tuple-element.91), channel_id=1, source_target_pairs={{0,192},{1,49},{2,194},{3,51},{4,196},{5,53},{6,198},{7,55},{8,200... | collective-permute-start | bytes 503816 | tf_op jit(solution)/shard_map/ppermute | solution.py:40
  110.7 8.7 %collective-permute-start.34 = (bf16[656,128]{1,0:T(8,128)(2,1)S(1)}, bf16[656,128]{1,0:T(8,128)(2,1)S(1)}, u32[]{:S(2)}, u32[]{:S(2)}) collective-permute-start(bf16[656,128]{1,0:T(8,128)(2,1)S(1)} %get-tuple-element.80), channel_id=1, source_target_pairs={{0,4},{1,5},{2,6},{3,7},{4,8},{5,9},{6,10},{7,11},{8,12},{9,13},{1... | collective-permute-start | bytes 503816 | tf_op jit(solution)/shard_map/ppermute | solution.py:31
  110.8 8.6 %collective-permute-start.35 = (bf16[656,128]{1,0:T(8,128)(2,1)S(1)}, bf16[656,128]{1,0:T(8,128)(2,1)S(1)}, u32[]{:S(2)}, u32[]{:S(2)}) collective-permute-start(bf16[656,128]{1,0:T(8,128)(2,1)S(1)} %get-tuple-element.81), channel_id=1, source_target_pairs={{0,12},{1,13},{2,14},{3,15},{4,0},{5,1},{6,2},{7,3},{8,4},{9,5},{1... | collective-permute-start | bytes 503816 | tf_op jit(solution)/shard_map/ppermute | solution.py:31

commit v3 on v2

--- a/solution.py
+++ b/solution.py
@@ -91,15 +91,14 @@
         in_specs=[vmem] * len(args),
         out_specs=[vmem] * len(outs),
         scratch_shapes=scratch,
-        cost_estimate=pl.CostEstimate(flops=flops, transcendentals=transcendentals, bytes_accessed=moved),
+        cost_estimate=pl.CostEstimate(flops=8 * flops, transcendentals=transcendentals, bytes_accessed=moved),
         compiler_params=pltpu.CompilerParams(vmem_limit_bytes=vmem_mib << 20),
     )(*args)
 
 
 def diagonal_blocks(c):
     for zz in range(NZ):
-        col = (zz // 4) * PLANE + (zz % 4) * NY * SHARD + c * 2 * SHARD
-        yield zz * SHARD, pl.multiple_of(col, 128)
+        yield zz // 4, zz * SHARD, pl.multiple_of((zz % 4) * NY * SHARD + c * 2 * SHARD, 128)
 
 
 def on_diagonal(x):
@@ -142,60 +141,75 @@
 STEPS = (0, 1, -1, 2)
 
 
-def scores_kernel(scale, at, *refs):
-    image_in, text_in = refs[:8], refs[8:16]
-    scores, img, txt, row_out, col_out, row_top, row_part = refs[16:]
-    x, y, z, c = at[0], at[1], at[2], at[3]
-    for ref, step in zip(image_in, (0, -1, 1, -2, 2, -3, 3, -4)):
-        where = lax.rem(z + step + NZ, NZ) * SHARD
-        img[pl.ds(pl.multiple_of(where, SHARD), SHARD), :] = ref[...]
-    for own in range(2):
-        core = c if own == 0 else 1 - c
-        for i, d in enumerate(STEPS):
-            for j, e in enumerate(STEPS):
-                dx, dy = jnp.where(core == 0, d, e), jnp.where(core == 0, e, d)
-                where = pl.multiple_of(core * PLANE + block_row(x - dx, y - dy), SHARD)
-                txt[pl.ds(where, SHARD), :] = text_in[own * 4 + i][j * SHARD : (j + 1) * SHARD, :]
-
+def place_text(at, core, parts, txt):
+    x, y = at[0], at[1]
+    for i, d in enumerate(STEPS):
+        for j, e in enumerate(STEPS):
+            dx, dy = jnp.where(core == 0, d, e), jnp.where(core == 0, e, d)
+            txt[pl.ds(block_row(x - dx, y - dy), SHARD), :] = parts[i][j * SHARD : (j + 1) * SHARD, :]
+
+
+def half_scores(scale, img, txt, scores, cols_out, row_top, row_sum):
     chunk = 512
-    row_part[...] = jnp.full((ROWS, 128), -jnp.inf, F32)
-
-    @pl.loop(0, COLS // chunk)
+    row_top[...] = jnp.full((ROWS, 128), -jnp.inf, F32)
+
+    @pl.loop(0, PLANE // chunk)
     def _(i):
         cols = pl.ds(pl.multiple_of(i * chunk, chunk), chunk)
         s = scale * lax.dot_general(
             img[...], txt[cols, :], (((1,), (1,)), ((), ())), preferred_element_type=F32
         )
         scores[:, cols] = s
-        tops = row_part[...]
+        tops = row_top[...]
         for j in range(chunk // 128):
             tops = jnp.maximum(tops, s[:, j * 128 : (j + 1) * 128])
-        row_part[...] = tops
+        row_top[...] = tops
         top = jnp.max(s, axis=0, keepdims=True)
-        col_out[:, cols] = top + jnp.log(jnp.sum(jnp.exp(s - top), axis=0, keepdims=True))
-
-    row_top[...] = jnp.broadcast_to(jnp.max(row_part[...], axis=1, keepdims=True), (ROWS, 128))
-    row_part[...] = jnp.zeros((ROWS, 128), F32)
-
-    @pl.loop(0, COLS // chunk)
+        cols_out[:, cols] = top + jnp.log(jnp.sum(jnp.exp(s - top), axis=0, keepdims=True))
+
+    row_top[...] = jnp.broadcast_to(jnp.max(row_top[...], axis=1, keepdims=True), (ROWS, 128))
+    row_sum[...] = jnp.zeros((ROWS, 128), F32)
+
+    @pl.loop(0, PLANE // 256)
     def _(i):
-        for j in range(chunk // 128):
-            cols = pl.ds(pl.multiple_of(i * chunk + j * 128, 128), 128)
-            row_part[...] += jnp.exp(scores[:, cols] - row_top[...])
-
-    row = row_top[...] + jnp.log(jnp.sum(row_part[...], axis=1, keepdims=True))
+        for j in range(2):
+            cols = pl.ds(pl.multiple_of(i * 256 + j * 128, 128), 128)
+            row_sum[...] += jnp.exp(scores[:, cols] - row_top[...])
+
+
+def own_scores_kernel(scale, at, *refs):
+    image_in, text_in = refs[:8], refs[8:12]
+    img, txt, scores, cols_out, row_top, row_sum = refs[12:]
+    for ref, step in zip(image_in, (0, -1, 1, -2, 2, -3, 3, -4)):
+        where = lax.rem(at[2] + step + NZ, NZ) * SHARD
+        img[pl.ds(pl.multiple_of(where, SHARD), SHARD), :] = ref[...]
+    place_text(at, at[3], text_in, txt)
+    half_scores(scale, img, txt, scores, cols_out, row_top, row_sum)
+
+
+def other_scores_kernel(scale, at, *refs):
+    text_in, (img, scores_own, cols_own, top_own, sum_own) = refs[:4], refs[4:9]
+    txt, scores, row_out, col_out, cols_other, row_top, row_sum = refs[9:]
+    x, y, z, c = at
+    place_text(at, 1 - c, text_in, txt)
+    half_scores(scale, img, txt, scores, cols_other, row_top, row_sum)
+    top = jnp.maximum(row_top[...], top_own[...])
+    total = row_sum[...] * jnp.exp(row_top[...] - top) + sum_own[...] * jnp.exp(top_own[...] - top)
+    row = top + jnp.log(jnp.sum(total, axis=1, keepdims=True))
     row_out[...] = jnp.transpose(row)[0:1, :]
+    col_out[:, pl.ds(pl.multiple_of(c * PLANE, PLANE), PLANE)] = cols_own[...]
+    col_out[:, pl.ds(pl.multiple_of((1 - c) * PLANE, PLANE), PLANE)] = cols_other[...]
     col_out[:, COLS:] = jnp.zeros((1, 128), F32)
 
     @pl.when(has_diagonal(x, y, z))
     def _():
         mask = on_diagonal(x)
         total = jnp.zeros((1, 128), F32)
-        for row, col in diagonal_blocks(c):
-            block = scores[row : row + SHARD, pl.ds(col, 128)]
+        for core, row, col in diagonal_blocks(c):
+            rows, cols = slice(row, row + SHARD), pl.ds(col, 128)
+            block = jnp.where(c == core, scores_own[rows, cols], scores[rows, cols])
             total += jnp.sum(jnp.where(mask, block, 0.0), axis=0, keepdims=True)
-        total = jnp.sum(total, axis=1, keepdims=True)
-        col_out[:, COLS:] = jnp.broadcast_to(total, (1, 128))
+        col_out[:, COLS:] = jnp.broadcast_to(jnp.sum(total, axis=1, keepdims=True), (1, 128))
 
 
 def line_kernel(text, *refs):
@@ -207,69 +221,77 @@
     copy.wait()
 
 
-def weights_kernel(own, at, scores, row_lse, col_lse, out, *refs):
+def weights_kernel(at, scores_own, scores_other, row_lse, col_lse, own_out, other_out, p_out, q_out, row_col):
     x, y, z, c = at
-    sums, row_col = refs[:-1], refs[-1]
     row_col[...] = jnp.transpose(jnp.broadcast_to(row_lse[...], (128, ROWS)))
-    half = c if own else 1 - c
 
     def weigh(s, rows, cols):
         return 0.5 * (jnp.exp(s - rows) + jnp.exp(s - cols))
 
     chunk = 128
-
-    @pl.loop(0, PLANE // chunk)
-    def _(i):
-        cols = pl.ds(pl.multiple_of(half * PLANE + i * chunk, chunk), chunk)
-        out[:, pl.ds(pl.multiple_of(i * chunk, chunk), chunk)] = weigh(
-            scores[:, cols], row_col[...], col_lse[:, cols]
-        ).astype(BF16)
+    for half, scores, out in ((1 - c, scores_other, other_out), (c, scores_own, own_out)):
+
+        @pl.loop(0, PLANE // chunk)
+        def _(i, half=half, scores=scores, out=out):
+            cols = pl.ds(pl.multiple_of(i * chunk, chunk), chunk)
+            lse = col_lse[:, pl.ds(pl.multiple_of(half * PLANE + i * chunk, chunk), chunk)]
+            out[:, cols] = weigh(scores[:, cols], row_col[...], lse).astype(BF16)
 
     @pl.when(has_diagonal(x, y, z))
     def _():
         mask = on_diagonal(x).astype(F32)
-        for zz, (row, col) in enumerate(diagonal_blocks(c)):
-            core = zz // 4
-
-            @pl.when(half == core)
-            def _(row=row, col=col, core=core):
+        for core, row, col in diagonal_blocks(c):
+
+            def subtract(scores, out):
                 rows, cols = pl.ds(row, SHARD), pl.ds(col, 128)
-                block = weigh(scores[rows, cols], row_col[rows, :], col_lse[:, cols]) - mask
-                out[rows, pl.ds(pl.multiple_of(col - core * PLANE, 128), 128)] = block.astype(BF16)
-
-    if own:
-        p_out, q_out = sums
-        row_sum = 0.5 * jnp.sum(row_lse[...], axis=1, keepdims=True)
-        p_out[...] = jnp.broadcast_to(row_sum, (1, 128))
-        col_sum = 0.5 * jnp.sum(col_lse[:, :COLS], axis=1, keepdims=True)
-        q_out[...] = jnp.broadcast_to(col_sum, (1, 128)) - col_lse[:, COLS:]
-
-
-def image_kernel(at, own, other, txt, q, up, down, far, here, up_two, down_two, total):
-    _, _, z, c = at
-    mine = pl.ds(pl.multiple_of(c * PLANE, PLANE), PLANE)
-    theirs = pl.ds(pl.multiple_of((1 - c) * PLANE, PLANE), PLANE)
+                lse = col_lse[:, pl.ds(pl.multiple_of(core * PLANE + col, 128), 128)]
+                out[rows, cols] = (weigh(scores[rows, cols], row_col[rows, :], lse) - mask).astype(BF16)
+
+            @pl.when(c == core)
+            def _():
+                subtract(scores_own, own_out)
+
+            @pl.when(c != core)
+            def _():
+                subtract(scores_other, other_out)
+
+    row_sum = 0.5 * jnp.sum(row_lse[...], axis=1, keepdims=True)
+    p_out[...] = jnp.broadcast_to(row_sum, (1, 128))
+    col_sum = 0.5 * jnp.sum(col_lse[:, :COLS], axis=1, keepdims=True)
+    q_out[...] = jnp.broadcast_to(col_sum, (1, 128)) - col_lse[:, COLS:]
+
+
+def image_kernel(steps, at, own, other, txt_own, txt_other, q, *refs):
+    z, first_core = at[2], at[3] == 0
+    far = refs[0] if steps[0][2] is None else None
+    outs, (rows_own, rows_other, total) = refs[0 if far is None else 1 : -3], refs[-3:]
+    for i, (dz, _, _) in enumerate(steps):
+        rows = pl.ds(pl.multiple_of(lax.rem(z + dz + NZ, NZ) * SHARD, SHARD), SHARD)
+        rows_own[i * SHARD : (i + 1) * SHARD, :] = own[rows, :]
+        rows_other[i * SHARD : (i + 1) * SHARD, :] = other[rows, :]
     chunk = 256
 
     @pl.loop(0, total.shape[1] // chunk)
     def _(i):
         cols = pl.ds(pl.multiple_of(i * chunk, chunk), chunk)
-        total[:, cols] = jnp.dot(own[...], txt[mine, cols], preferred_element_type=F32) + jnp.dot(
-            other[...], txt[theirs, cols], preferred_element_type=F32
+        total[:, cols] = jnp.dot(rows_own[...], txt_own[:, cols], preferred_element_type=F32) + jnp.dot(
+            rows_other[...], txt_other[:, cols], preferred_element_type=F32
         )
 
     strips = total.shape[1] // 128
-
-    def block(dz, strip):
-        return total[pl.ds(pl.multiple_of(lax.rem(z + dz + NZ, NZ) * SHARD, SHARD), SHARD), columns(strip)]
-
-    for i in range(strips):
-        for ref, index, dz in ((up, 0, 1), (up, 1, 3), (down, 0, -1), (down, 1, -3), (far, 0, 4)):
-            ref[part_of(ref, index, i, strips), :] = block(dz, i).astype(BF16)
-        for ref, dz in ((here, 0), (up_two, 2), (down_two, -2)):
-            ref[:, columns(i)] = block(dz, i)
-    for ref in (up, down, far):
-        write_note(ref, q[...])
+    for i, (_, out, place) in enumerate(steps):
+        for j in range(strips):
+            block = total[i * SHARD : (i + 1) * SHARD, columns(j)]
+            if place is None:
+                if out:
+                    far_rows = far[part_of(far, 0, j, strips), :].astype(F32)
+                    block += jnp.where(first_core == (out == 1), far_rows, 0.0)
+                outs[out][:, columns(j)] = block
+            else:
+                outs[out][part_of(outs[out], place, j, strips), :] = block.astype(BF16)
+    for ref in outs:
+        if ref.shape[1] == 128:
+            write_note(ref, q[...])
 
 
 def text_kernel(at, own, received, img, img_other, p_own, p_other, *refs):
@@ -309,9 +331,8 @@
     for i in range(strips):
         near, rest, cols = part_of(up, 0, i, strips), part_of(up, 1, i, strips), columns(i)
         here_out[:, cols] = here[:, cols] + up[near, :].astype(F32) + down[near, :].astype(F32)
-        far_rows = far[near, :].astype(F32)
-        above = up_two[:, cols] + up[rest, :].astype(F32) + jnp.where(first_core, far_rows, 0.0)
-        below = down_two[:, cols] + down[rest, :].astype(F32) + jnp.where(first_core, 0.0, far_rows)
+        above = up_two[:, cols] + up[rest, :].astype(F32)
+        below = down_two[:, cols] + down[rest, :].astype(F32)
         up_out[near, :] = above.astype(BF16)
         down_out[near, :] = below.astype(BF16)
     note_up, note_down, note_far = read_note(up), read_note(down), read_note(far)
@@ -375,24 +396,30 @@
     last, line, *far = lax.optimization_barrier((shift_z(up, 1), line, *far))
     image_in.append(last)
     text_in = [line, *far]
-    text_in += [swap_core(part) for part in text_in]
+    text_swapped = [swap_core(part) for part in text_in]
 
     tile = 2 * ROWS * COLS * embed
-    scores, img, txt, row_lse, col_lse = call(
-        functools.partial(scores_kernel, scale),
-        [
-            ((ROWS, COLS), F32),
-            ((ROWS, embed), BF16),
-            ((COLS, embed), BF16),
-            ((1, ROWS), F32),
-            ((1, COLS + 128), F32),
-        ],
+    half_scores_out = ((ROWS, PLANE), F32)
+    lanes = ((ROWS, 128), F32)
+    img, txt_own, scores_own, cols_own, top_own, sum_own = call(
+        functools.partial(own_scores_kernel, scale),
+        [((ROWS, embed), BF16), ((PLANE, embed), BF16), half_scores_out, ((1, PLANE), F32), lanes, lanes],
         image_in + text_in,
-        [pltpu.VMEM((ROWS, 128), F32), pltpu.VMEM((ROWS, 128), F32)],
-        tile,
-        2 * ROWS * COLS,
-        14 << 20,
-        16,
+        [],
+        tile // 2,
+        ROWS * COLS,
+        7 << 20,
+        12,
+    )
+    txt_other, scores_other, row_lse, col_lse = call(
+        functools.partial(other_scores_kernel, scale),
+        [((PLANE, embed), BF16), half_scores_out, ((1, ROWS), F32), ((1, COLS + 128), F32)],
+        [*text_swapped, img, scores_own, cols_own, top_own, sum_own],
+        [pltpu.VMEM((1, PLANE), F32), pltpu.VMEM((ROWS, 128), F32), pltpu.VMEM((ROWS, 128), F32)],
+        tile // 2,
+        ROWS * COLS,
+        7 << 20,
+        14,
     )
     img_other = swap_core(img)
     col_lse = merge_columns(col_lse, swap_core(col_lse))
@@ -403,22 +430,34 @@
 
     half = ((ROWS, PLANE), BF16)
     scalar = ((1, 128), F32)
-    weights = lambda own, outs, scores: call(
-        functools.partial(weights_kernel, own),
-        [half, *outs],
-        (scores, row_lse, col_lse),
+    own, other, p, q = call(
+        weights_kernel,
+        [half, half, scalar, scalar],
+        (scores_own, scores_other, row_lse, col_lse),
         [pltpu.VMEM((ROWS, 128), F32)],
-        4 * ROWS * COLS,
-        ROWS * COLS,
-        3 << 20,
+        8 * ROWS * COLS,
+        2 * ROWS * COLS,
+        6 << 20,
         12,
     )
-    (other,) = weights(False, [], scores)
-    scores, other = lax.optimization_barrier((scores, other))
     received = swap_core(other)
-    own, p, q = weights(True, [scalar, scalar], scores)
     p_other = swap_core(p)
     message = lambda rows: ((rows * embed // 128 + NOTE, 128), BF16)
+    image_part = lambda steps, outs, other, *far: call(
+        functools.partial(image_kernel, steps),
+        outs,
+        (own, other, txt_own, txt_other, q, *far),
+        [pltpu.VMEM((len(steps) * SHARD, PLANE), BF16)] * 2 + [pltpu.VMEM((len(steps) * SHARD, embed), F32)],
+        tile // 2,
+        0,
+        8 << 20,
+        16,
+    )
+    up, down, far = image_part(
+        ((1, 0, 0), (3, 0, 1), (-1, 1, 0), (-3, 1, 1), (4, 2, 0)), [message(2 * SHARD)] * 2 + [message(SHARD)], other
+    )
+    received, up = lax.optimization_barrier((received, up))
+    far = shift_far(far)
     *sent, kept, p = call(
         text_kernel,
         [message(4 * SHARD)] * 3 + [((4 * SHARD, embed), F32), scalar],
@@ -430,20 +469,11 @@
         24,
     )
     other, kept = lax.optimization_barrier((other, kept))
-    up, down, far, here, up_two, down_two = call(
-        image_kernel,
-        [message(2 * SHARD)] * 2 + [message(SHARD)] + [((SHARD, embed), F32)] * 3,
-        (own, other, txt, q),
-        [pltpu.VMEM((ROWS, embed), F32)],
-        tile,
-        0,
-        10 << 20,
-        16,
+    here, up_two, down_two = image_part(
+        ((0, 0, None), (2, 1, None), (-2, 2, None)), [((SHARD, embed), F32)] * 3, other, far
     )
     up, down = shift_z(up, 1), shift_z(down, -1)
     sent = [shift_plane(part, d, True) for d, part in enumerate(sent, 1)]
-    far, sent[0] = lax.optimization_barrier((far, sent[0]))
-    far = shift_far(far)
     up, down, here, q = call(
         image_middle_kernel,
         [message(SHARD)] * 2 + [((SHARD, embed), F32), scalar],

time: 120 us -> 114 us (0.950)
  waiting for transfers between devices: 45.7 us -> 38.5 us
    ppermute x11, waiting for transfers between devices: 6.13 us -> 1.1 us  [swap(): return lax.ppermute(value, AXES, pairs)]
    ppermute x12, waiting for transfers between devices: 12.8 us -> 15.3 us  [shift_plane(): return lax.ppermute(value, AXES, pairs)]
    ppermute x1, waiting for transfers between devices: 4.38 us -> 2.09 us  [shift_far(): return lax.ppermute(value, AXES, pairs)]
    ppermute x11, waiting for transfers between devices: 15 us -> 12.8 us  [shift_z(): return lax.ppermute(value, AXES, pairs)]
    ppermute x12, starting transfers between devices: 17.1 us -> 15.6 us  [shift_plane(): return lax.ppermute(value, AXES, pairs)]
    ppermute x6, starting transfers between devices: 9.66 us -> 8.39 us  [shift_one(): return lax.ppermute(value, AXES, pairs)]
    pallas_call x8 -> x9, Pallas kernels: 16.9 us -> 17.9 us  [call(): pl.pallas_call(lambda *refs: kernel(position(), *refs), out_shape=[jax.Sh...]
  transfers between devices with their start and end apart: 41 -> 41, of which waited for: 19 -> 17; matrix products, arithmetic and copies ran while one was open for 0% -> 0% of each run, Pallas kernels for 5% -> 12%
where the time goes in v3:
time: 114 us
  starting transfers between devices  54.7 us (48%)
  waiting for transfers between devices  38.5 us (34%)
  Pallas kernels  18.1 us (16%)
  local copies, waits for them, and re-layouts  1.83 us (2%)
    ppermute x11, starting transfers between devices, shift_z(): return lax.ppermute(value, AXES, pairs)  18.1 us
    pallas_call x9, Pallas kernels, call(): pl.pallas_call(lambda *refs: kernel(position(), *refs), out_shape=[jax.Sh...  17.9 us
    ppermute x12, starting transfers between devices, shift_plane(): return lax.ppermute(value, AXES, pairs)  15.6 us
    ppermute x12, waiting for transfers between devices, shift_plane(): return lax.ppermute(value, AXES, pairs)  15.3 us
    ppermute x11, waiting for transfers between devices, shift_z(): return lax.ppermute(value, AXES, pairs)  12.8 us
    ppermute x11, starting transfers between devices, swap(): return lax.ppermute(value, AXES, pairs)  11.5 us
    ppermute x6, starting transfers between devices, shift_one(): return lax.ppermute(value, AXES, pairs)  8.39 us
    ppermute x6, waiting for transfers between devices, shift_one(): return lax.ppermute(value, AXES, pairs)  7.17 us
  transfers between devices with their start and end apart: 41, of which 17 were waited for; matrix products, arithmetic and copies ran while one was open for 0% of the time, Pallas kernels for 12%

profile of v3, /device:TPU:32, one launch (start us, length us, event | category | flops | bytes accessed | tf_op | source)
XLA Modules:
  0.0 114.2 jit_solution(17630579779006111282)
XLA Ops:
  0.6 2.0 %collective-permute-start = (bf16[64,1280]{1,0:T(8,128)(2,1)}, bf16[64,1280]{1,0:T(8,128)(2,1)S(1)}, u32[]{:S(2)}, u32[]{:S(2)}) collective-permute-start(bf16[64,1280]{1,0:T(8,128)(2,1)} %refs_0_.1), channel_id=1, source_target_pairs={{0,2},{1,3},{2,4},{3,5},{4,6},{5,7},{6,8},{7,9},{8,10},{9,11},{10,... | collective-permute-start | bytes 491528 | tf_op jit(solution)/shard_map/ppermute | solution.py:31
  2.7 1.6 %collective-permute-start.4 = (bf16[64,1280]{1,0:T(8,128)(2,1)}, bf16[64,1280]{1,0:T(8,128)(2,1)S(1)}, u32[]{:S(2)}, u32[]{:S(2)}) collective-permute-start(bf16[64,1280]{1,0:T(8,128)(2,1)} %text.1), channel_id=1, source_target_pairs={{0,16},{1,65},{2,18},{3,67},{4,20},{5,69},{6,22},{7,71},{8,24},{9,... | collective-permute-start | bytes 491528 | tf_op jit(solution)/shard_map/ppermute | solution.py:40
  4.3 1.7 %collective-permute-start.5 = (bf16[64,1280]{1,0:T(8,128)(2,1)}, bf16[64,1280]{1,0:T(8,128)(2,1)S(1)}, u32[]{:S(2)}, u32[]{:S(2)}) collective-permute-start(bf16[64,1280]{1,0:T(8,128)(2,1)} %text.1), channel_id=1, source_target_pairs={{0,48},{1,193},{2,50},{3,195},{4,52},{5,197},{6,54},{7,199},{8,56}... | collective-permute-start | bytes 491528 | tf_op jit(solution)/shard_map/ppermute | solution.py:40
  6.0 2.0 %collective-permute-start.6 = (bf16[64,1280]{1,0:T(8,128)(2,1)}, bf16[64,1280]{1,0:T(8,128)(2,1)S(1)}, u32[]{:S(2)}, u32[]{:S(2)}) collective-permute-start(bf16[64,1280]{1,0:T(8,128)(2,1)} %text.1), channel_id=1, source_target_pairs={{0,32},{1,129},{2,34},{3,131},{4,36},{5,133},{6,38},{7,135},{8,40}... | collective-permute-start | bytes 491528 | tf_op jit(solution)/shard_map/ppermute | solution.py:40
  8.0 1.9 %collective-permute-start.2 = (bf16[64,1280]{1,0:T(8,128)(2,1)S(1)}, bf16[64,1280]{1,0:T(8,128)(2,1)S(1)}, u32[]{:S(2)}, u32[]{:S(2)}) collective-permute-start(bf16[64,1280]{1,0:T(8,128)(2,1)S(1)} %collective-permute-done.refs_1_), channel_id=1, source_target_pairs={{0,2},{1,3},{2,4},{3,5},{4,6},{5,7},{6,8},{7,9},{8,10},{9,11},{10,... | collective-permute-start | bytes 491528 | tf_op jit(solution)/shard_map/ppermute | solution.py:31
  9.9 2.2 %collective-permute-start.3 = (bf16[64,1280]{1,0:T(8,128)(2,1)S(1)}, bf16[64,1280]{1,0:T(8,128)(2,1)S(1)}, u32[]{:S(2)}, u32[]{:S(2)}) collective-permute-start(bf16[64,1280]{1,0:T(8,128)(2,1)S(1)} %collective-permute-done.1.refs_2_), channel_id=1, source_target_pairs={{0,14},{1,15},{2,0},{3,1},{4,2},{5,3},{6,4},{7,5},{8,6},{9,7},{10,... | collective-permute-start | bytes 491528 | tf_op jit(solution)/shard_map/ppermute | solution.py:31
  12.1 0.9 collective-permute-done.6.refs_2_
  13.0 0.9 copy-done
  14.1 1.1 collective-permute-done.2.refs_3_
  15.3 0.9 collective-permute-done.3.refs_4_
  16.2 1.5 %collective-permute-start.10 = (bf16[256,1280]{1,0:T(8,128)(2,1)S(1)}, bf16[256,1280]{1,0:T(8,128)(2,1)S(1)}, u32[]{:S(2)}, u32[]{:S(2)}) collective-permute-start(bf16[256,1280]{1,0:T(8,128)(2,1)S(1)} %shard_map.49.refs_8_), channel_id=1, source_target_pairs={{0,64},{1,17},{2,66},{3,19},{4,68},{5,21},{6,70},{7,23},{8,72},{9,... | collective-permute-start | bytes 1966088 | tf_op jit(solution)/shard_map/ppermute | solution.py:40
  17.7 1.7 %collective-permute-start.11 = (bf16[256,1280]{1,0:T(8,128)(2,1)S(1)}, bf16[256,1280]{1,0:T(8,128)(2,1)S(1)}, u32[]{:S(2)}, u32[]{:S(2)}) collective-permute-start(bf16[256,1280]{1,0:T(8,128)(2,1)S(1)} %shard_map.49.refs_8_), channel_id=1, source_target_pairs={{0,192},{1,49},{2,194},{3,51},{4,196},{5,53},{6,198},{7,55},{8,200... | collective-permute-start | bytes 1966088 | tf_op jit(solution)/shard_map/ppermute | solution.py:40
  19.4 1.8 %collective-permute-start.12 = (bf16[256,1280]{1,0:T(8,128)(2,1)S(1)}, bf16[256,1280]{1,0:T(8,128)(2,1)S(1)}, u32[]{:S(2)}, u32[]{:S(2)}) collective-permute-start(bf16[256,1280]{1,0:T(8,128)(2,1)S(1)} %shard_map.49.refs_8_), channel_id=1, source_target_pairs={{0,128},{1,33},{2,130},{3,35},{4,132},{5,37},{6,134},{7,39},{8,136... | collective-permute-start | bytes 1966088 | tf_op jit(solution)/shard_map/ppermute | solution.py:40
  21.3 3.2 %collective-permute-start.7 = (bf16[64,1280]{1,0:T(8,128)(2,1)S(1)}, bf16[64,1280]{1,0:T(8,128)(2,1)S(1)}, u32[]{:S(2)}, u32[]{:S(2)}) collective-permute-start(bf16[64,1280]{1,0:T(8,128)(2,1)S(1)} %collective-permute-done.2.refs_3_), channel_id=1, source_target_pairs={{0,2},{1,3},{2,4},{3,5},{4,6},{5,7},{6,8},{7,9},{8,10},{9,11},{10,... | collective-permute-start | bytes 491528 | tf_op jit(solution)/shard_map/ppermute | solution.py:31
  24.5 2.8 %collective-permute-done.7.refs_5_ = bf16[64,1280]{1,0:T(8,128)(2,1)S(1)} collective-permute-done((bf16[64,1280]{1,0:T(8,128)(2,1)S(1)}, bf16[64,1280]{1,0:T(8,128)(2,1)S(1)}, u32[]{:S(2)}, u32[]{:S(2)}) %collective-permute-start.7) | collective-permute-done | bytes 163872 | tf_op jit(solution)/shard_map/ppermute | solution.py:31
  27.3 3.7 %collective-permute-done.8.refs_6_ = bf16[64,1280]{1,0:T(8,128)(2,1)S(1)} collective-permute-done((bf16[64,1280]{1,0:T(8,128)(2,1)S(1)}, bf16[64,1280]{1,0:T(8,128)(2,1)S(1)}, u32[]{:S(2)}, u32[]{:S(2)}) %collective-permute-start.8) | collective-permute-done | bytes 163872 | tf_op jit(solution)/shard_map/ppermute | solution.py:31
  31.0 2.0 %collective-permute-start.9 = (bf16[64,1280]{1,0:T(8,128)(2,1)S(1)}, bf16[64,1280]{1,0:T(8,128)(2,1)S(1)}, u32[]{:S(2)}, u32[]{:S(2)}) collective-permute-start(bf16[64,1280]{1,0:T(8,128)(2,1)S(1)} %collective-permute-done.7.refs_5_), channel_id=1, source_target_pairs={{0,2},{1,3},{2,4},{3,5},{4,6},{5,7},{6,8},{7,9},{8,10},{9,11},{10,... | collective-permute-start | bytes 491528 | tf_op jit(solution)/shard_map/ppermute | solution.py:31
  33.0 3.3 %collective-permute-done.9.refs_7_ = bf16[64,1280]{1,0:T(8,128)(2,1)S(1)} collective-permute-done((bf16[64,1280]{1,0:T(8,128)(2,1)S(1)}, bf16[64,1280]{1,0:T(8,128)(2,1)S(1)}, u32[]{:S(2)}, u32[]{:S(2)}) %collective-permute-start.9) | collective-permute-done | bytes 163872 | tf_op jit(solution)/shard_map/ppermute | solution.py:31
  37.5 0.9 copy-done.1
  38.4 3.0 %shard_map.50 = (bf16[512,1280]{1,0:T(8,128)(2,1)S(1)}, bf16[1024,1280]{1,0:T(8,128)(2,1)S(1)}, f32[512,1024]{1,0:T(8,128)S(1)}, f32[1,1024]{1,0:T(1,128)S(1)}, ...) custom-call(bf16[64,1280]{1,0:T(8,128)(2,1)S(1)} %copy-done.1, bf16[64,1280]{1,0:T(8,128)(2,1)S(1)} %collective-permute-done.refs_1_, ...), custom_call_target="tpu_custom_call" | custom-call | flops 10737418240 | bytes 7340032 | tf_op jit(solution)/shard_map/pallas_call | solution.py:88
  41.5 3.2 %shard_map.51 = (bf16[1024,1280]{1,0:T(8,128)(2,1)S(1)}, f32[512,1024]{1,0:T(8,128)S(1)}, f32[1,512]{1,0:T(1,128)S(1)}, f32[1,2176]{1,0:T(1,128)S(1)}) custom-call(bf16[256,1280]{1,0:T(8,128)(2,1)S(1)} %collective-permute-done.13.refs_0_, bf16[256,1280]{1,0:T(8,128)(2,1)S(1)} %collective-permute-done.14.refs_1_, ...), custom_call_target="tpu_custom_call" | custom-call | flops 10737418240 | bytes 7340032 | tf_op jit(solution)/shard_map/pallas_call | solution.py:88
  44.7 2.1 %collective-permute-start.17 = (f32[1,512]{1,0:T(1,128)S(1)}, f32[1,512]{1,0:T(1,128)S(1)}, u32[]{:S(2)}, u32[]{:S(2)}) collective-permute-start(f32[1,512]{1,0:T(1,128)S(1)} %get-tuple-element.70), channel_id=1, source_target_pairs={{0,2},{1,3},{2,0},{3,1},{4,6},{5,7},{6,4},{7,5},{8,10},{9,11},{10,... | collective-permute-start | bytes 6152 | tf_op jit(solution)/shard_map/ppermute | solution.py:54
  47.2 1.1 collective-permute-done.17
  48.3 5.6 %collective-permute-start.18 = (f32[1,512]{1,0:T(1,128)S(1)}, f32[1,512]{1,0:T(1,128)S(1)}, u32[]{:S(2)}, u32[]{:S(2)}) collective-permute-start(f32[1,512]{1,0:T(1,128)S(1)} %log_add_fusion.2), channel_id=1, source_target_pairs={{0,4},{1,5},{2,6},{3,7},{4,0},{5,1},{6,2},{7,3},{8,12},{9,13},{10,... | collective-permute-start | bytes 6152 | tf_op jit(solution)/shard_map/ppermute | solution.py:54
  54.0 2.2 %collective-permute-start.23 = (f32[1,2176]{1,0:T(1,128)S(1)}, f32[1,2176]{1,0:T(1,128)S(1)}, u32[]{:S(2)}, u32[]{:S(2)}) collective-permute-start(f32[1,2176]{1,0:T(1,128)S(1)} %add_select_fusion.2), channel_id=1, source_target_pairs={{0,32},{1,33},{2,34},{3,35},{4,36},{5,37},{6,38},{7,39},{8,40},{9,... | collective-permute-start | bytes 26120 | tf_op jit(solution)/shard_map/ppermute | solution.py:77
  56.1 1.3 %collective-permute-start.22 = (f32[1,2176]{1,0:T(1,128)S(1)}, f32[1,2176]{1,0:T(1,128)S(1)}, u32[]{:S(2)}, u32[]{:S(2)}) collective-permute-start(f32[1,2176]{1,0:T(1,128)S(1)} %add_select_fusion.2), channel_id=1, source_target_pairs={{0,48},{1,49},{2,50},{3,51},{4,52},{5,53},{6,54},{7,55},{8,56},{9,... | collective-permute-start | bytes 26120 | tf_op jit(solution)/shard_map/ppermute | solution.py:77
  58.2 1.7 %collective-permute-start.19 = (f32[1,512]{1,0:T(1,128)S(1)}, f32[1,512]{1,0:T(1,128)S(1)}, u32[]{:S(2)}, u32[]{:S(2)}) collective-permute-start(f32[1,512]{1,0:T(1,128)S(1)} %log_add_fusion.1), channel_id=1, source_target_pairs={{0,8},{1,9},{2,10},{3,11},{4,12},{5,13},{6,14},{7,15},{8,0},{9,1},... | collective-permute-start | bytes 6152 | tf_op jit(solution)/shard_map/ppermute | solution.py:54
  59.9 2.3 %collective-permute-done.21 = f32[1,2176]{1,0:T(1,128)S(1)} collective-permute-done((f32[1,2176]{1,0:T(1,128)S(1)}, f32[1,2176]{1,0:T(1,128)S(1)}, u32[]{:S(2)}, u32[]{:S(2)}) %collective-permute-start.21) | collective-permute-done | bytes 8736 | tf_op jit(solution)/shard_map/ppermute | solution.py:77
  62.3 0.9 collective-permute-start.26
  63.2 3.3 %collective-permute-start.25 = (f32[1,2176]{1,0:T(1,128)S(1)}, f32[1,2176]{1,0:T(1,128)S(1)}, u32[]{:S(2)}, u32[]{:S(2)}) collective-permute-start(f32[1,2176]{1,0:T(1,128)S(1)} %add_select_fusion.1), channel_id=1, source_target_pairs={{0,192},{1,193},{2,194},{3,195},{4,196},{5,197},{6,198},{7,199},{8... | collective-permute-start | bytes 26120 | tf_op jit(solution)/shard_map/ppermute | solution.py:77
  66.5 1.0 collective-permute-done.26
  67.9 3.5 %collective-permute-done.24 = f32[1,2176]{1,0:T(1,128)S(1)} collective-permute-done((f32[1,2176]{1,0:T(1,128)S(1)}, f32[1,2176]{1,0:T(1,128)S(1)}, u32[]{:S(2)}, u32[]{:S(2)}) %collective-permute-start.24) | collective-permute-done | bytes 8736 | tf_op jit(solution)/shard_map/ppermute | solution.py:77
  71.4 1.7 %shard_map.52 = (bf16[512,1024]{1,0:T(8,128)(2,1)S(1)}, bf16[512,1024]{1,0:T(8,128)(2,1)S(1)}, f32[1,128]{1,0:T(1,128)S(1)}, f32[1,128]{1,0:T(1,128)S(1)}) custom-call(f32[512,1024]{1,0:T(8,128)S(1)} %get-tuple-element.64.refs_5_.refs_0_, f32[512,1024]{1,0:T(8,128)S(1)} %get-tuple-element.69.refs_1_, f32[1,512]{1,0:T(1,128)S(1)} %log_add_fusion.refs_2_, ...), custom_call_target="tpu_custom_call" | custom-call | flops 67108864 | bytes 6291456 | tf_op jit(solution)/shard_map/pallas_call | solution.py:88
  73.6 2.8 %shard_map.53 = (bf16[1296,128]{1,0:T(8,128)(2,1)S(1)}, bf16[1296,128]{1,0:T(8,128)(2,1)S(1)}, bf16[656,128]{1,0:T(8,128)(2,1)S(1)}) custom-call(bf16[512,1024]{1,0:T(8,128)(2,1)S(1)} %get-tuple-element.73.refs_0_, bf16[512,1024]{1,0:T(8,128)(2,1)S(1)} %get-tuple-element.84.refs_1_, bf16[1024,1280]{1,0:T(8,128)(2,1)S(1)} %get-tuple-element.74.refs_2_, ...), custom_call_target="tpu_custom_call" | custom-call | flops 10737418240 | bytes 8388608 | tf_op jit(solution)/shard_map/pallas_call | solution.py:88
  76.9 1.2 %collective-permute-start.30 = (bf16[656,128]{1,0:T(8,128)(2,1)S(1)}, bf16[656,128]{1,0:T(8,128)(2,1)S(1)}, u32[]{:S(2)}, u32[]{:S(2)}) collective-permute-start(bf16[656,128]{1,0:T(8,128)(2,1)S(1)} %get-tuple-element.80), channel_id=1, source_target_pairs={{0,4},{1,13},{2,6},{3,15},{4,8},{5,1},{6,10},{7,3},{8,12},{9,5},{1... | collective-permute-start | bytes 503816 | tf_op jit(solution)/shard_map/ppermute | solution.py:45
  78.1 1.9 %collective-permute-start.28 = (bf16[1296,128]{1,0:T(8,128)(2,1)S(1)}, bf16[1296,128]{1,0:T(8,128)(2,1)S(1)}, u32[]{:S(2)}, u32[]{:S(2)}) collective-permute-start(bf16[1296,128]{1,0:T(8,128)(2,1)S(1)} %get-tuple-element.78), channel_id=1, source_target_pairs={{0,2},{1,3},{2,4},{3,5},{4,6},{5,7},{6,8},{7,9},{8,10},{9,11},{10,... | collective-permute-start | bytes 995336 | tf_op jit(solution)/shard_map/ppermute | solution.py:31
  80.0 3.9 %shard_map.54 = (bf16[2576,128]{1,0:T(8,128)(2,1)S(1)}, bf16[2576,128]{1,0:T(8,128)(2,1)S(1)}, bf16[2576,128]{1,0:T(8,128)(2,1)S(1)}, f32[256,1280]{1,0:T(8,128)S(1)}, f32[1,128]{1,0:T(1,128)S(1)}) custom-call(bf16[512,1024]{1,0:T(8,128)(2,1)S(1)} %get-tuple-element.73.refs_0_, bf16[512,1024]{1,0:T(8,128)(2,1)S(1)} %collective-permute-done.27.refs_1_, ...), custom_call_target="tpu_custom_call" | custom-call | flops 10737418240 | bytes 12582912 | tf_op jit(solution)/shard_map/pallas_call | solution.py:88
  83.9 1.9 %collective-permute-start.36 = (bf16[2576,128]{1,0:T(8,128)(2,1)S(1)}, bf16[2576,128]{1,0:T(8,128)(2,1)S(1)}, u32[]{:S(2)}, u32[]{:S(2)}) collective-permute-start(bf16[2576,128]{1,0:T(8,128)(2,1)S(1)} %get-tuple-element.93), channel_id=1, source_target_pairs={{0,32},{1,129},{2,34},{3,131},{4,36},{5,133},{6,38},{7,135},{8,40}... | collective-permute-start | bytes 1978376 | tf_op jit(solution)/shard_map/ppermute | solution.py:40
  85.9 2.1 %collective-permute-done.30.refs_5_.refs_2_ = bf16[656,128]{1,0:T(8,128)(2,1)S(1)} collective-permute-done((bf16[656,128]{1,0:T(8,128)(2,1)S(1)}, bf16[656,128]{1,0:T(8,128)(2,1)S(1)}, u32[]{:S(2)}, u32[]{:S(2)}) %collective-permute-start.30) | collective-permute-done | bytes 167968 | tf_op jit(solution)/shard_map/ppermute | solution.py:45
  88.0 2.1 %shard_map.55 = (f32[64,1280]{1,0:T(8,128)S(1)}, f32[64,1280]{1,0:T(8,128)S(1)}, f32[64,1280]{1,0:T(8,128)S(1)}) custom-call(bf16[512,1024]{1,0:T(8,128)(2,1)S(1)} %get-tuple-element.73.refs_0_, bf16[512,1024]{1,0:T(8,128)(2,1)S(1)} %get-tuple-element.84.refs_1_, bf16[1024,1280]{1,0:T(8,128)(2,1)S(1)} %get-tuple-element.74.refs_2_, ...), custom_call_target="tpu_custom_call" | custom-call | flops 10737418240 | bytes 8388608 | tf_op jit(solution)/shard_map/pallas_call | solution.py:88
  90.1 0.9 collective-permute-done.28.refs_0_
  91.1 1.9 %collective-permute-start.33 = (bf16[656,128]{1,0:T(8,128)(2,1)S(1)}, bf16[656,128]{1,0:T(8,128)(2,1)S(1)}, u32[]{:S(2)}, u32[]{:S(2)}) collective-permute-start(bf16[656,128]{1,0:T(8,128)(2,1)S(1)} %get-tuple-element.88), channel_id=1, source_target_pairs={{0,4},{1,5},{2,6},{3,7},{4,8},{5,9},{6,10},{7,11},{8,12},{9,13},{1... | collective-permute-start | bytes 503816 | tf_op jit(solution)/shard_map/ppermute | solution.py:31
  93.1 2.3 %collective-permute-start.34 = (bf16[656,128]{1,0:T(8,128)(2,1)S(1)}, bf16[656,128]{1,0:T(8,128)(2,1)S(1)}, u32[]{:S(2)}, u32[]{:S(2)}) collective-permute-start(bf16[656,128]{1,0:T(8,128)(2,1)S(1)} %get-tuple-element.89), channel_id=1, source_target_pairs={{0,12},{1,13},{2,14},{3,15},{4,0},{5,1},{6,2},{7,3},{8,4},{9,5},{1... | collective-permute-start | bytes 503816 | tf_op jit(solution)/shard_map/ppermute | solution.py:31
  95.3 7.5 %collective-permute-done.35.refs_0_ = bf16[2576,128]{1,0:T(8,128)(2,1)S(1)} collective-permute-done((bf16[2576,128]{1,0:T(8,128)(2,1)S(1)}, bf16[2576,128]{1,0:T(8,128)(2,1)S(1)}, u32[]{:S(2)}, u32[]{:S(2)}) %collective-permute-start.35) | collective-permute-done | bytes 659488 | tf_op jit(solution)/shard_map/ppermute | solution.py:40
  104.2 1.4 %collective-permute-start.39 = (bf16[656,128]{1,0:T(8,128)(2,1)S(1)}, bf16[656,128]{1,0:T(8,128)(2,1)S(1)}, u32[]{:S(2)}, u32[]{:S(2)}) collective-permute-start(bf16[656,128]{1,0:T(8,128)(2,1)S(1)} %get-tuple-element.98), channel_id=1, source_target_pairs={{0,128},{1,33},{2,130},{3,35},{4,132},{5,37},{6,134},{7,39},{8,136... | collective-permute-start | bytes 503816 | tf_op jit(solution)/shard_map/ppermute | solution.py:40
  105.6 1.8 %collective-permute-start.40 = (bf16[656,128]{1,0:T(8,128)(2,1)S(1)}, bf16[656,128]{1,0:T(8,128)(2,1)S(1)}, u32[]{:S(2)}, u32[]{:S(2)}) collective-permute-start(bf16[656,128]{1,0:T(8,128)(2,1)S(1)} %get-tuple-element.99), channel_id=1, source_target_pairs={{0,192},{1,49},{2,194},{3,51},{4,196},{5,53},{6,198},{7,55},{8,200... | collective-permute-start | bytes 503816 | tf_op jit(solution)/shard_map/ppermute | solution.py:40
  107.4 5.1 %collective-permute-done.38.refs_4_ = bf16[656,128]{1,0:T(8,128)(2,1)S(1)} collective-permute-done((bf16[656,128]{1,0:T(8,128)(2,1)S(1)}, bf16[656,128]{1,0:T(8,128)(2,1)S(1)}, u32[]{:S(2)}, u32[]{:S(2)}) %collective-permute-start.38) | collective-permute-done | bytes 167968 | tf_op jit(solution)/shard_map/ppermute | solution.py:40
  112.5 0.9 collective-permute-done.40.refs_6_
  (54 shorter events, 6.7 us)
Async XLA Ops:
  0.6 7.3 %collective-permute-start = (bf16[64,1280]{1,0:T(8,128)(2,1)}, bf16[64,1280]{1,0:T(8,128)(2,1)S(1)}, u32[]{:S(2)}, u32[]{:S(2)}) collective-permute-start(bf16[64,1280]{1,0:T(8,128)(2,1)} %refs_0_.1), channel_id=1, source_target_pairs={{0,2},{1,3},{2,4},{3,5},{4,6},{5,7},{6,8},{7,9},{8,10},{9,11},{10,... | collective-permute-start | bytes 491528 | tf_op jit(solution)/shard_map/ppermute | solution.py:31
  2.6 7.3 %collective-permute-start.1 = (bf16[64,1280]{1,0:T(8,128)(2,1)}, bf16[64,1280]{1,0:T(8,128)(2,1)S(1)}, u32[]{:S(2)}, u32[]{:S(2)}) collective-permute-start(bf16[64,1280]{1,0:T(8,128)(2,1)} %refs_0_.1), channel_id=1, source_target_pairs={{0,14},{1,15},{2,0},{3,1},{4,2},{5,3},{6,4},{7,5},{8,6},{9,7},{10,... | collective-permute-start | bytes 491528 | tf_op jit(solution)/shard_map/ppermute | solution.py:31
  2.7 9.3 %collective-permute-start.4 = (bf16[64,1280]{1,0:T(8,128)(2,1)}, bf16[64,1280]{1,0:T(8,128)(2,1)S(1)}, u32[]{:S(2)}, u32[]{:S(2)}) collective-permute-start(bf16[64,1280]{1,0:T(8,128)(2,1)} %text.1), channel_id=1, source_target_pairs={{0,16},{1,65},{2,18},{3,67},{4,20},{5,69},{6,22},{7,71},{8,24},{9,... | collective-permute-start | bytes 491528 | tf_op jit(solution)/shard_map/ppermute | solution.py:40
  4.3 7.8 %collective-permute-start.5 = (bf16[64,1280]{1,0:T(8,128)(2,1)}, bf16[64,1280]{1,0:T(8,128)(2,1)S(1)}, u32[]{:S(2)}, u32[]{:S(2)}) collective-permute-start(bf16[64,1280]{1,0:T(8,128)(2,1)} %text.1), channel_id=1, source_target_pairs={{0,48},{1,193},{2,50},{3,195},{4,52},{5,197},{6,54},{7,199},{8,56}... | collective-permute-start | bytes 491528 | tf_op jit(solution)/shard_map/ppermute | solution.py:40
  6.0 7.0 %collective-permute-start.6 = (bf16[64,1280]{1,0:T(8,128)(2,1)}, bf16[64,1280]{1,0:T(8,128)(2,1)S(1)}, u32[]{:S(2)}, u32[]{:S(2)}) collective-permute-start(bf16[64,1280]{1,0:T(8,128)(2,1)} %text.1), channel_id=1, source_target_pairs={{0,32},{1,129},{2,34},{3,131},{4,36},{5,133},{6,38},{7,135},{8,40}... | collective-permute-start | bytes 491528 | tf_op jit(solution)/shard_map/ppermute | solution.py:40
  8.0 7.3 %collective-permute-start.2 = (bf16[64,1280]{1,0:T(8,128)(2,1)S(1)}, bf16[64,1280]{1,0:T(8,128)(2,1)S(1)}, u32[]{:S(2)}, u32[]{:S(2)}) collective-permute-start(bf16[64,1280]{1,0:T(8,128)(2,1)S(1)} %collective-permute-done.refs_1_), channel_id=1, source_target_pairs={{0,2},{1,3},{2,4},{3,5},{4,6},{5,7},{6,8},{7,9},{8,10},{9,11},{10,... | collective-permute-start | bytes 491528 | tf_op jit(solution)/shard_map/ppermute | solution.py:31
  9.9 6.3 %collective-permute-start.3 = (bf16[64,1280]{1,0:T(8,128)(2,1)S(1)}, bf16[64,1280]{1,0:T(8,128)(2,1)S(1)}, u32[]{:S(2)}, u32[]{:S(2)}) collective-permute-start(bf16[64,1280]{1,0:T(8,128)(2,1)S(1)} %collective-permute-done.1.refs_2_), channel_id=1, source_target_pairs={{0,14},{1,15},{2,0},{3,1},{4,2},{5,3},{6,4},{7,5},{8,6},{9,7},{10,... | collective-permute-start | bytes 491528 | tf_op jit(solution)/shard_map/ppermute | solution.py:31
  13.0 0.9 copy-start
  16.2 20.1 %collective-permute-start.10 = (bf16[256,1280]{1,0:T(8,128)(2,1)S(1)}, bf16[256,1280]{1,0:T(8,128)(2,1)S(1)}, u32[]{:S(2)}, u32[]{:S(2)}) collective-permute-start(bf16[256,1280]{1,0:T(8,128)(2,1)S(1)} %shard_map.49.refs_8_), channel_id=1, source_target_pairs={{0,64},{1,17},{2,66},{3,19},{4,68},{5,21},{6,70},{7,23},{8,72},{9,... | collective-permute-start | bytes 1966088 | tf_op jit(solution)/shard_map/ppermute | solution.py:40
  17.7 18.6 %collective-permute-start.11 = (bf16[256,1280]{1,0:T(8,128)(2,1)S(1)}, bf16[256,1280]{1,0:T(8,128)(2,1)S(1)}, u32[]{:S(2)}, u32[]{:S(2)}) collective-permute-start(bf16[256,1280]{1,0:T(8,128)(2,1)S(1)} %shard_map.49.refs_8_), channel_id=1, source_target_pairs={{0,192},{1,49},{2,194},{3,51},{4,196},{5,53},{6,198},{7,55},{8,200... | collective-permute-start | bytes 1966088 | tf_op jit(solution)/shard_map/ppermute | solution.py:40
  19.4 16.9 %collective-permute-start.12 = (bf16[256,1280]{1,0:T(8,128)(2,1)S(1)}, bf16[256,1280]{1,0:T(8,128)(2,1)S(1)}, u32[]{:S(2)}, u32[]{:S(2)}) collective-permute-start(bf16[256,1280]{1,0:T(8,128)(2,1)S(1)} %shard_map.49.refs_8_), channel_id=1, source_target_pairs={{0,128},{1,33},{2,130},{3,35},{4,132},{5,37},{6,134},{7,39},{8,136... | collective-permute-start | bytes 1966088 | tf_op jit(solution)/shard_map/ppermute | solution.py:40
  21.3 6.1 %collective-permute-start.7 = (bf16[64,1280]{1,0:T(8,128)(2,1)S(1)}, bf16[64,1280]{1,0:T(8,128)(2,1)S(1)}, u32[]{:S(2)}, u32[]{:S(2)}) collective-permute-start(bf16[64,1280]{1,0:T(8,128)(2,1)S(1)} %collective-permute-done.2.refs_3_), channel_id=1, source_target_pairs={{0,2},{1,3},{2,4},{3,5},{4,6},{5,7},{6,8},{7,9},{8,10},{9,11},{10,... | collective-permute-start | bytes 491528 | tf_op jit(solution)/shard_map/ppermute | solution.py:31
  24.5 6.5 %collective-permute-start.8 = (bf16[64,1280]{1,0:T(8,128)(2,1)S(1)}, bf16[64,1280]{1,0:T(8,128)(2,1)S(1)}, u32[]{:S(2)}, u32[]{:S(2)}) collective-permute-start(bf16[64,1280]{1,0:T(8,128)(2,1)S(1)} %collective-permute-done.3.refs_4_), channel_id=1, source_target_pairs={{0,14},{1,15},{2,0},{3,1},{4,2},{5,3},{6,4},{7,5},{8,6},{9,7},{10,... | collective-permute-start | bytes 491528 | tf_op jit(solution)/shard_map/ppermute | solution.py:31
  31.0 5.3 %collective-permute-start.9 = (bf16[64,1280]{1,0:T(8,128)(2,1)S(1)}, bf16[64,1280]{1,0:T(8,128)(2,1)S(1)}, u32[]{:S(2)}, u32[]{:S(2)}) collective-permute-start(bf16[64,1280]{1,0:T(8,128)(2,1)S(1)} %collective-permute-done.7.refs_5_), channel_id=1, source_target_pairs={{0,2},{1,3},{2,4},{3,5},{4,6},{5,7},{6,8},{7,9},{8,10},{9,11},{10,... | collective-permute-start | bytes 491528 | tf_op jit(solution)/shard_map/ppermute | solution.py:31
  36.3 5.1 %collective-permute-start.13 = (bf16[256,1280]{1,0:T(8,128)(2,1)S(1)}, bf16[256,1280]{1,0:T(8,128)(2,1)S(1)}, u32[]{:S(2)}, u32[]{:S(2)}) collective-permute-start(bf16[256,1280]{1,0:T(8,128)(2,1)S(1)} %shard_map.49.refs_8_), channel_id=1, source_target_pairs={{0,1},{1,0},{2,3},{3,2},{4,5},{5,4},{6,7},{7,6},{8,9},{9,8},{10,11... | collective-permute-start | bytes 1966088 | tf_op jit(solution)/shard_map/ppermute | solution.py:54
  36.4 5.0 %collective-permute-start.14 = (bf16[256,1280]{1,0:T(8,128)(2,1)S(1)}, bf16[256,1280]{1,0:T(8,128)(2,1)S(1)}, u32[]{:S(2)}, u32[]{:S(2)}) collective-permute-start(bf16[256,1280]{1,0:T(8,128)(2,1)S(1)} %collective-permute-done.10.refs_9_), channel_id=1, source_target_pairs={{0,1},{1,0},{2,3},{3,2},{4,5},{5,4},{6,7},{7,6},{8,9},{9,8},{10,11... | collective-permute-start | bytes 1966088 | tf_op jit(solution)/shard_map/ppermute | solution.py:54
  36.9 4.5 %collective-permute-start.15 = (bf16[256,1280]{1,0:T(8,128)(2,1)S(1)}, bf16[256,1280]{1,0:T(8,128)(2,1)S(1)}, u32[]{:S(2)}, u32[]{:S(2)}) collective-permute-start(bf16[256,1280]{1,0:T(8,128)(2,1)S(1)} %collective-permute-done.11.refs_10_), channel_id=1, source_target_pairs={{0,1},{1,0},{2,3},{3,2},{4,5},{5,4},{6,7},{7,6},{8,9},{9,8},{10,11... | collective-permute-start | bytes 1966088 | tf_op jit(solution)/shard_map/ppermute | solution.py:54
  37.0 4.4 %collective-permute-start.16 = (bf16[256,1280]{1,0:T(8,128)(2,1)S(1)}, bf16[256,1280]{1,0:T(8,128)(2,1)S(1)}, u32[]{:S(2)}, u32[]{:S(2)}) collective-permute-start(bf16[256,1280]{1,0:T(8,128)(2,1)S(1)} %collective-permute-done.12.refs_11_), channel_id=1, source_target_pairs={{0,1},{1,0},{2,3},{3,2},{4,5},{5,4},{6,7},{7,6},{8,9},{9,8},{10,11... | collective-permute-start | bytes 1966088 | tf_op jit(solution)/shard_map/ppermute | solution.py:54
  37.5 0.9 copy-start.1
  44.7 3.7 %collective-permute-start.17 = (f32[1,512]{1,0:T(1,128)S(1)}, f32[1,512]{1,0:T(1,128)S(1)}, u32[]{:S(2)}, u32[]{:S(2)}) collective-permute-start(f32[1,512]{1,0:T(1,128)S(1)} %get-tuple-element.70), channel_id=1, source_target_pairs={{0,2},{1,3},{2,0},{3,1},{4,6},{5,7},{6,4},{7,5},{8,10},{9,11},{10,... | collective-permute-start | bytes 6152 | tf_op jit(solution)/shard_map/ppermute | solution.py:54
  46.7 33.2 %collective-permute-start.31 = (bf16[512,1280]{1,0:T(8,128)(2,1)S(1)}, bf16[512,1280]{1,0:T(8,128)(2,1)S(1)}, u32[]{:S(2)}, u32[]{:S(2)}) collective-permute-start(bf16[512,1280]{1,0:T(8,128)(2,1)S(1)} %get-tuple-element.65.refs_4_.refs_2_), channel_id=1, source_target_pairs={{0,1},{1,0},{2,3},{3,2},{4,5},{5,4},{6,7},{7,6},{8,9},{9,8},{10,11... | collective-permute-start | bytes 3932168 | tf_op jit(solution)/shard_map/ppermute | solution.py:54
  46.7 7.2 %collective-permute-start.20 = (f32[1,2176]{1,0:T(1,128)S(1)}, f32[1,2176]{1,0:T(1,128)S(1)}, u32[]{:S(2)}, u32[]{:S(2)}) collective-permute-start(f32[1,2176]{1,0:T(1,128)S(1)} %get-tuple-element.71), channel_id=1, source_target_pairs={{0,1},{1,0},{2,3},{3,2},{4,5},{5,4},{6,7},{7,6},{8,9},{9,8},{10,11... | collective-permute-start | bytes 26120 | tf_op jit(solution)/shard_map/ppermute | solution.py:54
  48.3 9.8 %collective-permute-start.18 = (f32[1,512]{1,0:T(1,128)S(1)}, f32[1,512]{1,0:T(1,128)S(1)}, u32[]{:S(2)}, u32[]{:S(2)}) collective-permute-start(f32[1,512]{1,0:T(1,128)S(1)} %log_add_fusion.2), channel_id=1, source_target_pairs={{0,4},{1,5},{2,6},{3,7},{4,0},{5,1},{6,2},{7,3},{8,12},{9,13},{10,... | collective-permute-start | bytes 6152 | tf_op jit(solution)/shard_map/ppermute | solution.py:54
  54.0 6.0 %collective-permute-start.23 = (f32[1,2176]{1,0:T(1,128)S(1)}, f32[1,2176]{1,0:T(1,128)S(1)}, u32[]{:S(2)}, u32[]{:S(2)}) collective-permute-start(f32[1,2176]{1,0:T(1,128)S(1)} %add_select_fusion.2), channel_id=1, source_target_pairs={{0,32},{1,33},{2,34},{3,35},{4,36},{5,37},{6,38},{7,39},{8,40},{9,... | collective-permute-start | bytes 26120 | tf_op jit(solution)/shard_map/ppermute | solution.py:77
  56.1 3.8 %collective-permute-start.22 = (f32[1,2176]{1,0:T(1,128)S(1)}, f32[1,2176]{1,0:T(1,128)S(1)}, u32[]{:S(2)}, u32[]{:S(2)}) collective-permute-start(f32[1,2176]{1,0:T(1,128)S(1)} %add_select_fusion.2), channel_id=1, source_target_pairs={{0,48},{1,49},{2,50},{3,51},{4,52},{5,53},{6,54},{7,55},{8,56},{9,... | collective-permute-start | bytes 26120 | tf_op jit(solution)/shard_map/ppermute | solution.py:77
  57.4 4.9 %collective-permute-start.21 = (f32[1,2176]{1,0:T(1,128)S(1)}, f32[1,2176]{1,0:T(1,128)S(1)}, u32[]{:S(2)}, u32[]{:S(2)}) collective-permute-start(f32[1,2176]{1,0:T(1,128)S(1)} %add_select_fusion.2), channel_id=1, source_target_pairs={{0,16},{1,17},{2,18},{3,19},{4,20},{5,21},{6,22},{7,23},{8,24},{9,... | collective-permute-start | bytes 26120 | tf_op jit(solution)/shard_map/ppermute | solution.py:77
  58.2 8.3 %collective-permute-start.19 = (f32[1,512]{1,0:T(1,128)S(1)}, f32[1,512]{1,0:T(1,128)S(1)}, u32[]{:S(2)}, u32[]{:S(2)}) collective-permute-start(f32[1,512]{1,0:T(1,128)S(1)} %log_add_fusion.1), channel_id=1, source_target_pairs={{0,8},{1,9},{2,10},{3,11},{4,12},{5,13},{6,14},{7,15},{8,0},{9,1},... | collective-permute-start | bytes 6152 | tf_op jit(solution)/shard_map/ppermute | solution.py:54
  62.3 5.2 %collective-permute-start.26 = (f32[1,2176]{1,0:T(1,128)S(1)}, f32[1,2176]{1,0:T(1,128)S(1)}, u32[]{:S(2)}, u32[]{:S(2)}) collective-permute-start(f32[1,2176]{1,0:T(1,128)S(1)} %add_select_fusion.1), channel_id=1, source_target_pairs={{0,128},{1,129},{2,130},{3,131},{4,132},{5,133},{6,134},{7,135},{8... | collective-permute-start | bytes 26120 | tf_op jit(solution)/shard_map/ppermute | solution.py:77
  63.2 4.6 %collective-permute-start.25 = (f32[1,2176]{1,0:T(1,128)S(1)}, f32[1,2176]{1,0:T(1,128)S(1)}, u32[]{:S(2)}, u32[]{:S(2)}) collective-permute-start(f32[1,2176]{1,0:T(1,128)S(1)} %add_select_fusion.1), channel_id=1, source_target_pairs={{0,192},{1,193},{2,194},{3,195},{4,196},{5,197},{6,198},{7,199},{8... | collective-permute-start | bytes 26120 | tf_op jit(solution)/shard_map/ppermute | solution.py:77
  66.5 4.9 %collective-permute-start.24 = (f32[1,2176]{1,0:T(1,128)S(1)}, f32[1,2176]{1,0:T(1,128)S(1)}, u32[]{:S(2)}, u32[]{:S(2)}) collective-permute-start(f32[1,2176]{1,0:T(1,128)S(1)} %add_select_fusion.1), channel_id=1, source_target_pairs={{0,64},{1,65},{2,66},{3,67},{4,68},{5,69},{6,70},{7,71},{8,72},{9,... | collective-permute-start | bytes 26120 | tf_op jit(solution)/shard_map/ppermute | solution.py:77
  73.1 5.0 %collective-permute-start.27 = (bf16[512,1024]{1,0:T(8,128)(2,1)S(1)}, bf16[512,1024]{1,0:T(8,128)(2,1)S(1)}, u32[]{:S(2)}, u32[]{:S(2)}) collective-permute-start(bf16[512,1024]{1,0:T(8,128)(2,1)S(1)} %get-tuple-element.84.refs_1_), channel_id=1, source_target_pairs={{0,1},{1,0},{2,3},{3,2},{4,5},{5,4},{6,7},{7,6},{8,9},{9,8},{10,11... | collective-permute-start | bytes 3145736 | tf_op jit(solution)/shard_map/ppermute | solution.py:54
  73.1 6.8 %collective-permute-start.32 = (f32[1,128]{1,0:T(1,128)S(1)}, f32[1,128]{1,0:T(1,128)S(1)}, u32[]{:S(2)}, u32[]{:S(2)}) collective-permute-start(f32[1,128]{1,0:T(1,128)S(1)} %get-tuple-element.82.refs_4_), channel_id=1, source_target_pairs={{0,1},{1,0},{2,3},{3,2},{4,5},{5,4},{6,7},{7,6},{8,9},{9,8},{10,11... | collective-permute-start | bytes 1544 | tf_op jit(solution)/shard_map/ppermute | solution.py:54
  76.4 13.6 %collective-permute-start.29 = (bf16[1296,128]{1,0:T(8,128)(2,1)S(1)}, bf16[1296,128]{1,0:T(8,128)(2,1)S(1)}, u32[]{:S(2)}, u32[]{:S(2)}) collective-permute-start(bf16[1296,128]{1,0:T(8,128)(2,1)S(1)} %get-tuple-element.79), channel_id=1, source_target_pairs={{0,14},{1,15},{2,0},{3,1},{4,2},{5,3},{6,4},{7,5},{8,6},{9,7},{10,... | collective-permute-start | bytes 995336 | tf_op jit(solution)/shard_map/ppermute | solution.py:31
  76.9 11.1 %collective-permute-start.30 = (bf16[656,128]{1,0:T(8,128)(2,1)S(1)}, bf16[656,128]{1,0:T(8,128)(2,1)S(1)}, u32[]{:S(2)}, u32[]{:S(2)}) collective-permute-start(bf16[656,128]{1,0:T(8,128)(2,1)S(1)} %get-tuple-element.80), channel_id=1, source_target_pairs={{0,4},{1,13},{2,6},{3,15},{4,8},{5,1},{6,10},{7,3},{8,12},{9,5},{1... | collective-permute-start | bytes 503816 | tf_op jit(solution)/shard_map/ppermute | solution.py:45
  78.1 12.9 %collective-permute-start.28 = (bf16[1296,128]{1,0:T(8,128)(2,1)S(1)}, bf16[1296,128]{1,0:T(8,128)(2,1)S(1)}, u32[]{:S(2)}, u32[]{:S(2)}) collective-permute-start(bf16[1296,128]{1,0:T(8,128)(2,1)S(1)} %get-tuple-element.78), channel_id=1, source_target_pairs={{0,2},{1,3},{2,4},{3,5},{4,6},{5,7},{6,8},{7,9},{8,10},{9,11},{10,... | collective-permute-start | bytes 995336 | tf_op jit(solution)/shard_map/ppermute | solution.py:31
  83.8 19.0 %collective-permute-start.35 = (bf16[2576,128]{1,0:T(8,128)(2,1)S(1)}, bf16[2576,128]{1,0:T(8,128)(2,1)S(1)}, u32[]{:S(2)}, u32[]{:S(2)}) collective-permute-start(bf16[2576,128]{1,0:T(8,128)(2,1)S(1)} %get-tuple-element.92), channel_id=1, source_target_pairs={{0,16},{1,65},{2,18},{3,67},{4,20},{5,69},{6,22},{7,71},{8,24},{9,... | collective-permute-start | bytes 1978376 | tf_op jit(solution)/shard_map/ppermute | solution.py:40
  83.9 18.9 %collective-permute-start.36 = (bf16[2576,128]{1,0:T(8,128)(2,1)S(1)}, bf16[2576,128]{1,0:T(8,128)(2,1)S(1)}, u32[]{:S(2)}, u32[]{:S(2)}) collective-permute-start(bf16[2576,128]{1,0:T(8,128)(2,1)S(1)} %get-tuple-element.93), channel_id=1, source_target_pairs={{0,32},{1,129},{2,34},{3,131},{4,36},{5,133},{6,38},{7,135},{8,40}... | collective-permute-start | bytes 1978376 | tf_op jit(solution)/shard_map/ppermute | solution.py:40
  88.0 15.8 %collective-permute-start.37 = (bf16[2576,128]{1,0:T(8,128)(2,1)S(1)}, bf16[2576,128]{1,0:T(8,128)(2,1)S(1)}, u32[]{:S(2)}, u32[]{:S(2)}) collective-permute-start(bf16[2576,128]{1,0:T(8,128)(2,1)S(1)} %get-tuple-element.94), channel_id=1, source_target_pairs={{0,48},{1,193},{2,50},{3,195},{4,52},{5,197},{6,54},{7,199},{8,56}... | collective-permute-start | bytes 1978376 | tf_op jit(solution)/shard_map/ppermute | solution.py:40
  91.1 16.3 %collective-permute-start.33 = (bf16[656,128]{1,0:T(8,128)(2,1)S(1)}, bf16[656,128]{1,0:T(8,128)(2,1)S(1)}, u32[]{:S(2)}, u32[]{:S(2)}) collective-permute-start(bf16[656,128]{1,0:T(8,128)(2,1)S(1)} %get-tuple-element.88), channel_id=1, source_target_pairs={{0,4},{1,5},{2,6},{3,7},{4,8},{5,9},{6,10},{7,11},{8,12},{9,13},{1... | collective-permute-start | bytes 503816 | tf_op jit(solution)/shard_map/ppermute | solution.py:31
  93.1 14.3 %collective-permute-start.34 = (bf16[656,128]{1,0:T(8,128)(2,1)S(1)}, bf16[656,128]{1,0:T(8,128)(2,1)S(1)}, u32[]{:S(2)}, u32[]{:S(2)}) collective-permute-start(bf16[656,128]{1,0:T(8,128)(2,1)S(1)} %get-tuple-element.89), channel_id=1, source_target_pairs={{0,12},{1,13},{2,14},{3,15},{4,0},{5,1},{6,2},{7,3},{8,4},{9,5},{1... | collective-permute-start | bytes 503816 | tf_op jit(solution)/shard_map/ppermute | solution.py:31
  104.1 8.4 %collective-permute-start.38 = (bf16[656,128]{1,0:T(8,128)(2,1)S(1)}, bf16[656,128]{1,0:T(8,128)(2,1)S(1)}, u32[]{:S(2)}, u32[]{:S(2)}) collective-permute-start(bf16[656,128]{1,0:T(8,128)(2,1)S(1)} %get-tuple-element.97), channel_id=1, source_target_pairs={{0,64},{1,17},{2,66},{3,19},{4,68},{5,21},{6,70},{7,23},{8,72},{9,... | collective-permute-start | bytes 503816 | tf_op jit(solution)/shard_map/ppermute | solution.py:40
  104.2 8.4 %collective-permute-start.39 = (bf16[656,128]{1,0:T(8,128)(2,1)S(1)}, bf16[656,128]{1,0:T(8,128)(2,1)S(1)}, u32[]{:S(2)}, u32[]{:S(2)}) collective-permute-start(bf16[656,128]{1,0:T(8,128)(2,1)S(1)} %get-tuple-element.98), channel_id=1, source_target_pairs={{0,128},{1,33},{2,130},{3,35},{4,132},{5,37},{6,134},{7,39},{8,136... | collective-permute-start | bytes 503816 | tf_op jit(solution)/shard_map/ppermute | solution.py:40
  105.6 7.8 %collective-permute-start.40 = (bf16[656,128]{1,0:T(8,128)(2,1)S(1)}, bf16[656,128]{1,0:T(8,128)(2,1)S(1)}, u32[]{:S(2)}, u32[]{:S(2)}) collective-permute-start(bf16[656,128]{1,0:T(8,128)(2,1)S(1)} %get-tuple-element.99), channel_id=1, source_target_pairs={{0,192},{1,49},{2,194},{3,51},{4,196},{5,53},{6,198},{7,55},{8,200... | collective-permute-start | bytes 503816 | tf_op jit(solution)/shard_map/ppermute | solution.py:40

commit v4 on v3

--- a/solution.py
+++ b/solution.py
@@ -152,29 +152,30 @@
 def half_scores(scale, img, txt, scores, cols_out, row_top, row_sum):
     chunk = 512
     row_top[...] = jnp.full((ROWS, 128), -jnp.inf, F32)
-
-    @pl.loop(0, PLANE // chunk)
-    def _(i):
-        cols = pl.ds(pl.multiple_of(i * chunk, chunk), chunk)
-        s = scale * lax.dot_general(
+    row_sum[...] = jnp.zeros((ROWS, 128), F32)
+
+    def multiply(i):
+        cols = slice(i * chunk, (i + 1) * chunk)
+        scores[:, cols] = scale * lax.dot_general(
             img[...], txt[cols, :], (((1,), (1,)), ((), ())), preferred_element_type=F32
         )
-        scores[:, cols] = s
-        tops = row_top[...]
-        for j in range(chunk // 128):
-            tops = jnp.maximum(tops, s[:, j * 128 : (j + 1) * 128])
+
+    def reduce(i):
+        cols = slice(i * chunk, (i + 1) * chunk)
+        s = scores[:, cols]
+        lanes = [s[:, j * 128 : (j + 1) * 128] for j in range(chunk // 128)]
+        before = row_top[...]
+        tops = functools.reduce(jnp.maximum, lanes, before)
         row_top[...] = tops
+        row_sum[...] = row_sum[...] * jnp.exp(before - tops) + sum(jnp.exp(part - tops) for part in lanes)
         top = jnp.max(s, axis=0, keepdims=True)
         cols_out[:, cols] = top + jnp.log(jnp.sum(jnp.exp(s - top), axis=0, keepdims=True))
 
-    row_top[...] = jnp.broadcast_to(jnp.max(row_top[...], axis=1, keepdims=True), (ROWS, 128))
-    row_sum[...] = jnp.zeros((ROWS, 128), F32)
-
-    @pl.loop(0, PLANE // 256)
-    def _(i):
-        for j in range(2):
-            cols = pl.ds(pl.multiple_of(i * 256 + j * 128, 128), 128)
-            row_sum[...] += jnp.exp(scores[:, cols] - row_top[...])
+    multiply(0)
+    for i in range(1, PLANE // chunk):
+        reduce(i - 1)
+        multiply(i)
+    reduce(PLANE // chunk - 1)
 
 
 def own_scores_kernel(scale, at, *refs):
@@ -193,10 +194,10 @@
     x, y, z, c = at
     place_text(at, 1 - c, text_in, txt)
     half_scores(scale, img, txt, scores, cols_other, row_top, row_sum)
-    top = jnp.maximum(row_top[...], top_own[...])
+    top = jnp.max(jnp.maximum(row_top[...], top_own[...]), axis=1, keepdims=True)
     total = row_sum[...] * jnp.exp(row_top[...] - top) + sum_own[...] * jnp.exp(top_own[...] - top)
     row = top + jnp.log(jnp.sum(total, axis=1, keepdims=True))
-    row_out[...] = jnp.transpose(row)[0:1, :]
+    row_out[...] = jnp.transpose(jnp.broadcast_to(row, (ROWS, 128)))[0:1, :]
     col_out[:, pl.ds(pl.multiple_of(c * PLANE, PLANE), PLANE)] = cols_own[...]
     col_out[:, pl.ds(pl.multiple_of((1 - c) * PLANE, PLANE), PLANE)] = cols_other[...]
     col_out[:, COLS:] = jnp.zeros((1, 128), F32)
@@ -393,10 +394,11 @@
     far = [shift_plane(line, d, False) for d in STEPS[1:]]
     up, down = lax.optimization_barrier((shift_z(up, 1), shift_z(down, -1)))
     image_in += [up, down]
-    last, line, *far = lax.optimization_barrier((shift_z(up, 1), line, *far))
+    line_sent, up = lax.optimization_barrier((line, up))
+    last, *far = lax.optimization_barrier((shift_z(up, 1), *far))
     image_in.append(last)
     text_in = [line, *far]
-    text_swapped = [swap_core(part) for part in text_in]
+    text_swapped = [swap_core(part) for part in (line_sent, *far)]
 
     tile = 2 * ROWS * COLS * embed
     half_scores_out = ((ROWS, PLANE), F32)
@@ -472,6 +474,7 @@
     here, up_two, down_two = image_part(
         ((0, 0, None), (2, 1, None), (-2, 2, None)), [((SHARD, embed), F32)] * 3, other, far
     )
+    up, down, here = lax.optimization_barrier((up, down, here))
     up, down = shift_z(up, 1), shift_z(down, -1)
     sent = [shift_plane(part, d, True) for d, part in enumerate(sent, 1)]
     up, down, here, q = call(

time: 114 us -> 111 us (0.974); the launches traced: 114 us -> 109 us
  waiting for transfers between devices: 38.5 us -> 34.6 us
  Pallas kernels: 18.1 us -> 16.6 us
    ppermute x12, waiting for transfers between devices: 15.3 us -> 3.22 us  [shift_plane(): return lax.ppermute(value, AXES, pairs)]
    ppermute x11, waiting for transfers between devices: 12.8 us -> 21.3 us  [shift_z(): return lax.ppermute(value, AXES, pairs)]
    ppermute x12, starting transfers between devices: 15.6 us -> 17.8 us  [shift_plane(): return lax.ppermute(value, AXES, pairs)]
    pallas_call x9, Pallas kernels: 17.9 us -> 16.4 us  [call(): pl.pallas_call(lambda *refs: kernel(position(), *refs), out_shape=[jax.Sh...]
  transfers between devices with their start and end apart: 41 -> 41, of which waited for: 17 -> 18; matrix products, arithmetic and copies ran while one was open for 0% -> 0% of each run, Pallas kernels for 12% -> 12%
where the time goes in v4:
time: 111 us; the launch traced here: 109 us
  starting transfers between devices  55.4 us (50%)
  waiting for transfers between devices  34.6 us (31%)
  Pallas kernels  16.6 us (15%)
  local copies, waits for them, and re-layouts  1.83 us (2%)
    ppermute x11, waiting for transfers between devices, shift_z(): return lax.ppermute(value, AXES, pairs)  21.3 us
    ppermute x12, starting transfers between devices, shift_plane(): return lax.ppermute(value, AXES, pairs)  17.8 us
    ppermute x11, starting transfers between devices, shift_z(): return lax.ppermute(value, AXES, pairs)  17.8 us
    pallas_call x9, Pallas kernels, call(): pl.pallas_call(lambda *refs: kernel(position(), *refs), out_shape=[jax.Sh...  16.4 us
    ppermute x11, starting transfers between devices, swap(): return lax.ppermute(value, AXES, pairs)  11.3 us
    ppermute x6, starting transfers between devices, shift_one(): return lax.ppermute(value, AXES, pairs)  8.38 us
    ppermute x6, waiting for transfers between devices, shift_one(): return lax.ppermute(value, AXES, pairs)  7.17 us
    ppermute x12, waiting for transfers between devices, shift_plane(): return lax.ppermute(value, AXES, pairs)  3.22 us
  transfers between devices with their start and end apart: 41, of which 18 were waited for; matrix products, arithmetic and copies ran while one was open for 0% of the time, Pallas kernels for 12%

profile of v4, /device:TPU:32, one launch (start us, length us, event | category | flops | bytes accessed | tf_op | source)
XLA Modules:
  0.0 109.5 jit_solution(9210317814569226516)
XLA Ops:
  0.6 2.0 %collective-permute-start = (bf16[64,1280]{1,0:T(8,128)(2,1)}, bf16[64,1280]{1,0:T(8,128)(2,1)S(1)}, u32[]{:S(2)}, u32[]{:S(2)}) collective-permute-start(bf16[64,1280]{1,0:T(8,128)(2,1)} %refs_0_.1), channel_id=1, source_target_pairs={{0,2},{1,3},{2,4},{3,5},{4,6},{5,7},{6,8},{7,9},{8,10},{9,11},{10,... | collective-permute-start | bytes 491528 | tf_op jit(solution)/shard_map/ppermute | solution.py:31
  2.7 1.6 %collective-permute-start.4 = (bf16[64,1280]{1,0:T(8,128)(2,1)}, bf16[64,1280]{1,0:T(8,128)(2,1)S(1)}, u32[]{:S(2)}, u32[]{:S(2)}) collective-permute-start(bf16[64,1280]{1,0:T(8,128)(2,1)} %text.1), channel_id=1, source_target_pairs={{0,16},{1,65},{2,18},{3,67},{4,20},{5,69},{6,22},{7,71},{8,24},{9,... | collective-permute-start | bytes 491528 | tf_op jit(solution)/shard_map/ppermute | solution.py:40
  4.3 1.7 %collective-permute-start.5 = (bf16[64,1280]{1,0:T(8,128)(2,1)}, bf16[64,1280]{1,0:T(8,128)(2,1)S(1)}, u32[]{:S(2)}, u32[]{:S(2)}) collective-permute-start(bf16[64,1280]{1,0:T(8,128)(2,1)} %text.1), channel_id=1, source_target_pairs={{0,48},{1,193},{2,50},{3,195},{4,52},{5,197},{6,54},{7,199},{8,56}... | collective-permute-start | bytes 491528 | tf_op jit(solution)/shard_map/ppermute | solution.py:40
  6.0 2.0 %collective-permute-start.6 = (bf16[64,1280]{1,0:T(8,128)(2,1)}, bf16[64,1280]{1,0:T(8,128)(2,1)S(1)}, u32[]{:S(2)}, u32[]{:S(2)}) collective-permute-start(bf16[64,1280]{1,0:T(8,128)(2,1)} %text.1), channel_id=1, source_target_pairs={{0,32},{1,129},{2,34},{3,131},{4,36},{5,133},{6,38},{7,135},{8,40}... | collective-permute-start | bytes 491528 | tf_op jit(solution)/shard_map/ppermute | solution.py:40
  8.0 1.9 %collective-permute-start.2 = (bf16[64,1280]{1,0:T(8,128)(2,1)S(1)}, bf16[64,1280]{1,0:T(8,128)(2,1)S(1)}, u32[]{:S(2)}, u32[]{:S(2)}) collective-permute-start(bf16[64,1280]{1,0:T(8,128)(2,1)S(1)} %collective-permute-done.refs_1_), channel_id=1, source_target_pairs={{0,2},{1,3},{2,4},{3,5},{4,6},{5,7},{6,8},{7,9},{8,10},{9,11},{10,... | collective-permute-start | bytes 491528 | tf_op jit(solution)/shard_map/ppermute | solution.py:31
  9.9 2.2 %collective-permute-start.3 = (bf16[64,1280]{1,0:T(8,128)(2,1)S(1)}, bf16[64,1280]{1,0:T(8,128)(2,1)S(1)}, u32[]{:S(2)}, u32[]{:S(2)}) collective-permute-start(bf16[64,1280]{1,0:T(8,128)(2,1)S(1)} %collective-permute-done.1.refs_2_), channel_id=1, source_target_pairs={{0,14},{1,15},{2,0},{3,1},{4,2},{5,3},{6,4},{7,5},{8,6},{9,7},{10,... | collective-permute-start | bytes 491528 | tf_op jit(solution)/shard_map/ppermute | solution.py:31
  12.1 0.9 collective-permute-done.6.refs_2_
  13.0 0.9 copy-done
  14.1 1.1 %collective-permute-done.2.refs_3_ = bf16[64,1280]{1,0:T(8,128)(2,1)S(1)} collective-permute-done((bf16[64,1280]{1,0:T(8,128)(2,1)S(1)}, bf16[64,1280]{1,0:T(8,128)(2,1)S(1)}, u32[]{:S(2)}, u32[]{:S(2)}) %collective-permute-start.2) | collective-permute-done | bytes 163872 | tf_op jit(solution)/shard_map/ppermute | solution.py:31
  15.3 0.9 collective-permute-done.3.refs_4_
  16.2 1.5 %collective-permute-start.10 = (bf16[256,1280]{1,0:T(8,128)(2,1)S(1)}, bf16[256,1280]{1,0:T(8,128)(2,1)S(1)}, u32[]{:S(2)}, u32[]{:S(2)}) collective-permute-start(bf16[256,1280]{1,0:T(8,128)(2,1)S(1)} %shard_map.49.refs_8_), channel_id=1, source_target_pairs={{0,64},{1,17},{2,66},{3,19},{4,68},{5,21},{6,70},{7,23},{8,72},{9,... | collective-permute-start | bytes 1966088 | tf_op jit(solution)/shard_map/ppermute | solution.py:40
  17.7 1.7 %collective-permute-start.11 = (bf16[256,1280]{1,0:T(8,128)(2,1)S(1)}, bf16[256,1280]{1,0:T(8,128)(2,1)S(1)}, u32[]{:S(2)}, u32[]{:S(2)}) collective-permute-start(bf16[256,1280]{1,0:T(8,128)(2,1)S(1)} %shard_map.49.refs_8_), channel_id=1, source_target_pairs={{0,192},{1,49},{2,194},{3,51},{4,196},{5,53},{6,198},{7,55},{8,200... | collective-permute-start | bytes 1966088 | tf_op jit(solution)/shard_map/ppermute | solution.py:40
  19.4 1.8 %collective-permute-start.12 = (bf16[256,1280]{1,0:T(8,128)(2,1)S(1)}, bf16[256,1280]{1,0:T(8,128)(2,1)S(1)}, u32[]{:S(2)}, u32[]{:S(2)}) collective-permute-start(bf16[256,1280]{1,0:T(8,128)(2,1)S(1)} %shard_map.49.refs_8_), channel_id=1, source_target_pairs={{0,128},{1,33},{2,130},{3,35},{4,132},{5,37},{6,134},{7,39},{8,136... | collective-permute-start | bytes 1966088 | tf_op jit(solution)/shard_map/ppermute | solution.py:40
  21.3 3.2 %collective-permute-start.7 = (bf16[64,1280]{1,0:T(8,128)(2,1)S(1)}, bf16[64,1280]{1,0:T(8,128)(2,1)S(1)}, u32[]{:S(2)}, u32[]{:S(2)}) collective-permute-start(bf16[64,1280]{1,0:T(8,128)(2,1)S(1)} %collective-permute-done.2.refs_3_), channel_id=1, source_target_pairs={{0,2},{1,3},{2,4},{3,5},{4,6},{5,7},{6,8},{7,9},{8,10},{9,11},{10,... | collective-permute-start | bytes 491528 | tf_op jit(solution)/shard_map/ppermute | solution.py:31
  24.5 2.8 %collective-permute-done.7.refs_5_ = bf16[64,1280]{1,0:T(8,128)(2,1)S(1)} collective-permute-done((bf16[64,1280]{1,0:T(8,128)(2,1)S(1)}, bf16[64,1280]{1,0:T(8,128)(2,1)S(1)}, u32[]{:S(2)}, u32[]{:S(2)}) %collective-permute-start.7) | collective-permute-done | bytes 163872 | tf_op jit(solution)/shard_map/ppermute | solution.py:31
  27.3 3.7 %collective-permute-done.8.refs_6_ = bf16[64,1280]{1,0:T(8,128)(2,1)S(1)} collective-permute-done((bf16[64,1280]{1,0:T(8,128)(2,1)S(1)}, bf16[64,1280]{1,0:T(8,128)(2,1)S(1)}, u32[]{:S(2)}, u32[]{:S(2)}) %collective-permute-start.8) | collective-permute-done | bytes 163872 | tf_op jit(solution)/shard_map/ppermute | solution.py:31
  31.0 2.0 %collective-permute-start.9 = (bf16[64,1280]{1,0:T(8,128)(2,1)S(1)}, bf16[64,1280]{1,0:T(8,128)(2,1)S(1)}, u32[]{:S(2)}, u32[]{:S(2)}) collective-permute-start(bf16[64,1280]{1,0:T(8,128)(2,1)S(1)} %collective-permute-done.7.refs_5_), channel_id=1, source_target_pairs={{0,2},{1,3},{2,4},{3,5},{4,6},{5,7},{6,8},{7,9},{8,10},{9,11},{10,... | collective-permute-start | bytes 491528 | tf_op jit(solution)/shard_map/ppermute | solution.py:31
  33.0 3.3 %collective-permute-done.9.refs_7_ = bf16[64,1280]{1,0:T(8,128)(2,1)S(1)} collective-permute-done((bf16[64,1280]{1,0:T(8,128)(2,1)S(1)}, bf16[64,1280]{1,0:T(8,128)(2,1)S(1)}, u32[]{:S(2)}, u32[]{:S(2)}) %collective-permute-start.9) | collective-permute-done | bytes 163872 | tf_op jit(solution)/shard_map/ppermute | solution.py:31
  37.0 0.9 copy-done.1
  38.0 2.4 %shard_map.50 = (bf16[512,1280]{1,0:T(8,128)(2,1)S(1)}, bf16[1024,1280]{1,0:T(8,128)(2,1)S(1)}, f32[512,1024]{1,0:T(8,128)S(1)}, f32[1,1024]{1,0:T(1,128)S(1)}, ...) custom-call(bf16[64,1280]{1,0:T(8,128)(2,1)S(1)} %copy-done.1, bf16[64,1280]{1,0:T(8,128)(2,1)S(1)} %collective-permute-done.refs_1_, ...), custom_call_target="tpu_custom_call" | custom-call | flops 10737418240 | bytes 7340032 | tf_op jit(solution)/shard_map/pallas_call | solution.py:88
  40.4 2.4 %shard_map.51 = (bf16[1024,1280]{1,0:T(8,128)(2,1)S(1)}, f32[512,1024]{1,0:T(8,128)S(1)}, f32[1,512]{1,0:T(1,128)S(1)}, f32[1,2176]{1,0:T(1,128)S(1)}) custom-call(bf16[256,1280]{1,0:T(8,128)(2,1)S(1)} %collective-permute-done.13.refs_0_, bf16[256,1280]{1,0:T(8,128)(2,1)S(1)} %collective-permute-done.14.refs_1_, ...), custom_call_target="tpu_custom_call" | custom-call | flops 10737418240 | bytes 7340032 | tf_op jit(solution)/shard_map/pallas_call | solution.py:88
  42.8 2.1 %collective-permute-start.17 = (f32[1,512]{1,0:T(1,128)S(1)}, f32[1,512]{1,0:T(1,128)S(1)}, u32[]{:S(2)}, u32[]{:S(2)}) collective-permute-start(f32[1,512]{1,0:T(1,128)S(1)} %get-tuple-element.75), channel_id=1, source_target_pairs={{0,2},{1,3},{2,0},{3,1},{4,6},{5,7},{6,4},{7,5},{8,10},{9,11},{10,... | collective-permute-start | bytes 6152 | tf_op jit(solution)/shard_map/ppermute | solution.py:54
  45.4 1.1 %collective-permute-done.17 = f32[1,512]{1,0:T(1,128)S(1)} collective-permute-done((f32[1,512]{1,0:T(1,128)S(1)}, f32[1,512]{1,0:T(1,128)S(1)}, u32[]{:S(2)}, u32[]{:S(2)}) %collective-permute-start.17) | collective-permute-done | bytes 2080 | tf_op jit(solution)/shard_map/ppermute | solution.py:54
  46.5 5.6 %collective-permute-start.18 = (f32[1,512]{1,0:T(1,128)S(1)}, f32[1,512]{1,0:T(1,128)S(1)}, u32[]{:S(2)}, u32[]{:S(2)}) collective-permute-start(f32[1,512]{1,0:T(1,128)S(1)} %log_add_fusion.2), channel_id=1, source_target_pairs={{0,4},{1,5},{2,6},{3,7},{4,0},{5,1},{6,2},{7,3},{8,12},{9,13},{10,... | collective-permute-start | bytes 6152 | tf_op jit(solution)/shard_map/ppermute | solution.py:54
  52.1 2.2 %collective-permute-start.23 = (f32[1,2176]{1,0:T(1,128)S(1)}, f32[1,2176]{1,0:T(1,128)S(1)}, u32[]{:S(2)}, u32[]{:S(2)}) collective-permute-start(f32[1,2176]{1,0:T(1,128)S(1)} %add_select_fusion.2), channel_id=1, source_target_pairs={{0,32},{1,33},{2,34},{3,35},{4,36},{5,37},{6,38},{7,39},{8,40},{9,... | collective-permute-start | bytes 26120 | tf_op jit(solution)/shard_map/ppermute | solution.py:77
  54.3 1.3 %collective-permute-start.22 = (f32[1,2176]{1,0:T(1,128)S(1)}, f32[1,2176]{1,0:T(1,128)S(1)}, u32[]{:S(2)}, u32[]{:S(2)}) collective-permute-start(f32[1,2176]{1,0:T(1,128)S(1)} %add_select_fusion.2), channel_id=1, source_target_pairs={{0,48},{1,49},{2,50},{3,51},{4,52},{5,53},{6,54},{7,55},{8,56},{9,... | collective-permute-start | bytes 26120 | tf_op jit(solution)/shard_map/ppermute | solution.py:77
  56.3 1.7 %collective-permute-start.19 = (f32[1,512]{1,0:T(1,128)S(1)}, f32[1,512]{1,0:T(1,128)S(1)}, u32[]{:S(2)}, u32[]{:S(2)}) collective-permute-start(f32[1,512]{1,0:T(1,128)S(1)} %log_add_fusion.1), channel_id=1, source_target_pairs={{0,8},{1,9},{2,10},{3,11},{4,12},{5,13},{6,14},{7,15},{8,0},{9,1},... | collective-permute-start | bytes 6152 | tf_op jit(solution)/shard_map/ppermute | solution.py:54
  58.1 2.3 %collective-permute-done.21 = f32[1,2176]{1,0:T(1,128)S(1)} collective-permute-done((f32[1,2176]{1,0:T(1,128)S(1)}, f32[1,2176]{1,0:T(1,128)S(1)}, u32[]{:S(2)}, u32[]{:S(2)}) %collective-permute-start.21) | collective-permute-done | bytes 8736 | tf_op jit(solution)/shard_map/ppermute | solution.py:77
  60.5 0.9 collective-permute-start.26
  61.4 3.3 %collective-permute-start.25 = (f32[1,2176]{1,0:T(1,128)S(1)}, f32[1,2176]{1,0:T(1,128)S(1)}, u32[]{:S(2)}, u32[]{:S(2)}) collective-permute-start(f32[1,2176]{1,0:T(1,128)S(1)} %add_select_fusion.1), channel_id=1, source_target_pairs={{0,192},{1,193},{2,194},{3,195},{4,196},{5,197},{6,198},{7,199},{8... | collective-permute-start | bytes 26120 | tf_op jit(solution)/shard_map/ppermute | solution.py:77
  64.7 1.0 collective-permute-done.26
  66.0 3.5 %collective-permute-done.24 = f32[1,2176]{1,0:T(1,128)S(1)} collective-permute-done((f32[1,2176]{1,0:T(1,128)S(1)}, f32[1,2176]{1,0:T(1,128)S(1)}, u32[]{:S(2)}, u32[]{:S(2)}) %collective-permute-start.24) | collective-permute-done | bytes 8736 | tf_op jit(solution)/shard_map/ppermute | solution.py:77
  69.6 1.7 %shard_map.52 = (bf16[512,1024]{1,0:T(8,128)(2,1)S(1)}, bf16[512,1024]{1,0:T(8,128)(2,1)S(1)}, f32[1,128]{1,0:T(1,128)S(1)}, f32[1,128]{1,0:T(1,128)S(1)}) custom-call(f32[512,1024]{1,0:T(8,128)S(1)} %get-tuple-element.68.refs_5_.refs_0_, f32[512,1024]{1,0:T(8,128)S(1)} %get-tuple-element.74.refs_1_, f32[1,512]{1,0:T(1,128)S(1)} %log_add_fusion.refs_2_, ...), custom_call_target="tpu_custom_call" | custom-call | flops 67108864 | bytes 6291456 | tf_op jit(solution)/shard_map/pallas_call | solution.py:88
  72.0 2.8 %shard_map.53 = (bf16[1296,128]{1,0:T(8,128)(2,1)S(1)}, bf16[1296,128]{1,0:T(8,128)(2,1)S(1)}, bf16[656,128]{1,0:T(8,128)(2,1)S(1)}) custom-call(bf16[512,1024]{1,0:T(8,128)(2,1)S(1)} %get-tuple-element.78.refs_0_, bf16[512,1024]{1,0:T(8,128)(2,1)S(1)} %get-tuple-element.88.refs_1_, bf16[1024,1280]{1,0:T(8,128)(2,1)S(1)} %get-tuple-element.79.refs_2_, ...), custom_call_target="tpu_custom_call" | custom-call | flops 10737418240 | bytes 8388608 | tf_op jit(solution)/shard_map/pallas_call | solution.py:88
  74.9 3.8 %shard_map.54 = (bf16[2576,128]{1,0:T(8,128)(2,1)S(1)}, bf16[2576,128]{1,0:T(8,128)(2,1)S(1)}, bf16[2576,128]{1,0:T(8,128)(2,1)S(1)}, f32[256,1280]{1,0:T(8,128)S(1)}, f32[1,128]{1,0:T(1,128)S(1)}) custom-call(bf16[512,1024]{1,0:T(8,128)(2,1)S(1)} %get-tuple-element.78.refs_0_, bf16[512,1024]{1,0:T(8,128)(2,1)S(1)} %collective-permute-done.27.refs_1_, ...), custom_call_target="tpu_custom_call" | custom-call | flops 10737418240 | bytes 12582912 | tf_op jit(solution)/shard_map/pallas_call | solution.py:88
  78.8 1.9 %collective-permute-start.36 = (bf16[2576,128]{1,0:T(8,128)(2,1)S(1)}, bf16[2576,128]{1,0:T(8,128)(2,1)S(1)}, u32[]{:S(2)}, u32[]{:S(2)}) collective-permute-start(bf16[2576,128]{1,0:T(8,128)(2,1)S(1)} %get-tuple-element.101), channel_id=1, source_target_pairs={{0,32},{1,129},{2,34},{3,131},{4,36},{5,133},{6,38},{7,135},{8,40}... | collective-permute-start | bytes 1978376 | tf_op jit(solution)/shard_map/ppermute | solution.py:40
  80.7 1.3 %collective-permute-start.37 = (bf16[2576,128]{1,0:T(8,128)(2,1)S(1)}, bf16[2576,128]{1,0:T(8,128)(2,1)S(1)}, u32[]{:S(2)}, u32[]{:S(2)}) collective-permute-start(bf16[2576,128]{1,0:T(8,128)(2,1)S(1)} %get-tuple-element.102), channel_id=1, source_target_pairs={{0,48},{1,193},{2,50},{3,195},{4,52},{5,197},{6,54},{7,199},{8,56}... | collective-permute-start | bytes 1978376 | tf_op jit(solution)/shard_map/ppermute | solution.py:40
  82.1 1.7 %collective-permute-done.30.refs_5_.refs_2_ = bf16[656,128]{1,0:T(8,128)(2,1)S(1)} collective-permute-done((bf16[656,128]{1,0:T(8,128)(2,1)S(1)}, bf16[656,128]{1,0:T(8,128)(2,1)S(1)}, u32[]{:S(2)}, u32[]{:S(2)}) %collective-permute-start.30) | collective-permute-done | bytes 167968 | tf_op jit(solution)/shard_map/ppermute | solution.py:45
  83.8 2.1 %shard_map.55 = (f32[64,1280]{1,0:T(8,128)S(1)}, f32[64,1280]{1,0:T(8,128)S(1)}, f32[64,1280]{1,0:T(8,128)S(1)}) custom-call(bf16[512,1024]{1,0:T(8,128)(2,1)S(1)} %get-tuple-element.78.refs_0_, bf16[512,1024]{1,0:T(8,128)(2,1)S(1)} %get-tuple-element.88.refs_1_, bf16[1024,1280]{1,0:T(8,128)(2,1)S(1)} %get-tuple-element.79.refs_2_, ...), custom_call_target="tpu_custom_call" | custom-call | flops 10737418240 | bytes 8388608 | tf_op jit(solution)/shard_map/pallas_call | solution.py:88
  86.1 1.9 %collective-permute-start.32 = (bf16[1296,128]{1,0:T(8,128)(2,1)S(1)}, bf16[1296,128]{1,0:T(8,128)(2,1)S(1)}, u32[]{:S(2)}, u32[]{:S(2)}) collective-permute-start(bf16[1296,128]{1,0:T(8,128)(2,1)S(1)} %get-tuple-element.92), channel_id=1, source_target_pairs={{0,14},{1,15},{2,0},{3,1},{4,2},{5,3},{6,4},{7,5},{8,6},{9,7},{10,... | collective-permute-start | bytes 995336 | tf_op jit(solution)/shard_map/ppermute | solution.py:31
  88.0 5.5 %collective-permute-done.31.refs_0_ = bf16[1296,128]{1,0:T(8,128)(2,1)S(1)} collective-permute-done((bf16[1296,128]{1,0:T(8,128)(2,1)S(1)}, bf16[1296,128]{1,0:T(8,128)(2,1)S(1)}, u32[]{:S(2)}, u32[]{:S(2)}) %collective-permute-start.31) | collective-permute-done | bytes 331808 | tf_op jit(solution)/shard_map/ppermute | solution.py:31
  93.5 1.2 %collective-permute-done.32.refs_1_ = bf16[1296,128]{1,0:T(8,128)(2,1)S(1)} collective-permute-done((bf16[1296,128]{1,0:T(8,128)(2,1)S(1)}, bf16[1296,128]{1,0:T(8,128)(2,1)S(1)}, u32[]{:S(2)}, u32[]{:S(2)}) %collective-permute-start.32) | collective-permute-done | bytes 331808 | tf_op jit(solution)/shard_map/ppermute | solution.py:31
  94.7 3.6 %collective-permute-start.33 = (bf16[656,128]{1,0:T(8,128)(2,1)S(1)}, bf16[656,128]{1,0:T(8,128)(2,1)S(1)}, u32[]{:S(2)}, u32[]{:S(2)}) collective-permute-start(bf16[656,128]{1,0:T(8,128)(2,1)S(1)} %get-tuple-element.96), channel_id=1, source_target_pairs={{0,4},{1,5},{2,6},{3,7},{4,8},{5,9},{6,10},{7,11},{8,12},{9,13},{1... | collective-permute-start | bytes 503816 | tf_op jit(solution)/shard_map/ppermute | solution.py:31
  99.3 0.9 collective-permute-start.38
  100.3 1.6 %collective-permute-start.39 = (bf16[656,128]{1,0:T(8,128)(2,1)S(1)}, bf16[656,128]{1,0:T(8,128)(2,1)S(1)}, u32[]{:S(2)}, u32[]{:S(2)}) collective-permute-start(bf16[656,128]{1,0:T(8,128)(2,1)S(1)} %get-tuple-element.106), channel_id=1, source_target_pairs={{0,128},{1,33},{2,130},{3,35},{4,132},{5,37},{6,134},{7,39},{8,136... | collective-permute-start | bytes 503816 | tf_op jit(solution)/shard_map/ppermute | solution.py:40
  101.8 1.7 %collective-permute-start.40 = (bf16[656,128]{1,0:T(8,128)(2,1)S(1)}, bf16[656,128]{1,0:T(8,128)(2,1)S(1)}, u32[]{:S(2)}, u32[]{:S(2)}) collective-permute-start(bf16[656,128]{1,0:T(8,128)(2,1)S(1)} %get-tuple-element.107), channel_id=1, source_target_pairs={{0,192},{1,49},{2,194},{3,51},{4,196},{5,53},{6,198},{7,55},{8,200... | collective-permute-start | bytes 503816 | tf_op jit(solution)/shard_map/ppermute | solution.py:40
  103.8 2.6 %collective-permute-done.34.refs_1_ = bf16[656,128]{1,0:T(8,128)(2,1)S(1)} collective-permute-done((bf16[656,128]{1,0:T(8,128)(2,1)S(1)}, bf16[656,128]{1,0:T(8,128)(2,1)S(1)}, u32[]{:S(2)}, u32[]{:S(2)}) %collective-permute-start.34) | collective-permute-done | bytes 167968 | tf_op jit(solution)/shard_map/ppermute | solution.py:31
  106.3 1.4 %collective-permute-done.38.refs_4_ = bf16[656,128]{1,0:T(8,128)(2,1)S(1)} collective-permute-done((bf16[656,128]{1,0:T(8,128)(2,1)S(1)}, bf16[656,128]{1,0:T(8,128)(2,1)S(1)}, u32[]{:S(2)}, u32[]{:S(2)}) %collective-permute-start.38) | collective-permute-done | bytes 167968 | tf_op jit(solution)/shard_map/ppermute | solution.py:40
  (54 shorter events, 7.0 us)
Async XLA Ops:
  0.6 7.3 %collective-permute-start = (bf16[64,1280]{1,0:T(8,128)(2,1)}, bf16[64,1280]{1,0:T(8,128)(2,1)S(1)}, u32[]{:S(2)}, u32[]{:S(2)}) collective-permute-start(bf16[64,1280]{1,0:T(8,128)(2,1)} %refs_0_.1), channel_id=1, source_target_pairs={{0,2},{1,3},{2,4},{3,5},{4,6},{5,7},{6,8},{7,9},{8,10},{9,11},{10,... | collective-permute-start | bytes 491528 | tf_op jit(solution)/shard_map/ppermute | solution.py:31
  2.6 7.3 %collective-permute-start.1 = (bf16[64,1280]{1,0:T(8,128)(2,1)}, bf16[64,1280]{1,0:T(8,128)(2,1)S(1)}, u32[]{:S(2)}, u32[]{:S(2)}) collective-permute-start(bf16[64,1280]{1,0:T(8,128)(2,1)} %refs_0_.1), channel_id=1, source_target_pairs={{0,14},{1,15},{2,0},{3,1},{4,2},{5,3},{6,4},{7,5},{8,6},{9,7},{10,... | collective-permute-start | bytes 491528 | tf_op jit(solution)/shard_map/ppermute | solution.py:31
  2.7 9.3 %collective-permute-start.4 = (bf16[64,1280]{1,0:T(8,128)(2,1)}, bf16[64,1280]{1,0:T(8,128)(2,1)S(1)}, u32[]{:S(2)}, u32[]{:S(2)}) collective-permute-start(bf16[64,1280]{1,0:T(8,128)(2,1)} %text.1), channel_id=1, source_target_pairs={{0,16},{1,65},{2,18},{3,67},{4,20},{5,69},{6,22},{7,71},{8,24},{9,... | collective-permute-start | bytes 491528 | tf_op jit(solution)/shard_map/ppermute | solution.py:40
  4.3 7.8 %collective-permute-start.5 = (bf16[64,1280]{1,0:T(8,128)(2,1)}, bf16[64,1280]{1,0:T(8,128)(2,1)S(1)}, u32[]{:S(2)}, u32[]{:S(2)}) collective-permute-start(bf16[64,1280]{1,0:T(8,128)(2,1)} %text.1), channel_id=1, source_target_pairs={{0,48},{1,193},{2,50},{3,195},{4,52},{5,197},{6,54},{7,199},{8,56}... | collective-permute-start | bytes 491528 | tf_op jit(solution)/shard_map/ppermute | solution.py:40
  6.0 7.0 %collective-permute-start.6 = (bf16[64,1280]{1,0:T(8,128)(2,1)}, bf16[64,1280]{1,0:T(8,128)(2,1)S(1)}, u32[]{:S(2)}, u32[]{:S(2)}) collective-permute-start(bf16[64,1280]{1,0:T(8,128)(2,1)} %text.1), channel_id=1, source_target_pairs={{0,32},{1,129},{2,34},{3,131},{4,36},{5,133},{6,38},{7,135},{8,40}... | collective-permute-start | bytes 491528 | tf_op jit(solution)/shard_map/ppermute | solution.py:40
  8.0 7.3 %collective-permute-start.2 = (bf16[64,1280]{1,0:T(8,128)(2,1)S(1)}, bf16[64,1280]{1,0:T(8,128)(2,1)S(1)}, u32[]{:S(2)}, u32[]{:S(2)}) collective-permute-start(bf16[64,1280]{1,0:T(8,128)(2,1)S(1)} %collective-permute-done.refs_1_), channel_id=1, source_target_pairs={{0,2},{1,3},{2,4},{3,5},{4,6},{5,7},{6,8},{7,9},{8,10},{9,11},{10,... | collective-permute-start | bytes 491528 | tf_op jit(solution)/shard_map/ppermute | solution.py:31
  9.9 6.3 %collective-permute-start.3 = (bf16[64,1280]{1,0:T(8,128)(2,1)S(1)}, bf16[64,1280]{1,0:T(8,128)(2,1)S(1)}, u32[]{:S(2)}, u32[]{:S(2)}) collective-permute-start(bf16[64,1280]{1,0:T(8,128)(2,1)S(1)} %collective-permute-done.1.refs_2_), channel_id=1, source_target_pairs={{0,14},{1,15},{2,0},{3,1},{4,2},{5,3},{6,4},{7,5},{8,6},{9,7},{10,... | collective-permute-start | bytes 491528 | tf_op jit(solution)/shard_map/ppermute | solution.py:31
  13.0 0.9 copy-start
  16.2 20.1 %collective-permute-start.10 = (bf16[256,1280]{1,0:T(8,128)(2,1)S(1)}, bf16[256,1280]{1,0:T(8,128)(2,1)S(1)}, u32[]{:S(2)}, u32[]{:S(2)}) collective-permute-start(bf16[256,1280]{1,0:T(8,128)(2,1)S(1)} %shard_map.49.refs_8_), channel_id=1, source_target_pairs={{0,64},{1,17},{2,66},{3,19},{4,68},{5,21},{6,70},{7,23},{8,72},{9,... | collective-permute-start | bytes 1966088 | tf_op jit(solution)/shard_map/ppermute | solution.py:40
  17.7 18.6 %collective-permute-start.11 = (bf16[256,1280]{1,0:T(8,128)(2,1)S(1)}, bf16[256,1280]{1,0:T(8,128)(2,1)S(1)}, u32[]{:S(2)}, u32[]{:S(2)}) collective-permute-start(bf16[256,1280]{1,0:T(8,128)(2,1)S(1)} %shard_map.49.refs_8_), channel_id=1, source_target_pairs={{0,192},{1,49},{2,194},{3,51},{4,196},{5,53},{6,198},{7,55},{8,200... | collective-permute-start | bytes 1966088 | tf_op jit(solution)/shard_map/ppermute | solution.py:40
  19.4 16.9 %collective-permute-start.12 = (bf16[256,1280]{1,0:T(8,128)(2,1)S(1)}, bf16[256,1280]{1,0:T(8,128)(2,1)S(1)}, u32[]{:S(2)}, u32[]{:S(2)}) collective-permute-start(bf16[256,1280]{1,0:T(8,128)(2,1)S(1)} %shard_map.49.refs_8_), channel_id=1, source_target_pairs={{0,128},{1,33},{2,130},{3,35},{4,132},{5,37},{6,134},{7,39},{8,136... | collective-permute-start | bytes 1966088 | tf_op jit(solution)/shard_map/ppermute | solution.py:40
  21.3 6.1 %collective-permute-start.7 = (bf16[64,1280]{1,0:T(8,128)(2,1)S(1)}, bf16[64,1280]{1,0:T(8,128)(2,1)S(1)}, u32[]{:S(2)}, u32[]{:S(2)}) collective-permute-start(bf16[64,1280]{1,0:T(8,128)(2,1)S(1)} %collective-permute-done.2.refs_3_), channel_id=1, source_target_pairs={{0,2},{1,3},{2,4},{3,5},{4,6},{5,7},{6,8},{7,9},{8,10},{9,11},{10,... | collective-permute-start | bytes 491528 | tf_op jit(solution)/shard_map/ppermute | solution.py:31
  24.5 6.5 %collective-permute-start.8 = (bf16[64,1280]{1,0:T(8,128)(2,1)S(1)}, bf16[64,1280]{1,0:T(8,128)(2,1)S(1)}, u32[]{:S(2)}, u32[]{:S(2)}) collective-permute-start(bf16[64,1280]{1,0:T(8,128)(2,1)S(1)} %collective-permute-done.3.refs_4_), channel_id=1, source_target_pairs={{0,14},{1,15},{2,0},{3,1},{4,2},{5,3},{6,4},{7,5},{8,6},{9,7},{10,... | collective-permute-start | bytes 491528 | tf_op jit(solution)/shard_map/ppermute | solution.py:31
  31.0 5.3 %collective-permute-start.9 = (bf16[64,1280]{1,0:T(8,128)(2,1)S(1)}, bf16[64,1280]{1,0:T(8,128)(2,1)S(1)}, u32[]{:S(2)}, u32[]{:S(2)}) collective-permute-start(bf16[64,1280]{1,0:T(8,128)(2,1)S(1)} %collective-permute-done.7.refs_5_), channel_id=1, source_target_pairs={{0,2},{1,3},{2,4},{3,5},{4,6},{5,7},{6,8},{7,9},{8,10},{9,11},{10,... | collective-permute-start | bytes 491528 | tf_op jit(solution)/shard_map/ppermute | solution.py:31
  33.0 7.3 %collective-permute-start.13 = (bf16[256,1280]{1,0:T(8,128)(2,1)S(1)}, bf16[256,1280]{1,0:T(8,128)(2,1)S(1)}, u32[]{:S(2)}, u32[]{:S(2)}) collective-permute-start(bf16[256,1280]{1,0:T(8,128)(2,1)S(1)} %shard_map.49.refs_8_), channel_id=1, source_target_pairs={{0,1},{1,0},{2,3},{3,2},{4,5},{5,4},{6,7},{7,6},{8,9},{9,8},{10,11... | collective-permute-start | bytes 1966088 | tf_op jit(solution)/shard_map/ppermute | solution.py:54
  36.3 4.0 %collective-permute-start.14 = (bf16[256,1280]{1,0:T(8,128)(2,1)S(1)}, bf16[256,1280]{1,0:T(8,128)(2,1)S(1)}, u32[]{:S(2)}, u32[]{:S(2)}) collective-permute-start(bf16[256,1280]{1,0:T(8,128)(2,1)S(1)} %collective-permute-done.10.refs_9_), channel_id=1, source_target_pairs={{0,1},{1,0},{2,3},{3,2},{4,5},{5,4},{6,7},{7,6},{8,9},{9,8},{10,11... | collective-permute-start | bytes 1966088 | tf_op jit(solution)/shard_map/ppermute | solution.py:54
  36.4 3.9 %collective-permute-start.15 = (bf16[256,1280]{1,0:T(8,128)(2,1)S(1)}, bf16[256,1280]{1,0:T(8,128)(2,1)S(1)}, u32[]{:S(2)}, u32[]{:S(2)}) collective-permute-start(bf16[256,1280]{1,0:T(8,128)(2,1)S(1)} %collective-permute-done.11.refs_10_), channel_id=1, source_target_pairs={{0,1},{1,0},{2,3},{3,2},{4,5},{5,4},{6,7},{7,6},{8,9},{9,8},{10,11... | collective-permute-start | bytes 1966088 | tf_op jit(solution)/shard_map/ppermute | solution.py:54
  36.9 3.5 %collective-permute-start.16 = (bf16[256,1280]{1,0:T(8,128)(2,1)S(1)}, bf16[256,1280]{1,0:T(8,128)(2,1)S(1)}, u32[]{:S(2)}, u32[]{:S(2)}) collective-permute-start(bf16[256,1280]{1,0:T(8,128)(2,1)S(1)} %collective-permute-done.12.refs_11_), channel_id=1, source_target_pairs={{0,1},{1,0},{2,3},{3,2},{4,5},{5,4},{6,7},{7,6},{8,9},{9,8},{10,11... | collective-permute-start | bytes 1966088 | tf_op jit(solution)/shard_map/ppermute | solution.py:54
  37.0 0.9 copy-start.1
  42.8 3.7 %collective-permute-start.17 = (f32[1,512]{1,0:T(1,128)S(1)}, f32[1,512]{1,0:T(1,128)S(1)}, u32[]{:S(2)}, u32[]{:S(2)}) collective-permute-start(f32[1,512]{1,0:T(1,128)S(1)} %get-tuple-element.75), channel_id=1, source_target_pairs={{0,2},{1,3},{2,0},{3,1},{4,6},{5,7},{6,4},{7,5},{8,10},{9,11},{10,... | collective-permute-start | bytes 6152 | tf_op jit(solution)/shard_map/ppermute | solution.py:54
  44.9 30.0 %collective-permute-start.28 = (bf16[512,1280]{1,0:T(8,128)(2,1)S(1)}, bf16[512,1280]{1,0:T(8,128)(2,1)S(1)}, u32[]{:S(2)}, u32[]{:S(2)}) collective-permute-start(bf16[512,1280]{1,0:T(8,128)(2,1)S(1)} %get-tuple-element.70.refs_4_.refs_2_), channel_id=1, source_target_pairs={{0,1},{1,0},{2,3},{3,2},{4,5},{5,4},{6,7},{7,6},{8,9},{9,8},{10,11... | collective-permute-start | bytes 3932168 | tf_op jit(solution)/shard_map/ppermute | solution.py:54
  45.0 7.1 %collective-permute-start.20 = (f32[1,2176]{1,0:T(1,128)S(1)}, f32[1,2176]{1,0:T(1,128)S(1)}, u32[]{:S(2)}, u32[]{:S(2)}) collective-permute-start(f32[1,2176]{1,0:T(1,128)S(1)} %get-tuple-element.76), channel_id=1, source_target_pairs={{0,1},{1,0},{2,3},{3,2},{4,5},{5,4},{6,7},{7,6},{8,9},{9,8},{10,11... | collective-permute-start | bytes 26120 | tf_op jit(solution)/shard_map/ppermute | solution.py:54
  46.5 9.8 %collective-permute-start.18 = (f32[1,512]{1,0:T(1,128)S(1)}, f32[1,512]{1,0:T(1,128)S(1)}, u32[]{:S(2)}, u32[]{:S(2)}) collective-permute-start(f32[1,512]{1,0:T(1,128)S(1)} %log_add_fusion.2), channel_id=1, source_target_pairs={{0,4},{1,5},{2,6},{3,7},{4,0},{5,1},{6,2},{7,3},{8,12},{9,13},{10,... | collective-permute-start | bytes 6152 | tf_op jit(solution)/shard_map/ppermute | solution.py:54
  52.1 6.0 %collective-permute-start.23 = (f32[1,2176]{1,0:T(1,128)S(1)}, f32[1,2176]{1,0:T(1,128)S(1)}, u32[]{:S(2)}, u32[]{:S(2)}) collective-permute-start(f32[1,2176]{1,0:T(1,128)S(1)} %add_select_fusion.2), channel_id=1, source_target_pairs={{0,32},{1,33},{2,34},{3,35},{4,36},{5,37},{6,38},{7,39},{8,40},{9,... | collective-permute-start | bytes 26120 | tf_op jit(solution)/shard_map/ppermute | solution.py:77
  54.3 3.8 %collective-permute-start.22 = (f32[1,2176]{1,0:T(1,128)S(1)}, f32[1,2176]{1,0:T(1,128)S(1)}, u32[]{:S(2)}, u32[]{:S(2)}) collective-permute-start(f32[1,2176]{1,0:T(1,128)S(1)} %add_select_fusion.2), channel_id=1, source_target_pairs={{0,48},{1,49},{2,50},{3,51},{4,52},{5,53},{6,54},{7,55},{8,56},{9,... | collective-permute-start | bytes 26120 | tf_op jit(solution)/shard_map/ppermute | solution.py:77
  55.6 4.9 %collective-permute-start.21 = (f32[1,2176]{1,0:T(1,128)S(1)}, f32[1,2176]{1,0:T(1,128)S(1)}, u32[]{:S(2)}, u32[]{:S(2)}) collective-permute-start(f32[1,2176]{1,0:T(1,128)S(1)} %add_select_fusion.2), channel_id=1, source_target_pairs={{0,16},{1,17},{2,18},{3,19},{4,20},{5,21},{6,22},{7,23},{8,24},{9,... | collective-permute-start | bytes 26120 | tf_op jit(solution)/shard_map/ppermute | solution.py:77
  56.3 8.3 %collective-permute-start.19 = (f32[1,512]{1,0:T(1,128)S(1)}, f32[1,512]{1,0:T(1,128)S(1)}, u32[]{:S(2)}, u32[]{:S(2)}) collective-permute-start(f32[1,512]{1,0:T(1,128)S(1)} %log_add_fusion.1), channel_id=1, source_target_pairs={{0,8},{1,9},{2,10},{3,11},{4,12},{5,13},{6,14},{7,15},{8,0},{9,1},... | collective-permute-start | bytes 6152 | tf_op jit(solution)/shard_map/ppermute | solution.py:54
  60.5 5.2 %collective-permute-start.26 = (f32[1,2176]{1,0:T(1,128)S(1)}, f32[1,2176]{1,0:T(1,128)S(1)}, u32[]{:S(2)}, u32[]{:S(2)}) collective-permute-start(f32[1,2176]{1,0:T(1,128)S(1)} %add_select_fusion.1), channel_id=1, source_target_pairs={{0,128},{1,129},{2,130},{3,131},{4,132},{5,133},{6,134},{7,135},{8... | collective-permute-start | bytes 26120 | tf_op jit(solution)/shard_map/ppermute | solution.py:77
  61.4 4.6 %collective-permute-start.25 = (f32[1,2176]{1,0:T(1,128)S(1)}, f32[1,2176]{1,0:T(1,128)S(1)}, u32[]{:S(2)}, u32[]{:S(2)}) collective-permute-start(f32[1,2176]{1,0:T(1,128)S(1)} %add_select_fusion.1), channel_id=1, source_target_pairs={{0,192},{1,193},{2,194},{3,195},{4,196},{5,197},{6,198},{7,199},{8... | collective-permute-start | bytes 26120 | tf_op jit(solution)/shard_map/ppermute | solution.py:77
  64.7 4.9 %collective-permute-start.24 = (f32[1,2176]{1,0:T(1,128)S(1)}, f32[1,2176]{1,0:T(1,128)S(1)}, u32[]{:S(2)}, u32[]{:S(2)}) collective-permute-start(f32[1,2176]{1,0:T(1,128)S(1)} %add_select_fusion.1), channel_id=1, source_target_pairs={{0,64},{1,65},{2,66},{3,67},{4,68},{5,69},{6,70},{7,71},{8,72},{9,... | collective-permute-start | bytes 26120 | tf_op jit(solution)/shard_map/ppermute | solution.py:77
  71.3 3.6 %collective-permute-start.27 = (bf16[512,1024]{1,0:T(8,128)(2,1)S(1)}, bf16[512,1024]{1,0:T(8,128)(2,1)S(1)}, u32[]{:S(2)}, u32[]{:S(2)}) collective-permute-start(bf16[512,1024]{1,0:T(8,128)(2,1)S(1)} %get-tuple-element.88.refs_1_), channel_id=1, source_target_pairs={{0,1},{1,0},{2,3},{3,2},{4,5},{5,4},{6,7},{7,6},{8,9},{9,8},{10,11... | collective-permute-start | bytes 3145736 | tf_op jit(solution)/shard_map/ppermute | solution.py:54
  71.5 3.4 %collective-permute-start.29 = (f32[1,128]{1,0:T(1,128)S(1)}, f32[1,128]{1,0:T(1,128)S(1)}, u32[]{:S(2)}, u32[]{:S(2)}) collective-permute-start(f32[1,128]{1,0:T(1,128)S(1)} %get-tuple-element.86.refs_4_), channel_id=1, source_target_pairs={{0,1},{1,0},{2,3},{3,2},{4,5},{5,4},{6,7},{7,6},{8,9},{9,8},{10,11... | collective-permute-start | bytes 1544 | tf_op jit(solution)/shard_map/ppermute | solution.py:54
  74.8 9.0 %collective-permute-start.30 = (bf16[656,128]{1,0:T(8,128)(2,1)S(1)}, bf16[656,128]{1,0:T(8,128)(2,1)S(1)}, u32[]{:S(2)}, u32[]{:S(2)}) collective-permute-start(bf16[656,128]{1,0:T(8,128)(2,1)S(1)} %get-tuple-element.89), channel_id=1, source_target_pairs={{0,4},{1,13},{2,6},{3,15},{4,8},{5,1},{6,10},{7,3},{8,12},{9,5},{1... | collective-permute-start | bytes 503816 | tf_op jit(solution)/shard_map/ppermute | solution.py:45
  78.7 20.2 %collective-permute-start.35 = (bf16[2576,128]{1,0:T(8,128)(2,1)S(1)}, bf16[2576,128]{1,0:T(8,128)(2,1)S(1)}, u32[]{:S(2)}, u32[]{:S(2)}) collective-permute-start(bf16[2576,128]{1,0:T(8,128)(2,1)S(1)} %get-tuple-element.100), channel_id=1, source_target_pairs={{0,16},{1,65},{2,18},{3,67},{4,20},{5,69},{6,22},{7,71},{8,24},{9,... | collective-permute-start | bytes 1978376 | tf_op jit(solution)/shard_map/ppermute | solution.py:40
  78.8 20.1 %collective-permute-start.36 = (bf16[2576,128]{1,0:T(8,128)(2,1)S(1)}, bf16[2576,128]{1,0:T(8,128)(2,1)S(1)}, u32[]{:S(2)}, u32[]{:S(2)}) collective-permute-start(bf16[2576,128]{1,0:T(8,128)(2,1)S(1)} %get-tuple-element.101), channel_id=1, source_target_pairs={{0,32},{1,129},{2,34},{3,131},{4,36},{5,133},{6,38},{7,135},{8,40}... | collective-permute-start | bytes 1978376 | tf_op jit(solution)/shard_map/ppermute | solution.py:40
  80.7 18.2 %collective-permute-start.37 = (bf16[2576,128]{1,0:T(8,128)(2,1)S(1)}, bf16[2576,128]{1,0:T(8,128)(2,1)S(1)}, u32[]{:S(2)}, u32[]{:S(2)}) collective-permute-start(bf16[2576,128]{1,0:T(8,128)(2,1)S(1)} %get-tuple-element.102), channel_id=1, source_target_pairs={{0,48},{1,193},{2,50},{3,195},{4,52},{5,197},{6,54},{7,199},{8,56}... | collective-permute-start | bytes 1978376 | tf_op jit(solution)/shard_map/ppermute | solution.py:40
  85.9 7.6 %collective-permute-start.31 = (bf16[1296,128]{1,0:T(8,128)(2,1)S(1)}, bf16[1296,128]{1,0:T(8,128)(2,1)S(1)}, u32[]{:S(2)}, u32[]{:S(2)}) collective-permute-start(bf16[1296,128]{1,0:T(8,128)(2,1)S(1)} %get-tuple-element.91), channel_id=1, source_target_pairs={{0,2},{1,3},{2,4},{3,5},{4,6},{5,7},{6,8},{7,9},{8,10},{9,11},{10,... | collective-permute-start | bytes 995336 | tf_op jit(solution)/shard_map/ppermute | solution.py:31
  86.1 8.5 %collective-permute-start.32 = (bf16[1296,128]{1,0:T(8,128)(2,1)S(1)}, bf16[1296,128]{1,0:T(8,128)(2,1)S(1)}, u32[]{:S(2)}, u32[]{:S(2)}) collective-permute-start(bf16[1296,128]{1,0:T(8,128)(2,1)S(1)} %get-tuple-element.92), channel_id=1, source_target_pairs={{0,14},{1,15},{2,0},{3,1},{4,2},{5,3},{6,4},{7,5},{8,6},{9,7},{10,... | collective-permute-start | bytes 995336 | tf_op jit(solution)/shard_map/ppermute | solution.py:31
  94.7 9.0 %collective-permute-start.33 = (bf16[656,128]{1,0:T(8,128)(2,1)S(1)}, bf16[656,128]{1,0:T(8,128)(2,1)S(1)}, u32[]{:S(2)}, u32[]{:S(2)}) collective-permute-start(bf16[656,128]{1,0:T(8,128)(2,1)S(1)} %get-tuple-element.96), channel_id=1, source_target_pairs={{0,4},{1,5},{2,6},{3,7},{4,8},{5,9},{6,10},{7,11},{8,12},{9,13},{1... | collective-permute-start | bytes 503816 | tf_op jit(solution)/shard_map/ppermute | solution.py:31
  98.3 8.0 %collective-permute-start.34 = (bf16[656,128]{1,0:T(8,128)(2,1)S(1)}, bf16[656,128]{1,0:T(8,128)(2,1)S(1)}, u32[]{:S(2)}, u32[]{:S(2)}) collective-permute-start(bf16[656,128]{1,0:T(8,128)(2,1)S(1)} %get-tuple-element.97), channel_id=1, source_target_pairs={{0,12},{1,13},{2,14},{3,15},{4,0},{5,1},{6,2},{7,3},{8,4},{9,5},{1... | collective-permute-start | bytes 503816 | tf_op jit(solution)/shard_map/ppermute | solution.py:31
  99.3 8.4 %collective-permute-start.38 = (bf16[656,128]{1,0:T(8,128)(2,1)S(1)}, bf16[656,128]{1,0:T(8,128)(2,1)S(1)}, u32[]{:S(2)}, u32[]{:S(2)}) collective-permute-start(bf16[656,128]{1,0:T(8,128)(2,1)S(1)} %get-tuple-element.105), channel_id=1, source_target_pairs={{0,64},{1,17},{2,66},{3,19},{4,68},{5,21},{6,70},{7,23},{8,72},{9,... | collective-permute-start | bytes 503816 | tf_op jit(solution)/shard_map/ppermute | solution.py:40
  100.3 7.5 %collective-permute-start.39 = (bf16[656,128]{1,0:T(8,128)(2,1)S(1)}, bf16[656,128]{1,0:T(8,128)(2,1)S(1)}, u32[]{:S(2)}, u32[]{:S(2)}) collective-permute-start(bf16[656,128]{1,0:T(8,128)(2,1)S(1)} %get-tuple-element.106), channel_id=1, source_target_pairs={{0,128},{1,33},{2,130},{3,35},{4,132},{5,37},{6,134},{7,39},{8,136... | collective-permute-start | bytes 503816 | tf_op jit(solution)/shard_map/ppermute | solution.py:40
  101.8 6.8 %collective-permute-start.40 = (bf16[656,128]{1,0:T(8,128)(2,1)S(1)}, bf16[656,128]{1,0:T(8,128)(2,1)S(1)}, u32[]{:S(2)}, u32[]{:S(2)}) collective-permute-start(bf16[656,128]{1,0:T(8,128)(2,1)S(1)} %get-tuple-element.107), channel_id=1, source_target_pairs={{0,192},{1,49},{2,194},{3,51},{4,196},{5,53},{6,198},{7,55},{8,200... | collective-permute-start | bytes 503816 | tf_op jit(solution)/shard_map/ppermute | solution.py:40

commit v5 on v4

--- a/solution.py
+++ b/solution.py
@@ -270,7 +270,7 @@
         rows = pl.ds(pl.multiple_of(lax.rem(z + dz + NZ, NZ) * SHARD, SHARD), SHARD)
         rows_own[i * SHARD : (i + 1) * SHARD, :] = own[rows, :]
         rows_other[i * SHARD : (i + 1) * SHARD, :] = other[rows, :]
-    chunk = 256
+    chunk = 640
 
     @pl.loop(0, total.shape[1] // chunk)
     def _(i):
@@ -300,7 +300,7 @@
     x, y, _, c = at
     p = p_own[...] + p_other[...]
     p_out[...] = p
-    chunk = 256
+    chunk = 512
 
     @pl.loop(0, PLANE // chunk)
     def _(i):
@@ -360,17 +360,22 @@
             write_note(sent[e - 1], total)
 
 
-def last_kernel(at, up, down, here, q, first, second, third, kept, p, image_out, text_out, loss_out):
-    strips = kept.shape[1] // 128
+def image_last_kernel(at, up, down, here, q, image_out, q_out):
+    strips = here.shape[1] // 128
     for i in range(strips):
         rows, cols = part_of(up, 0, i, strips), columns(i)
         image = here[:, cols] + up[rows, :].astype(F32) + down[rows, :].astype(F32)
         image_out[:, cols] = image.astype(BF16)
+    q_out[...] = q[...] + read_note(up) + read_note(down)
+
+
+def text_last_kernel(at, first, second, third, kept, p, q, text_out, loss_out):
+    strips = kept.shape[1] // 128
+    for i in range(strips):
+        rows, cols = part_of(first, 0, i, strips), columns(i)
         text = kept[:, cols] + first[rows, :].astype(F32) + second[rows, :].astype(F32) + third[rows, :].astype(F32)
         text_out[:, cols] = text.astype(BF16)
-    loss = q[...] + p[...]
-    for message in (up, down, first, second, third):
-        loss += read_note(message)
+    loss = q[...] + p[...] + read_note(first) + read_note(second) + read_note(third)
     loss_out[...] = loss / (ROWS * NC * NX * NY)
 
 
@@ -499,15 +504,25 @@
         12,
     )
     sent = [shift_plane(part, d, False) for d, part in enumerate(sent, 1)]
-    image_grad, text_grad, loss = call(
-        last_kernel,
-        [((SHARD, embed), BF16)] * 2 + [scalar],
-        (up, down, here, q, *sent, kept, p),
+    image_grad, q = call(
+        image_last_kernel,
+        [((SHARD, embed), BF16), scalar],
+        (up, down, here, q),
         [],
+        1 << 19,
+        0,
         1 << 20,
+        8,
+    )
+    text_grad, loss = call(
+        text_last_kernel,
+        [((SHARD, embed), BF16), scalar],
+        (*sent, kept, p, q),
+        [],
+        1 << 19,
         0,
-        2 << 20,
-        12,
+        1 << 20,
+        8,
     )
     return image_grad, text_grad, loss[0, 0]
 

time: 111 us -> 110 us (level)
    pallas_call x9 -> x10, Pallas kernels: 16.4 us -> 16.2 us  [call(): pl.pallas_call(lambda *refs: kernel(position(), *refs), out_shape=[jax.Sh...]
where the time goes in v5:
time: 110 us; the launch traced here: 109 us
  starting transfers between devices  55.6 us (51%)
  waiting for transfers between devices  34 us (31%)
  Pallas kernels  16.4 us (15%)
  local copies, waits for them, and re-layouts  1.83 us (2%)
    ppermute x11, waiting for transfers between devices, shift_z(): return lax.ppermute(value, AXES, pairs)  20.8 us
    ppermute x12, starting transfers between devices, shift_plane(): return lax.ppermute(value, AXES, pairs)  18 us
    ppermute x11, starting transfers between devices, shift_z(): return lax.ppermute(value, AXES, pairs)  17.8 us
    pallas_call x10, Pallas kernels, call(): pl.pallas_call(lambda *refs: kernel(position(), *refs), out_shape=[jax.Sh...  16.2 us
    ppermute x11, starting transfers between devices, swap(): return lax.ppermute(value, AXES, pairs)  11.3 us
    ppermute x6, starting transfers between devices, shift_one(): return lax.ppermute(value, AXES, pairs)  8.38 us
    ppermute x6, waiting for transfers between devices, shift_one(): return lax.ppermute(value, AXES, pairs)  7.17 us
    ppermute x12, waiting for transfers between devices, shift_plane(): return lax.ppermute(value, AXES, pairs)  2.79 us
  transfers between devices with their start and end apart: 41, of which 18 were waited for; matrix products, arithmetic and copies ran while one was open for 0% of the time, Pallas kernels for 12%

profile of v5, /device:TPU:32, one launch (start us, length us, event | category | flops | bytes accessed | tf_op | source)
XLA Modules:
  0.0 108.8 jit_solution(3748126042038403511)
XLA Ops:
  0.6 2.0 %collective-permute-start = (bf16[64,1280]{1,0:T(8,128)(2,1)}, bf16[64,1280]{1,0:T(8,128)(2,1)S(1)}, u32[]{:S(2)}, u32[]{:S(2)}) collective-permute-start(bf16[64,1280]{1,0:T(8,128)(2,1)} %refs_0_.1), channel_id=1, source_target_pairs={{0,2},{1,3},{2,4},{3,5},{4,6},{5,7},{6,8},{7,9},{8,10},{9,11},{10,... | collective-permute-start | bytes 491528 | tf_op jit(solution)/shard_map/ppermute | solution.py:31
  2.7 1.6 %collective-permute-start.4 = (bf16[64,1280]{1,0:T(8,128)(2,1)}, bf16[64,1280]{1,0:T(8,128)(2,1)S(1)}, u32[]{:S(2)}, u32[]{:S(2)}) collective-permute-start(bf16[64,1280]{1,0:T(8,128)(2,1)} %text.1), channel_id=1, source_target_pairs={{0,16},{1,65},{2,18},{3,67},{4,20},{5,69},{6,22},{7,71},{8,24},{9,... | collective-permute-start | bytes 491528 | tf_op jit(solution)/shard_map/ppermute | solution.py:40
  4.3 1.7 %collective-permute-start.5 = (bf16[64,1280]{1,0:T(8,128)(2,1)}, bf16[64,1280]{1,0:T(8,128)(2,1)S(1)}, u32[]{:S(2)}, u32[]{:S(2)}) collective-permute-start(bf16[64,1280]{1,0:T(8,128)(2,1)} %text.1), channel_id=1, source_target_pairs={{0,48},{1,193},{2,50},{3,195},{4,52},{5,197},{6,54},{7,199},{8,56}... | collective-permute-start | bytes 491528 | tf_op jit(solution)/shard_map/ppermute | solution.py:40
  6.0 2.0 %collective-permute-start.6 = (bf16[64,1280]{1,0:T(8,128)(2,1)}, bf16[64,1280]{1,0:T(8,128)(2,1)S(1)}, u32[]{:S(2)}, u32[]{:S(2)}) collective-permute-start(bf16[64,1280]{1,0:T(8,128)(2,1)} %text.1), channel_id=1, source_target_pairs={{0,32},{1,129},{2,34},{3,131},{4,36},{5,133},{6,38},{7,135},{8,40}... | collective-permute-start | bytes 491528 | tf_op jit(solution)/shard_map/ppermute | solution.py:40
  8.0 1.9 %collective-permute-start.2 = (bf16[64,1280]{1,0:T(8,128)(2,1)S(1)}, bf16[64,1280]{1,0:T(8,128)(2,1)S(1)}, u32[]{:S(2)}, u32[]{:S(2)}) collective-permute-start(bf16[64,1280]{1,0:T(8,128)(2,1)S(1)} %collective-permute-done.refs_1_), channel_id=1, source_target_pairs={{0,2},{1,3},{2,4},{3,5},{4,6},{5,7},{6,8},{7,9},{8,10},{9,11},{10,... | collective-permute-start | bytes 491528 | tf_op jit(solution)/shard_map/ppermute | solution.py:31
  9.9 2.2 %collective-permute-start.3 = (bf16[64,1280]{1,0:T(8,128)(2,1)S(1)}, bf16[64,1280]{1,0:T(8,128)(2,1)S(1)}, u32[]{:S(2)}, u32[]{:S(2)}) collective-permute-start(bf16[64,1280]{1,0:T(8,128)(2,1)S(1)} %collective-permute-done.1.refs_2_), channel_id=1, source_target_pairs={{0,14},{1,15},{2,0},{3,1},{4,2},{5,3},{6,4},{7,5},{8,6},{9,7},{10,... | collective-permute-start | bytes 491528 | tf_op jit(solution)/shard_map/ppermute | solution.py:31
  12.1 0.9 collective-permute-done.6.refs_2_
  13.0 0.9 copy-done
  14.1 1.1 %collective-permute-done.2.refs_3_ = bf16[64,1280]{1,0:T(8,128)(2,1)S(1)} collective-permute-done((bf16[64,1280]{1,0:T(8,128)(2,1)S(1)}, bf16[64,1280]{1,0:T(8,128)(2,1)S(1)}, u32[]{:S(2)}, u32[]{:S(2)}) %collective-permute-start.2) | collective-permute-done | bytes 163872 | tf_op jit(solution)/shard_map/ppermute | solution.py:31
  15.3 0.9 collective-permute-done.3.refs_4_
  16.2 1.5 %collective-permute-start.10 = (bf16[256,1280]{1,0:T(8,128)(2,1)S(1)}, bf16[256,1280]{1,0:T(8,128)(2,1)S(1)}, u32[]{:S(2)}, u32[]{:S(2)}) collective-permute-start(bf16[256,1280]{1,0:T(8,128)(2,1)S(1)} %shard_map.49.refs_8_), channel_id=1, source_target_pairs={{0,64},{1,17},{2,66},{3,19},{4,68},{5,21},{6,70},{7,23},{8,72},{9,... | collective-permute-start | bytes 1966088 | tf_op jit(solution)/shard_map/ppermute | solution.py:40
  17.7 1.7 %collective-permute-start.11 = (bf16[256,1280]{1,0:T(8,128)(2,1)S(1)}, bf16[256,1280]{1,0:T(8,128)(2,1)S(1)}, u32[]{:S(2)}, u32[]{:S(2)}) collective-permute-start(bf16[256,1280]{1,0:T(8,128)(2,1)S(1)} %shard_map.49.refs_8_), channel_id=1, source_target_pairs={{0,192},{1,49},{2,194},{3,51},{4,196},{5,53},{6,198},{7,55},{8,200... | collective-permute-start | bytes 1966088 | tf_op jit(solution)/shard_map/ppermute | solution.py:40
  19.4 1.8 %collective-permute-start.12 = (bf16[256,1280]{1,0:T(8,128)(2,1)S(1)}, bf16[256,1280]{1,0:T(8,128)(2,1)S(1)}, u32[]{:S(2)}, u32[]{:S(2)}) collective-permute-start(bf16[256,1280]{1,0:T(8,128)(2,1)S(1)} %shard_map.49.refs_8_), channel_id=1, source_target_pairs={{0,128},{1,33},{2,130},{3,35},{4,132},{5,37},{6,134},{7,39},{8,136... | collective-permute-start | bytes 1966088 | tf_op jit(solution)/shard_map/ppermute | solution.py:40
  21.3 3.2 %collective-permute-start.7 = (bf16[64,1280]{1,0:T(8,128)(2,1)S(1)}, bf16[64,1280]{1,0:T(8,128)(2,1)S(1)}, u32[]{:S(2)}, u32[]{:S(2)}) collective-permute-start(bf16[64,1280]{1,0:T(8,128)(2,1)S(1)} %collective-permute-done.2.refs_3_), channel_id=1, source_target_pairs={{0,2},{1,3},{2,4},{3,5},{4,6},{5,7},{6,8},{7,9},{8,10},{9,11},{10,... | collective-permute-start | bytes 491528 | tf_op jit(solution)/shard_map/ppermute | solution.py:31
  24.5 2.8 %collective-permute-done.7.refs_5_ = bf16[64,1280]{1,0:T(8,128)(2,1)S(1)} collective-permute-done((bf16[64,1280]{1,0:T(8,128)(2,1)S(1)}, bf16[64,1280]{1,0:T(8,128)(2,1)S(1)}, u32[]{:S(2)}, u32[]{:S(2)}) %collective-permute-start.7) | collective-permute-done | bytes 163872 | tf_op jit(solution)/shard_map/ppermute | solution.py:31
  27.3 3.7 %collective-permute-done.8.refs_6_ = bf16[64,1280]{1,0:T(8,128)(2,1)S(1)} collective-permute-done((bf16[64,1280]{1,0:T(8,128)(2,1)S(1)}, bf16[64,1280]{1,0:T(8,128)(2,1)S(1)}, u32[]{:S(2)}, u32[]{:S(2)}) %collective-permute-start.8) | collective-permute-done | bytes 163872 | tf_op jit(solution)/shard_map/ppermute | solution.py:31
  31.0 2.0 %collective-permute-start.9 = (bf16[64,1280]{1,0:T(8,128)(2,1)S(1)}, bf16[64,1280]{1,0:T(8,128)(2,1)S(1)}, u32[]{:S(2)}, u32[]{:S(2)}) collective-permute-start(bf16[64,1280]{1,0:T(8,128)(2,1)S(1)} %collective-permute-done.7.refs_5_), channel_id=1, source_target_pairs={{0,2},{1,3},{2,4},{3,5},{4,6},{5,7},{6,8},{7,9},{8,10},{9,11},{10,... | collective-permute-start | bytes 491528 | tf_op jit(solution)/shard_map/ppermute | solution.py:31
  33.0 3.3 %collective-permute-done.9.refs_7_ = bf16[64,1280]{1,0:T(8,128)(2,1)S(1)} collective-permute-done((bf16[64,1280]{1,0:T(8,128)(2,1)S(1)}, bf16[64,1280]{1,0:T(8,128)(2,1)S(1)}, u32[]{:S(2)}, u32[]{:S(2)}) %collective-permute-start.9) | collective-permute-done | bytes 163872 | tf_op jit(solution)/shard_map/ppermute | solution.py:31
  37.0 0.9 copy-done.1
  38.0 2.4 %shard_map.50 = (bf16[512,1280]{1,0:T(8,128)(2,1)S(1)}, bf16[1024,1280]{1,0:T(8,128)(2,1)S(1)}, f32[512,1024]{1,0:T(8,128)S(1)}, f32[1,1024]{1,0:T(1,128)S(1)}, ...) custom-call(bf16[64,1280]{1,0:T(8,128)(2,1)S(1)} %copy-done.1, bf16[64,1280]{1,0:T(8,128)(2,1)S(1)} %collective-permute-done.refs_1_, ...), custom_call_target="tpu_custom_call" | custom-call | flops 10737418240 | bytes 7340032 | tf_op jit(solution)/shard_map/pallas_call | solution.py:88
  40.4 2.4 %shard_map.51 = (bf16[1024,1280]{1,0:T(8,128)(2,1)S(1)}, f32[512,1024]{1,0:T(8,128)S(1)}, f32[1,512]{1,0:T(1,128)S(1)}, f32[1,2176]{1,0:T(1,128)S(1)}) custom-call(bf16[256,1280]{1,0:T(8,128)(2,1)S(1)} %collective-permute-done.13.refs_0_, bf16[256,1280]{1,0:T(8,128)(2,1)S(1)} %collective-permute-done.14.refs_1_, ...), custom_call_target="tpu_custom_call" | custom-call | flops 10737418240 | bytes 7340032 | tf_op jit(solution)/shard_map/pallas_call | solution.py:88
  42.8 2.1 %collective-permute-start.17 = (f32[1,512]{1,0:T(1,128)S(1)}, f32[1,512]{1,0:T(1,128)S(1)}, u32[]{:S(2)}, u32[]{:S(2)}) collective-permute-start(f32[1,512]{1,0:T(1,128)S(1)} %get-tuple-element.76), channel_id=1, source_target_pairs={{0,2},{1,3},{2,0},{3,1},{4,6},{5,7},{6,4},{7,5},{8,10},{9,11},{10,... | collective-permute-start | bytes 6152 | tf_op jit(solution)/shard_map/ppermute | solution.py:54
  45.4 1.1 collective-permute-done.17
  46.5 5.6 %collective-permute-start.18 = (f32[1,512]{1,0:T(1,128)S(1)}, f32[1,512]{1,0:T(1,128)S(1)}, u32[]{:S(2)}, u32[]{:S(2)}) collective-permute-start(f32[1,512]{1,0:T(1,128)S(1)} %log_add_fusion.2), channel_id=1, source_target_pairs={{0,4},{1,5},{2,6},{3,7},{4,0},{5,1},{6,2},{7,3},{8,12},{9,13},{10,... | collective-permute-start | bytes 6152 | tf_op jit(solution)/shard_map/ppermute | solution.py:54
  52.1 2.2 %collective-permute-start.23 = (f32[1,2176]{1,0:T(1,128)S(1)}, f32[1,2176]{1,0:T(1,128)S(1)}, u32[]{:S(2)}, u32[]{:S(2)}) collective-permute-start(f32[1,2176]{1,0:T(1,128)S(1)} %add_select_fusion.2), channel_id=1, source_target_pairs={{0,32},{1,33},{2,34},{3,35},{4,36},{5,37},{6,38},{7,39},{8,40},{9,... | collective-permute-start | bytes 26120 | tf_op jit(solution)/shard_map/ppermute | solution.py:77
  54.3 1.3 %collective-permute-start.22 = (f32[1,2176]{1,0:T(1,128)S(1)}, f32[1,2176]{1,0:T(1,128)S(1)}, u32[]{:S(2)}, u32[]{:S(2)}) collective-permute-start(f32[1,2176]{1,0:T(1,128)S(1)} %add_select_fusion.2), channel_id=1, source_target_pairs={{0,48},{1,49},{2,50},{3,51},{4,52},{5,53},{6,54},{7,55},{8,56},{9,... | collective-permute-start | bytes 26120 | tf_op jit(solution)/shard_map/ppermute | solution.py:77
  56.3 1.7 %collective-permute-start.19 = (f32[1,512]{1,0:T(1,128)S(1)}, f32[1,512]{1,0:T(1,128)S(1)}, u32[]{:S(2)}, u32[]{:S(2)}) collective-permute-start(f32[1,512]{1,0:T(1,128)S(1)} %log_add_fusion.1), channel_id=1, source_target_pairs={{0,8},{1,9},{2,10},{3,11},{4,12},{5,13},{6,14},{7,15},{8,0},{9,1},... | collective-permute-start | bytes 6152 | tf_op jit(solution)/shard_map/ppermute | solution.py:54
  58.1 2.3 %collective-permute-done.21 = f32[1,2176]{1,0:T(1,128)S(1)} collective-permute-done((f32[1,2176]{1,0:T(1,128)S(1)}, f32[1,2176]{1,0:T(1,128)S(1)}, u32[]{:S(2)}, u32[]{:S(2)}) %collective-permute-start.21) | collective-permute-done | bytes 8736 | tf_op jit(solution)/shard_map/ppermute | solution.py:77
  60.5 0.9 collective-permute-start.26
  61.4 3.3 %collective-permute-start.25 = (f32[1,2176]{1,0:T(1,128)S(1)}, f32[1,2176]{1,0:T(1,128)S(1)}, u32[]{:S(2)}, u32[]{:S(2)}) collective-permute-start(f32[1,2176]{1,0:T(1,128)S(1)} %add_select_fusion.1), channel_id=1, source_target_pairs={{0,192},{1,193},{2,194},{3,195},{4,196},{5,197},{6,198},{7,199},{8... | collective-permute-start | bytes 26120 | tf_op jit(solution)/shard_map/ppermute | solution.py:77
  64.7 1.0 collective-permute-done.26
  66.0 3.5 %collective-permute-done.24 = f32[1,2176]{1,0:T(1,128)S(1)} collective-permute-done((f32[1,2176]{1,0:T(1,128)S(1)}, f32[1,2176]{1,0:T(1,128)S(1)}, u32[]{:S(2)}, u32[]{:S(2)}) %collective-permute-start.24) | collective-permute-done | bytes 8736 | tf_op jit(solution)/shard_map/ppermute | solution.py:77
  69.6 1.7 %shard_map.52 = (bf16[512,1024]{1,0:T(8,128)(2,1)S(1)}, bf16[512,1024]{1,0:T(8,128)(2,1)S(1)}, f32[1,128]{1,0:T(1,128)S(1)}, f32[1,128]{1,0:T(1,128)S(1)}) custom-call(f32[512,1024]{1,0:T(8,128)S(1)} %get-tuple-element.69.refs_5_.refs_0_, f32[512,1024]{1,0:T(8,128)S(1)} %get-tuple-element.75.refs_1_, f32[1,512]{1,0:T(1,128)S(1)} %log_add_fusion.refs_2_, ...), custom_call_target="tpu_custom_call" | custom-call | flops 67108864 | bytes 6291456 | tf_op jit(solution)/shard_map/pallas_call | solution.py:88
  72.0 2.6 %shard_map.53 = (bf16[1296,128]{1,0:T(8,128)(2,1)S(1)}, bf16[1296,128]{1,0:T(8,128)(2,1)S(1)}, bf16[656,128]{1,0:T(8,128)(2,1)S(1)}) custom-call(bf16[512,1024]{1,0:T(8,128)(2,1)S(1)} %get-tuple-element.79.refs_0_, bf16[512,1024]{1,0:T(8,128)(2,1)S(1)} %get-tuple-element.89.refs_1_, bf16[1024,1280]{1,0:T(8,128)(2,1)S(1)} %get-tuple-element.80.refs_2_, ...), custom_call_target="tpu_custom_call" | custom-call | flops 10737418240 | bytes 8388608 | tf_op jit(solution)/shard_map/pallas_call | solution.py:88
  74.7 3.5 %shard_map.54 = (bf16[2576,128]{1,0:T(8,128)(2,1)S(1)}, bf16[2576,128]{1,0:T(8,128)(2,1)S(1)}, bf16[2576,128]{1,0:T(8,128)(2,1)S(1)}, f32[256,1280]{1,0:T(8,128)S(1)}, f32[1,128]{1,0:T(1,128)S(1)}) custom-call(bf16[512,1024]{1,0:T(8,128)(2,1)S(1)} %get-tuple-element.79.refs_0_, bf16[512,1024]{1,0:T(8,128)(2,1)S(1)} %collective-permute-done.27.refs_1_, ...), custom_call_target="tpu_custom_call" | custom-call | flops 10737418240 | bytes 12582912 | tf_op jit(solution)/shard_map/pallas_call | solution.py:88
  78.3 1.9 %collective-permute-start.36 = (bf16[2576,128]{1,0:T(8,128)(2,1)S(1)}, bf16[2576,128]{1,0:T(8,128)(2,1)S(1)}, u32[]{:S(2)}, u32[]{:S(2)}) collective-permute-start(bf16[2576,128]{1,0:T(8,128)(2,1)S(1)} %get-tuple-element.103), channel_id=1, source_target_pairs={{0,32},{1,129},{2,34},{3,131},{4,36},{5,133},{6,38},{7,135},{8,40}... | collective-permute-start | bytes 1978376 | tf_op jit(solution)/shard_map/ppermute | solution.py:40
  80.2 1.3 %collective-permute-start.37 = (bf16[2576,128]{1,0:T(8,128)(2,1)S(1)}, bf16[2576,128]{1,0:T(8,128)(2,1)S(1)}, u32[]{:S(2)}, u32[]{:S(2)}) collective-permute-start(bf16[2576,128]{1,0:T(8,128)(2,1)S(1)} %get-tuple-element.104), channel_id=1, source_target_pairs={{0,48},{1,193},{2,50},{3,195},{4,52},{5,197},{6,54},{7,199},{8,56}... | collective-permute-start | bytes 1978376 | tf_op jit(solution)/shard_map/ppermute | solution.py:40
  81.5 2.1 %collective-permute-done.30.refs_5_.refs_2_ = bf16[656,128]{1,0:T(8,128)(2,1)S(1)} collective-permute-done((bf16[656,128]{1,0:T(8,128)(2,1)S(1)}, bf16[656,128]{1,0:T(8,128)(2,1)S(1)}, u32[]{:S(2)}, u32[]{:S(2)}) %collective-permute-start.30) | collective-permute-done | bytes 167968 | tf_op jit(solution)/shard_map/ppermute | solution.py:45
  83.6 1.7 %shard_map.55 = (f32[64,1280]{1,0:T(8,128)S(1)}, f32[64,1280]{1,0:T(8,128)S(1)}, f32[64,1280]{1,0:T(8,128)S(1)}) custom-call(bf16[512,1024]{1,0:T(8,128)(2,1)S(1)} %get-tuple-element.79.refs_0_, bf16[512,1024]{1,0:T(8,128)(2,1)S(1)} %get-tuple-element.89.refs_1_, bf16[1024,1280]{1,0:T(8,128)(2,1)S(1)} %get-tuple-element.80.refs_2_, ...), custom_call_target="tpu_custom_call" | custom-call | flops 10737418240 | bytes 8388608 | tf_op jit(solution)/shard_map/pallas_call | solution.py:88
  85.4 2.0 %collective-permute-start.32 = (bf16[1296,128]{1,0:T(8,128)(2,1)S(1)}, bf16[1296,128]{1,0:T(8,128)(2,1)S(1)}, u32[]{:S(2)}, u32[]{:S(2)}) collective-permute-start(bf16[1296,128]{1,0:T(8,128)(2,1)S(1)} %get-tuple-element.93), channel_id=1, source_target_pairs={{0,14},{1,15},{2,0},{3,1},{4,2},{5,3},{6,4},{7,5},{8,6},{9,7},{10,... | collective-permute-start | bytes 995336 | tf_op jit(solution)/shard_map/ppermute | solution.py:31
  87.4 5.3 %collective-permute-done.31.refs_0_ = bf16[1296,128]{1,0:T(8,128)(2,1)S(1)} collective-permute-done((bf16[1296,128]{1,0:T(8,128)(2,1)S(1)}, bf16[1296,128]{1,0:T(8,128)(2,1)S(1)}, u32[]{:S(2)}, u32[]{:S(2)}) %collective-permute-start.31) | collective-permute-done | bytes 331808 | tf_op jit(solution)/shard_map/ppermute | solution.py:31
  92.7 1.3 %collective-permute-done.32.refs_1_ = bf16[1296,128]{1,0:T(8,128)(2,1)S(1)} collective-permute-done((bf16[1296,128]{1,0:T(8,128)(2,1)S(1)}, bf16[1296,128]{1,0:T(8,128)(2,1)S(1)}, u32[]{:S(2)}, u32[]{:S(2)}) %collective-permute-start.32) | collective-permute-done | bytes 331808 | tf_op jit(solution)/shard_map/ppermute | solution.py:31
  94.2 3.3 %collective-permute-start.33 = (bf16[656,128]{1,0:T(8,128)(2,1)S(1)}, bf16[656,128]{1,0:T(8,128)(2,1)S(1)}, u32[]{:S(2)}, u32[]{:S(2)}) collective-permute-start(bf16[656,128]{1,0:T(8,128)(2,1)S(1)} %get-tuple-element.97), channel_id=1, source_target_pairs={{0,4},{1,5},{2,6},{3,7},{4,8},{5,9},{6,10},{7,11},{8,12},{9,13},{1... | collective-permute-start | bytes 503816 | tf_op jit(solution)/shard_map/ppermute | solution.py:31
  97.5 0.9 collective-permute-start.34
  99.4 1.6 %collective-permute-start.39 = (bf16[656,128]{1,0:T(8,128)(2,1)S(1)}, bf16[656,128]{1,0:T(8,128)(2,1)S(1)}, u32[]{:S(2)}, u32[]{:S(2)}) collective-permute-start(bf16[656,128]{1,0:T(8,128)(2,1)S(1)} %get-tuple-element.108), channel_id=1, source_target_pairs={{0,128},{1,33},{2,130},{3,35},{4,132},{5,37},{6,134},{7,39},{8,136... | collective-permute-start | bytes 503816 | tf_op jit(solution)/shard_map/ppermute | solution.py:40
  100.9 2.2 %collective-permute-start.40 = (bf16[656,128]{1,0:T(8,128)(2,1)S(1)}, bf16[656,128]{1,0:T(8,128)(2,1)S(1)}, u32[]{:S(2)}, u32[]{:S(2)}) collective-permute-start(bf16[656,128]{1,0:T(8,128)(2,1)S(1)} %get-tuple-element.109), channel_id=1, source_target_pairs={{0,192},{1,49},{2,194},{3,51},{4,196},{5,53},{6,198},{7,55},{8,200... | collective-permute-start | bytes 503816 | tf_op jit(solution)/shard_map/ppermute | solution.py:40
  103.2 2.2 %collective-permute-done.34.refs_1_ = bf16[656,128]{1,0:T(8,128)(2,1)S(1)} collective-permute-done((bf16[656,128]{1,0:T(8,128)(2,1)S(1)}, bf16[656,128]{1,0:T(8,128)(2,1)S(1)}, u32[]{:S(2)}, u32[]{:S(2)}) %collective-permute-start.34) | collective-permute-done | bytes 167968 | tf_op jit(solution)/shard_map/ppermute | solution.py:31
  106.2 1.0 collective-permute-done.38.refs_0_
  (55 shorter events, 7.5 us)
Async XLA Ops:
  0.6 7.3 %collective-permute-start = (bf16[64,1280]{1,0:T(8,128)(2,1)}, bf16[64,1280]{1,0:T(8,128)(2,1)S(1)}, u32[]{:S(2)}, u32[]{:S(2)}) collective-permute-start(bf16[64,1280]{1,0:T(8,128)(2,1)} %refs_0_.1), channel_id=1, source_target_pairs={{0,2},{1,3},{2,4},{3,5},{4,6},{5,7},{6,8},{7,9},{8,10},{9,11},{10,... | collective-permute-start | bytes 491528 | tf_op jit(solution)/shard_map/ppermute | solution.py:31
  2.6 7.3 %collective-permute-start.1 = (bf16[64,1280]{1,0:T(8,128)(2,1)}, bf16[64,1280]{1,0:T(8,128)(2,1)S(1)}, u32[]{:S(2)}, u32[]{:S(2)}) collective-permute-start(bf16[64,1280]{1,0:T(8,128)(2,1)} %refs_0_.1), channel_id=1, source_target_pairs={{0,14},{1,15},{2,0},{3,1},{4,2},{5,3},{6,4},{7,5},{8,6},{9,7},{10,... | collective-permute-start | bytes 491528 | tf_op jit(solution)/shard_map/ppermute | solution.py:31
  2.7 9.3 %collective-permute-start.4 = (bf16[64,1280]{1,0:T(8,128)(2,1)}, bf16[64,1280]{1,0:T(8,128)(2,1)S(1)}, u32[]{:S(2)}, u32[]{:S(2)}) collective-permute-start(bf16[64,1280]{1,0:T(8,128)(2,1)} %text.1), channel_id=1, source_target_pairs={{0,16},{1,65},{2,18},{3,67},{4,20},{5,69},{6,22},{7,71},{8,24},{9,... | collective-permute-start | bytes 491528 | tf_op jit(solution)/shard_map/ppermute | solution.py:40
  4.3 7.8 %collective-permute-start.5 = (bf16[64,1280]{1,0:T(8,128)(2,1)}, bf16[64,1280]{1,0:T(8,128)(2,1)S(1)}, u32[]{:S(2)}, u32[]{:S(2)}) collective-permute-start(bf16[64,1280]{1,0:T(8,128)(2,1)} %text.1), channel_id=1, source_target_pairs={{0,48},{1,193},{2,50},{3,195},{4,52},{5,197},{6,54},{7,199},{8,56}... | collective-permute-start | bytes 491528 | tf_op jit(solution)/shard_map/ppermute | solution.py:40
  6.0 7.0 %collective-permute-start.6 = (bf16[64,1280]{1,0:T(8,128)(2,1)}, bf16[64,1280]{1,0:T(8,128)(2,1)S(1)}, u32[]{:S(2)}, u32[]{:S(2)}) collective-permute-start(bf16[64,1280]{1,0:T(8,128)(2,1)} %text.1), channel_id=1, source_target_pairs={{0,32},{1,129},{2,34},{3,131},{4,36},{5,133},{6,38},{7,135},{8,40}... | collective-permute-start | bytes 491528 | tf_op jit(solution)/shard_map/ppermute | solution.py:40
  8.0 7.3 %collective-permute-start.2 = (bf16[64,1280]{1,0:T(8,128)(2,1)S(1)}, bf16[64,1280]{1,0:T(8,128)(2,1)S(1)}, u32[]{:S(2)}, u32[]{:S(2)}) collective-permute-start(bf16[64,1280]{1,0:T(8,128)(2,1)S(1)} %collective-permute-done.refs_1_), channel_id=1, source_target_pairs={{0,2},{1,3},{2,4},{3,5},{4,6},{5,7},{6,8},{7,9},{8,10},{9,11},{10,... | collective-permute-start | bytes 491528 | tf_op jit(solution)/shard_map/ppermute | solution.py:31
  9.9 6.3 %collective-permute-start.3 = (bf16[64,1280]{1,0:T(8,128)(2,1)S(1)}, bf16[64,1280]{1,0:T(8,128)(2,1)S(1)}, u32[]{:S(2)}, u32[]{:S(2)}) collective-permute-start(bf16[64,1280]{1,0:T(8,128)(2,1)S(1)} %collective-permute-done.1.refs_2_), channel_id=1, source_target_pairs={{0,14},{1,15},{2,0},{3,1},{4,2},{5,3},{6,4},{7,5},{8,6},{9,7},{10,... | collective-permute-start | bytes 491528 | tf_op jit(solution)/shard_map/ppermute | solution.py:31
  13.0 0.9 copy-start
  16.2 20.1 %collective-permute-start.10 = (bf16[256,1280]{1,0:T(8,128)(2,1)S(1)}, bf16[256,1280]{1,0:T(8,128)(2,1)S(1)}, u32[]{:S(2)}, u32[]{:S(2)}) collective-permute-start(bf16[256,1280]{1,0:T(8,128)(2,1)S(1)} %shard_map.49.refs_8_), channel_id=1, source_target_pairs={{0,64},{1,17},{2,66},{3,19},{4,68},{5,21},{6,70},{7,23},{8,72},{9,... | collective-permute-start | bytes 1966088 | tf_op jit(solution)/shard_map/ppermute | solution.py:40
  17.7 18.6 %collective-permute-start.11 = (bf16[256,1280]{1,0:T(8,128)(2,1)S(1)}, bf16[256,1280]{1,0:T(8,128)(2,1)S(1)}, u32[]{:S(2)}, u32[]{:S(2)}) collective-permute-start(bf16[256,1280]{1,0:T(8,128)(2,1)S(1)} %shard_map.49.refs_8_), channel_id=1, source_target_pairs={{0,192},{1,49},{2,194},{3,51},{4,196},{5,53},{6,198},{7,55},{8,200... | collective-permute-start | bytes 1966088 | tf_op jit(solution)/shard_map/ppermute | solution.py:40
  19.4 16.9 %collective-permute-start.12 = (bf16[256,1280]{1,0:T(8,128)(2,1)S(1)}, bf16[256,1280]{1,0:T(8,128)(2,1)S(1)}, u32[]{:S(2)}, u32[]{:S(2)}) collective-permute-start(bf16[256,1280]{1,0:T(8,128)(2,1)S(1)} %shard_map.49.refs_8_), channel_id=1, source_target_pairs={{0,128},{1,33},{2,130},{3,35},{4,132},{5,37},{6,134},{7,39},{8,136... | collective-permute-start | bytes 1966088 | tf_op jit(solution)/shard_map/ppermute | solution.py:40
  21.3 6.1 %collective-permute-start.7 = (bf16[64,1280]{1,0:T(8,128)(2,1)S(1)}, bf16[64,1280]{1,0:T(8,128)(2,1)S(1)}, u32[]{:S(2)}, u32[]{:S(2)}) collective-permute-start(bf16[64,1280]{1,0:T(8,128)(2,1)S(1)} %collective-permute-done.2.refs_3_), channel_id=1, source_target_pairs={{0,2},{1,3},{2,4},{3,5},{4,6},{5,7},{6,8},{7,9},{8,10},{9,11},{10,... | collective-permute-start | bytes 491528 | tf_op jit(solution)/shard_map/ppermute | solution.py:31
  24.5 6.5 %collective-permute-start.8 = (bf16[64,1280]{1,0:T(8,128)(2,1)S(1)}, bf16[64,1280]{1,0:T(8,128)(2,1)S(1)}, u32[]{:S(2)}, u32[]{:S(2)}) collective-permute-start(bf16[64,1280]{1,0:T(8,128)(2,1)S(1)} %collective-permute-done.3.refs_4_), channel_id=1, source_target_pairs={{0,14},{1,15},{2,0},{3,1},{4,2},{5,3},{6,4},{7,5},{8,6},{9,7},{10,... | collective-permute-start | bytes 491528 | tf_op jit(solution)/shard_map/ppermute | solution.py:31
  31.0 5.3 %collective-permute-start.9 = (bf16[64,1280]{1,0:T(8,128)(2,1)S(1)}, bf16[64,1280]{1,0:T(8,128)(2,1)S(1)}, u32[]{:S(2)}, u32[]{:S(2)}) collective-permute-start(bf16[64,1280]{1,0:T(8,128)(2,1)S(1)} %collective-permute-done.7.refs_5_), channel_id=1, source_target_pairs={{0,2},{1,3},{2,4},{3,5},{4,6},{5,7},{6,8},{7,9},{8,10},{9,11},{10,... | collective-permute-start | bytes 491528 | tf_op jit(solution)/shard_map/ppermute | solution.py:31
  33.0 7.3 %collective-permute-start.13 = (bf16[256,1280]{1,0:T(8,128)(2,1)S(1)}, bf16[256,1280]{1,0:T(8,128)(2,1)S(1)}, u32[]{:S(2)}, u32[]{:S(2)}) collective-permute-start(bf16[256,1280]{1,0:T(8,128)(2,1)S(1)} %shard_map.49.refs_8_), channel_id=1, source_target_pairs={{0,1},{1,0},{2,3},{3,2},{4,5},{5,4},{6,7},{7,6},{8,9},{9,8},{10,11... | collective-permute-start | bytes 1966088 | tf_op jit(solution)/shard_map/ppermute | solution.py:54
  36.3 4.0 %collective-permute-start.14 = (bf16[256,1280]{1,0:T(8,128)(2,1)S(1)}, bf16[256,1280]{1,0:T(8,128)(2,1)S(1)}, u32[]{:S(2)}, u32[]{:S(2)}) collective-permute-start(bf16[256,1280]{1,0:T(8,128)(2,1)S(1)} %collective-permute-done.10.refs_9_), channel_id=1, source_target_pairs={{0,1},{1,0},{2,3},{3,2},{4,5},{5,4},{6,7},{7,6},{8,9},{9,8},{10,11... | collective-permute-start | bytes 1966088 | tf_op jit(solution)/shard_map/ppermute | solution.py:54
  36.4 3.9 %collective-permute-start.15 = (bf16[256,1280]{1,0:T(8,128)(2,1)S(1)}, bf16[256,1280]{1,0:T(8,128)(2,1)S(1)}, u32[]{:S(2)}, u32[]{:S(2)}) collective-permute-start(bf16[256,1280]{1,0:T(8,128)(2,1)S(1)} %collective-permute-done.11.refs_10_), channel_id=1, source_target_pairs={{0,1},{1,0},{2,3},{3,2},{4,5},{5,4},{6,7},{7,6},{8,9},{9,8},{10,11... | collective-permute-start | bytes 1966088 | tf_op jit(solution)/shard_map/ppermute | solution.py:54
  36.9 3.5 %collective-permute-start.16 = (bf16[256,1280]{1,0:T(8,128)(2,1)S(1)}, bf16[256,1280]{1,0:T(8,128)(2,1)S(1)}, u32[]{:S(2)}, u32[]{:S(2)}) collective-permute-start(bf16[256,1280]{1,0:T(8,128)(2,1)S(1)} %collective-permute-done.12.refs_11_), channel_id=1, source_target_pairs={{0,1},{1,0},{2,3},{3,2},{4,5},{5,4},{6,7},{7,6},{8,9},{9,8},{10,11... | collective-permute-start | bytes 1966088 | tf_op jit(solution)/shard_map/ppermute | solution.py:54
  37.0 0.9 copy-start.1
  42.8 3.7 %collective-permute-start.17 = (f32[1,512]{1,0:T(1,128)S(1)}, f32[1,512]{1,0:T(1,128)S(1)}, u32[]{:S(2)}, u32[]{:S(2)}) collective-permute-start(f32[1,512]{1,0:T(1,128)S(1)} %get-tuple-element.76), channel_id=1, source_target_pairs={{0,2},{1,3},{2,0},{3,1},{4,6},{5,7},{6,4},{7,5},{8,10},{9,11},{10,... | collective-permute-start | bytes 6152 | tf_op jit(solution)/shard_map/ppermute | solution.py:54
  44.9 29.8 %collective-permute-start.28 = (bf16[512,1280]{1,0:T(8,128)(2,1)S(1)}, bf16[512,1280]{1,0:T(8,128)(2,1)S(1)}, u32[]{:S(2)}, u32[]{:S(2)}) collective-permute-start(bf16[512,1280]{1,0:T(8,128)(2,1)S(1)} %get-tuple-element.71.refs_4_.refs_2_), channel_id=1, source_target_pairs={{0,1},{1,0},{2,3},{3,2},{4,5},{5,4},{6,7},{7,6},{8,9},{9,8},{10,11... | collective-permute-start | bytes 3932168 | tf_op jit(solution)/shard_map/ppermute | solution.py:54
  45.0 7.1 %collective-permute-start.20 = (f32[1,2176]{1,0:T(1,128)S(1)}, f32[1,2176]{1,0:T(1,128)S(1)}, u32[]{:S(2)}, u32[]{:S(2)}) collective-permute-start(f32[1,2176]{1,0:T(1,128)S(1)} %get-tuple-element.77), channel_id=1, source_target_pairs={{0,1},{1,0},{2,3},{3,2},{4,5},{5,4},{6,7},{7,6},{8,9},{9,8},{10,11... | collective-permute-start | bytes 26120 | tf_op jit(solution)/shard_map/ppermute | solution.py:54
  46.5 9.8 %collective-permute-start.18 = (f32[1,512]{1,0:T(1,128)S(1)}, f32[1,512]{1,0:T(1,128)S(1)}, u32[]{:S(2)}, u32[]{:S(2)}) collective-permute-start(f32[1,512]{1,0:T(1,128)S(1)} %log_add_fusion.2), channel_id=1, source_target_pairs={{0,4},{1,5},{2,6},{3,7},{4,0},{5,1},{6,2},{7,3},{8,12},{9,13},{10,... | collective-permute-start | bytes 6152 | tf_op jit(solution)/shard_map/ppermute | solution.py:54
  52.1 6.0 %collective-permute-start.23 = (f32[1,2176]{1,0:T(1,128)S(1)}, f32[1,2176]{1,0:T(1,128)S(1)}, u32[]{:S(2)}, u32[]{:S(2)}) collective-permute-start(f32[1,2176]{1,0:T(1,128)S(1)} %add_select_fusion.2), channel_id=1, source_target_pairs={{0,32},{1,33},{2,34},{3,35},{4,36},{5,37},{6,38},{7,39},{8,40},{9,... | collective-permute-start | bytes 26120 | tf_op jit(solution)/shard_map/ppermute | solution.py:77
  54.3 3.8 %collective-permute-start.22 = (f32[1,2176]{1,0:T(1,128)S(1)}, f32[1,2176]{1,0:T(1,128)S(1)}, u32[]{:S(2)}, u32[]{:S(2)}) collective-permute-start(f32[1,2176]{1,0:T(1,128)S(1)} %add_select_fusion.2), channel_id=1, source_target_pairs={{0,48},{1,49},{2,50},{3,51},{4,52},{5,53},{6,54},{7,55},{8,56},{9,... | collective-permute-start | bytes 26120 | tf_op jit(solution)/shard_map/ppermute | solution.py:77
  55.5 4.9 %collective-permute-start.21 = (f32[1,2176]{1,0:T(1,128)S(1)}, f32[1,2176]{1,0:T(1,128)S(1)}, u32[]{:S(2)}, u32[]{:S(2)}) collective-permute-start(f32[1,2176]{1,0:T(1,128)S(1)} %add_select_fusion.2), channel_id=1, source_target_pairs={{0,16},{1,17},{2,18},{3,19},{4,20},{5,21},{6,22},{7,23},{8,24},{9,... | collective-permute-start | bytes 26120 | tf_op jit(solution)/shard_map/ppermute | solution.py:77
  56.3 8.3 %collective-permute-start.19 = (f32[1,512]{1,0:T(1,128)S(1)}, f32[1,512]{1,0:T(1,128)S(1)}, u32[]{:S(2)}, u32[]{:S(2)}) collective-permute-start(f32[1,512]{1,0:T(1,128)S(1)} %log_add_fusion.1), channel_id=1, source_target_pairs={{0,8},{1,9},{2,10},{3,11},{4,12},{5,13},{6,14},{7,15},{8,0},{9,1},... | collective-permute-start | bytes 6152 | tf_op jit(solution)/shard_map/ppermute | solution.py:54
  60.5 5.2 %collective-permute-start.26 = (f32[1,2176]{1,0:T(1,128)S(1)}, f32[1,2176]{1,0:T(1,128)S(1)}, u32[]{:S(2)}, u32[]{:S(2)}) collective-permute-start(f32[1,2176]{1,0:T(1,128)S(1)} %add_select_fusion.1), channel_id=1, source_target_pairs={{0,128},{1,129},{2,130},{3,131},{4,132},{5,133},{6,134},{7,135},{8... | collective-permute-start | bytes 26120 | tf_op jit(solution)/shard_map/ppermute | solution.py:77
  61.4 4.6 %collective-permute-start.25 = (f32[1,2176]{1,0:T(1,128)S(1)}, f32[1,2176]{1,0:T(1,128)S(1)}, u32[]{:S(2)}, u32[]{:S(2)}) collective-permute-start(f32[1,2176]{1,0:T(1,128)S(1)} %add_select_fusion.1), channel_id=1, source_target_pairs={{0,192},{1,193},{2,194},{3,195},{4,196},{5,197},{6,198},{7,199},{8... | collective-permute-start | bytes 26120 | tf_op jit(solution)/shard_map/ppermute | solution.py:77
  64.6 4.9 %collective-permute-start.24 = (f32[1,2176]{1,0:T(1,128)S(1)}, f32[1,2176]{1,0:T(1,128)S(1)}, u32[]{:S(2)}, u32[]{:S(2)}) collective-permute-start(f32[1,2176]{1,0:T(1,128)S(1)} %add_select_fusion.1), channel_id=1, source_target_pairs={{0,64},{1,65},{2,66},{3,67},{4,68},{5,69},{6,70},{7,71},{8,72},{9,... | collective-permute-start | bytes 26120 | tf_op jit(solution)/shard_map/ppermute | solution.py:77
  71.2 3.4 %collective-permute-start.27 = (bf16[512,1024]{1,0:T(8,128)(2,1)S(1)}, bf16[512,1024]{1,0:T(8,128)(2,1)S(1)}, u32[]{:S(2)}, u32[]{:S(2)}) collective-permute-start(bf16[512,1024]{1,0:T(8,128)(2,1)S(1)} %get-tuple-element.89.refs_1_), channel_id=1, source_target_pairs={{0,1},{1,0},{2,3},{3,2},{4,5},{5,4},{6,7},{7,6},{8,9},{9,8},{10,11... | collective-permute-start | bytes 3145736 | tf_op jit(solution)/shard_map/ppermute | solution.py:54
  71.5 3.2 %collective-permute-start.29 = (f32[1,128]{1,0:T(1,128)S(1)}, f32[1,128]{1,0:T(1,128)S(1)}, u32[]{:S(2)}, u32[]{:S(2)}) collective-permute-start(f32[1,128]{1,0:T(1,128)S(1)} %get-tuple-element.87.refs_4_), channel_id=1, source_target_pairs={{0,1},{1,0},{2,3},{3,2},{4,5},{5,4},{6,7},{7,6},{8,9},{9,8},{10,11... | collective-permute-start | bytes 1544 | tf_op jit(solution)/shard_map/ppermute | solution.py:54
  74.6 9.0 %collective-permute-start.30 = (bf16[656,128]{1,0:T(8,128)(2,1)S(1)}, bf16[656,128]{1,0:T(8,128)(2,1)S(1)}, u32[]{:S(2)}, u32[]{:S(2)}) collective-permute-start(bf16[656,128]{1,0:T(8,128)(2,1)S(1)} %get-tuple-element.90), channel_id=1, source_target_pairs={{0,4},{1,13},{2,6},{3,15},{4,8},{5,1},{6,10},{7,3},{8,12},{9,5},{1... | collective-permute-start | bytes 503816 | tf_op jit(solution)/shard_map/ppermute | solution.py:45
  78.2 20.2 %collective-permute-start.35 = (bf16[2576,128]{1,0:T(8,128)(2,1)S(1)}, bf16[2576,128]{1,0:T(8,128)(2,1)S(1)}, u32[]{:S(2)}, u32[]{:S(2)}) collective-permute-start(bf16[2576,128]{1,0:T(8,128)(2,1)S(1)} %get-tuple-element.102), channel_id=1, source_target_pairs={{0,16},{1,65},{2,18},{3,67},{4,20},{5,69},{6,22},{7,71},{8,24},{9,... | collective-permute-start | bytes 1978376 | tf_op jit(solution)/shard_map/ppermute | solution.py:40
  78.3 20.1 %collective-permute-start.36 = (bf16[2576,128]{1,0:T(8,128)(2,1)S(1)}, bf16[2576,128]{1,0:T(8,128)(2,1)S(1)}, u32[]{:S(2)}, u32[]{:S(2)}) collective-permute-start(bf16[2576,128]{1,0:T(8,128)(2,1)S(1)} %get-tuple-element.103), channel_id=1, source_target_pairs={{0,32},{1,129},{2,34},{3,131},{4,36},{5,133},{6,38},{7,135},{8,40}... | collective-permute-start | bytes 1978376 | tf_op jit(solution)/shard_map/ppermute | solution.py:40
  80.2 18.2 %collective-permute-start.37 = (bf16[2576,128]{1,0:T(8,128)(2,1)S(1)}, bf16[2576,128]{1,0:T(8,128)(2,1)S(1)}, u32[]{:S(2)}, u32[]{:S(2)}) collective-permute-start(bf16[2576,128]{1,0:T(8,128)(2,1)S(1)} %get-tuple-element.104), channel_id=1, source_target_pairs={{0,48},{1,193},{2,50},{3,195},{4,52},{5,197},{6,54},{7,199},{8,56}... | collective-permute-start | bytes 1978376 | tf_op jit(solution)/shard_map/ppermute | solution.py:40
  85.3 7.4 %collective-permute-start.31 = (bf16[1296,128]{1,0:T(8,128)(2,1)S(1)}, bf16[1296,128]{1,0:T(8,128)(2,1)S(1)}, u32[]{:S(2)}, u32[]{:S(2)}) collective-permute-start(bf16[1296,128]{1,0:T(8,128)(2,1)S(1)} %get-tuple-element.92), channel_id=1, source_target_pairs={{0,2},{1,3},{2,4},{3,5},{4,6},{5,7},{6,8},{7,9},{8,10},{9,11},{10,... | collective-permute-start | bytes 995336 | tf_op jit(solution)/shard_map/ppermute | solution.py:31
  85.4 8.6 %collective-permute-start.32 = (bf16[1296,128]{1,0:T(8,128)(2,1)S(1)}, bf16[1296,128]{1,0:T(8,128)(2,1)S(1)}, u32[]{:S(2)}, u32[]{:S(2)}) collective-permute-start(bf16[1296,128]{1,0:T(8,128)(2,1)S(1)} %get-tuple-element.93), channel_id=1, source_target_pairs={{0,14},{1,15},{2,0},{3,1},{4,2},{5,3},{6,4},{7,5},{8,6},{9,7},{10,... | collective-permute-start | bytes 995336 | tf_op jit(solution)/shard_map/ppermute | solution.py:31
  94.2 9.1 %collective-permute-start.33 = (bf16[656,128]{1,0:T(8,128)(2,1)S(1)}, bf16[656,128]{1,0:T(8,128)(2,1)S(1)}, u32[]{:S(2)}, u32[]{:S(2)}) collective-permute-start(bf16[656,128]{1,0:T(8,128)(2,1)S(1)} %get-tuple-element.97), channel_id=1, source_target_pairs={{0,4},{1,5},{2,6},{3,7},{4,8},{5,9},{6,10},{7,11},{8,12},{9,13},{1... | collective-permute-start | bytes 503816 | tf_op jit(solution)/shard_map/ppermute | solution.py:31
  97.5 8.0 %collective-permute-start.34 = (bf16[656,128]{1,0:T(8,128)(2,1)S(1)}, bf16[656,128]{1,0:T(8,128)(2,1)S(1)}, u32[]{:S(2)}, u32[]{:S(2)}) collective-permute-start(bf16[656,128]{1,0:T(8,128)(2,1)S(1)} %get-tuple-element.98), channel_id=1, source_target_pairs={{0,12},{1,13},{2,14},{3,15},{4,0},{5,1},{6,2},{7,3},{8,4},{9,5},{1... | collective-permute-start | bytes 503816 | tf_op jit(solution)/shard_map/ppermute | solution.py:31
  98.7 8.4 %collective-permute-start.38 = (bf16[656,128]{1,0:T(8,128)(2,1)S(1)}, bf16[656,128]{1,0:T(8,128)(2,1)S(1)}, u32[]{:S(2)}, u32[]{:S(2)}) collective-permute-start(bf16[656,128]{1,0:T(8,128)(2,1)S(1)} %get-tuple-element.107), channel_id=1, source_target_pairs={{0,64},{1,17},{2,66},{3,19},{4,68},{5,21},{6,70},{7,23},{8,72},{9,... | collective-permute-start | bytes 503816 | tf_op jit(solution)/shard_map/ppermute | solution.py:40
  99.4 7.8 %collective-permute-start.39 = (bf16[656,128]{1,0:T(8,128)(2,1)S(1)}, bf16[656,128]{1,0:T(8,128)(2,1)S(1)}, u32[]{:S(2)}, u32[]{:S(2)}) collective-permute-start(bf16[656,128]{1,0:T(8,128)(2,1)S(1)} %get-tuple-element.108), channel_id=1, source_target_pairs={{0,128},{1,33},{2,130},{3,35},{4,132},{5,37},{6,134},{7,39},{8,136... | collective-permute-start | bytes 503816 | tf_op jit(solution)/shard_map/ppermute | solution.py:40
  100.9 7.1 %collective-permute-start.40 = (bf16[656,128]{1,0:T(8,128)(2,1)S(1)}, bf16[656,128]{1,0:T(8,128)(2,1)S(1)}, u32[]{:S(2)}, u32[]{:S(2)}) collective-permute-start(bf16[656,128]{1,0:T(8,128)(2,1)S(1)} %get-tuple-element.109), channel_id=1, source_target_pairs={{0,192},{1,49},{2,194},{3,51},{4,196},{5,53},{6,198},{7,55},{8,200... | collective-permute-start | bytes 503816 | tf_op jit(solution)/shard_map/ppermute | solution.py:40
